TPU v7x, 32 devices: a whole 2x2x4 slice. The times are simulated.
32 devices in a mesh: field: 2 (over x), tile: 16 (over z, y, core).
Axes of the slice: x: 2, y: 2, z: 4, core: 2. Of those that a mesh axis runs over, the one named last changes fastest.
Arguments:
- psi_det: float32 [128, 8, 8, 128], P(('field', 'tile')), parts along dimension 0, may hold values from -6 to 6
- phi_det: float32 [128, 8, 8, 128], P(('field', 'tile')), parts along dimension 0, may hold values from 0.25 to 4
- dest_tile: int32 [128, 8, 1], P(('field', 'tile')), parts along dimension 0, may hold values from 0 to 15; in each aligned block of 32 rows (0 to 31, 32 to 63, ..., all dimensions but the last counted through in order) at most 4 rows name the same one
- dest_cell: int32 [128, 8], P(('field', 'tile')), parts along dimension 0, may hold values from 0 to 3
- kernel_id: int32 [128, 8], P(('field', 'tile')), parts along dimension 0, may hold values from 0 to 7
- intersection_weight: float32 [128, 8], P(('field', 'tile')), parts along dimension 0, may hold values from 0.5 to 1.5
- kernels: float32 [8, 128, 128], replicated, may hold values from 0 to 2
- row_offsets: int32 [16, 16], P('field'), parts along dimension 0, may hold values from -8 to 8
- col_offsets: int32 [16, 16], P('field'), parts along dimension 0, may hold values from -64 to 64
Outputs:
- best: float32 [256, 512], P(('field', 'tile')), parts along dimension 0
There are 2 independent parts, one for each index of `field`. A program takes and returns all parts, laid end to end along the dimension named above; an argument that names none is the same for every part. Nothing has to cross between parts.
Inputs may be any that keep to these rules, and one draw needn't show every extreme that they name: `dest_tile`: among one device's 4 blocks over all 8 epochs no tile is named more than 4 times, a bound that some block reaches. `kernels`: every kernel is tridiagonal; kernels[k, i, j] = 0 whenever |i - j| > 1.
All inputs are finite; a program needn't handle non-finite values.
Results may differ from a plain program's by a relative error of at most 0.0003.
Values sent between devices are 32-bit elements; how exact they have to be, the bound alone decides.
No kernel may reach another device: no remote copies, remote signals or barrier semaphores. Data moves between devices by JAX's collectives and lax.ppermute only.
A program may use at most 64 MiB of HBM per device.

v0:
```python
import math

import jax
import jax.numpy as jnp
from jax import lax
from jax.sharding import PartitionSpec as P

VELS = 16
XREACH = 64
RREACH = 8


def with_halo(block, sides, width):
    for axis, dim in sides:
        count = lax.axis_size(axis)
        forward = [(i, i + 1) for i in range(count - 1)]
        backward = [(target, source) for source, target in forward]
        low = lax.ppermute(
            lax.slice_in_dim(block, block.shape[dim] - width, None, axis=dim), axis, forward
        )
        high = lax.ppermute(lax.slice_in_dim(block, 0, width, axis=dim), axis, backward)
        block = jnp.concatenate([low, block, high], axis=dim)
    return block


def reproject(payload, kernel_ids, weights, kernels_table):
    row_total = payload.shape[0]
    group_size = math.gcd(row_total, 32)

    def one_group(group_items):
        pieces, chosen_ids, factors = group_items
        chosen = kernels_table[chosen_ids]
        moved = jnp.einsum("ncrb,nbk->ncrk", pieces, chosen, precision=lax.Precision.HIGHEST)
        return moved * factors[:, None, None, None]

    grouped = (
        payload.reshape((row_total // group_size, group_size) + payload.shape[1:]),
        kernel_ids.reshape(row_total // group_size, group_size),
        weights.reshape(row_total // group_size, group_size),
    )
    return lax.map(one_group, grouped).reshape(payload.shape)


def pack_rows(receivers, payload, details, tile_count, capacity):
    matches = (receivers[:, None] == jnp.arange(tile_count, dtype=jnp.int32)[None, :]).astype(
        jnp.int32
    )
    before = jnp.cumsum(matches, axis=0) - matches
    slot_rank = jnp.sum(before * matches, axis=1)
    position = jnp.where(receivers >= 0, receivers * capacity + slot_rank, tile_count * capacity)
    outgoing = (
        jnp.zeros((tile_count * capacity,) + payload.shape[1:], payload.dtype)
        .at[position]
        .set(payload, mode="drop")
    )
    send_meta = (
        jnp.zeros((tile_count * capacity, details.shape[1]), details.dtype)
        .at[position]
        .set(details, mode="drop")
    )
    return (
        outgoing.reshape((tile_count, capacity) + payload.shape[1:]),
        send_meta.reshape(tile_count, capacity, details.shape[1]),
    )


def receive_sum(incoming, in_meta, kernels_table, segment_total):
    slots_flat = incoming.reshape((-1,) + incoming.shape[2:])
    details = in_meta.reshape(-1, in_meta.shape[2])
    slots_flat = reproject(
        slots_flat, details[:, 1].astype(jnp.int32), details[:, 2], kernels_table
    )
    slot_target = details[:, 0].astype(jnp.int32) - 1
    return jax.ops.segment_sum(
        slots_flat.reshape(slots_flat.shape[0], -1), slot_target, num_segments=segment_total
    )


def body(
    psi_det,
    phi_det,
    dest_tile,
    dest_cell,
    kernel_id,
    intersection_weight,
    kernels,
    row_offsets,
    col_offsets,
):
    tile_count = lax.axis_size("tile")
    cell_count = psi_det.shape[0]
    epochs = psi_det.shape[1]
    row_count = psi_det.shape[2]
    block_width = psi_det.shape[3]
    side_cols = cell_count * block_width
    row_total = cell_count * epochs
    blocks = jnp.stack([psi_det, phi_det], axis=2).reshape(row_total, 2, row_count, block_width)
    kernel_ids = kernel_id.reshape(row_total)
    weights = intersection_weight.reshape(row_total)
    receivers = dest_tile.reshape(row_total)
    epoch_of = jnp.arange(row_total, dtype=jnp.int32) % epochs
    target = epoch_of * cell_count + dest_cell.reshape(row_total)
    capacity = max(2, 2 * row_total // tile_count)
    segment_count = epochs * cell_count
    details = jnp.stack(
        [(target + 1).astype(jnp.float32), kernel_ids.astype(jnp.float32), weights], axis=1
    )
    outgoing, send_meta = pack_rows(receivers, blocks, details, tile_count, capacity)
    incoming, in_meta = (
        lax.all_to_all(outgoing, "tile", split_axis=0, concat_axis=0, tiled=True),
        lax.all_to_all(send_meta, "tile", split_axis=0, concat_axis=0, tiled=True),
    )
    summed = receive_sum(incoming, in_meta, kernels, segment_count)
    sky_image = summed.reshape(epochs, cell_count, 2, row_count, block_width).transpose(
        2, 0, 3, 1, 4
    )
    sky_image = sky_image.reshape(2, epochs, row_count, side_cols)
    padded = with_halo(sky_image, (("tile", 2),), RREACH)
    base_row = RREACH
    widened = jnp.pad(padded, ((0, 0), (0, 0), (0, 0), (XREACH, XREACH)))

    def stacked(offsets):
        row_shift, col_shift = offsets
        sums = jnp.zeros((2, row_count, side_cols), jnp.float32)
        for epoch_idx in range(epochs):
            start_row = base_row + row_shift[epoch_idx]
            start_col = XREACH + col_shift[epoch_idx]
            sums = sums + lax.dynamic_slice(
                widened[:, epoch_idx],
                (jnp.int32(0), start_row, start_col),
                (2, row_count, side_cols),
            )
        return sums[0] / jnp.sqrt(jnp.maximum(sums[1], 1.0))

    def per_group(offsets):
        return jax.vmap(stacked)(offsets)

    row_groups = row_offsets.T.reshape(VELS // 8, 8, epochs)
    col_groups = col_offsets.T.reshape(VELS // 8, 8, epochs)
    scores = lax.map(per_group, (row_groups, col_groups))
    return jnp.max(scores.reshape(VELS, row_count, side_cols), axis=0)


def solution(mesh):
    placed = (
        P(("field", "tile"), None, None, None),
        P(("field", "tile"), None, None, None),
        P(("field", "tile"), None, None),
        P(("field", "tile"), None),
        P(("field", "tile"), None),
        P(("field", "tile"), None),
        P(),
        P("field", None),
        P("field", None),
    )
    return jax.shard_map(
        body, mesh=mesh, in_specs=placed, out_specs=P(("field", "tile"), None), check_vma=False
    )
```

profile of v0, /device:TPU:1, one launch (start us, length us, event | category | flops | bytes accessed | tf_op | source)
XLA Modules:
  0.0 319.9 jit_solution(18229314593134390359)
XLA Ops:
  1.3 1.3 fusion.38
  7.1 7.3 %all-to-all-start = ((f32[16,4,3]{1,2,0:T(4,128)}), f32[16,4,3]{1,2,0:T(4,128)S(1)}, u32[]{:S(2)}, u32[]{:S(2)}) async-start(f32[16,4,3]{1,2,0:T(4,128)} %copy.92), calls=%async_computation | async-start | bytes 65536 | tf_op jit(solution)/shard_map/all_to_all | solution.py:111
  16.3 3.8 %scatter_fusion = f32[64,2,8,128]{3,2,1,0:T(8,128)} fusion(f32[64,2,8,128]{3,2,1,0:T(8,128)} %broadcast_in_dim.26, s32[32]{0:T(128)S(1)} %fusion.36, f32[32,2,8,128]{3,2,1,0:T(8,128)S(1)} %pad_maximum_fusion.1), kind=kCustom, calls=%fused_computation.2 | custom fusion | bytes 786560 | tf_op jit(solution)/shard_map/scatter | solution.py:54
  20.4 5.8 %all-to-all-start.1 = ((f32[16,4,2,8,128]{4,3,2,1,0:T(8,128)}), f32[16,4,2,8,128]{4,3,2,1,0:T(8,128)S(1)}, u32[]{:S(2)}, u32[]{:S(2)}) async-start(f32[16,4,2,8,128]{4,3,2,1,0:T(8,128)} %bitcast.26), calls=%async_computation.1 | async-start | bytes 1048576 | tf_op jit(solution)/shard_map/all_to_all | solution.py:110
  26.5 13.8 %all-to-all-done.1 = f32[16,4,2,8,128]{4,3,2,1,0:T(8,128)S(1)} async-done(((f32[16,4,2,8,128]{4,3,2,1,0:T(8,128)}), f32[16,4,2,8,128]{4,3,2,1,0:T(8,128)S(1)}, u32[]{:S(2)}, u32[]{:S(2)}) %all-to-all-start.1) | async-done | bytes 524320 | tf_op jit(solution)/shard_map/all_to_all | solution.py:110
  40.2 6.6 %while.39 = (s32[]{:T(128)}, f32[2,32,2,8,128]{4,3,2,1,0:T(8,128)}, f32[2,32,2,8,128]{4,3,2,1,0:T(8,128)S(1)}, s32[2,32]{1,0:T(2,128)S(1)}, f32[8,128,128]{2,1,0:T(8,128)S(1)}, /*index=5*/f32[2,32]{1,0:T(2,128)S(1)}, s32[]{:T(128)}) while((s32[]{:T(128)}, f32[2,32,2,8,128]{4,3,2,1,0:T(8,128)}, f32[2,32,2,8,128]{4,3,2,1,0:T(8,128)S(1)}, ...), condition=%wide.region_5.6_spmd, body=%wide.region_4.5_spmd.sunk | while | flops 100729952 | bytes 6822229 | solution.py:41
  41.0 2.6 fusion.67
  44.3 2.6 fusion.67
  48.0 1.4 scatter_custom_fusion.2
  49.5 2.4 collective-permute-start
  51.9 1.9 collective-permute-start.1
  55.2 4.4 %collective-permute-done.1 = f32[2,8,8,512]{3,2,1,0:T(8,128)S(1)} collective-permute-done((f32[2,8,8,512]{3,2,1,0:T(8,128)S(1)}, f32[2,8,8,512]{3,2,1,0:T(8,128)S(1)}, u32[]{:S(2)}, u32[]{:S(2)}) %collective-permute-start.1) | collective-permute-done | bytes 262176 | tf_op jit(solution)/shard_map/ppermute | solution.py:21
  60.1 259.2 %while.48 = (s32[]{:T(128)}, f32[2,8,8,512]{3,2,1,0:T(8,128)S(1)}, f32[2,8,24,640]{3,2,0,1:T(8,128)S(1)}, s32[2,8,8]{2,1,0:T(8,128)S(1)}, s32[2,8,8]{2,1,0:T(8,1...) while((s32[]{:T(128)}, f32[2,8,8,512]{3,2,1,0:T(8,128)S(1)}, ...), condition=%wide.region_8.9_spmd, body=%wide.region_7.8_spmd.sunk | while | flops 525202 | bytes 7344969 | solution.py:140
  60.5 16.1 %while.50 = (s32[]{:T(128)}, f32[2,24,640]{2,1,0:T(8,128)S(1)}, s32[8,3]{1,0:T(8,128)S(1)}, f32[8,2,8,512]{3,2,0,1:T(8,128)S(1)}, s32[]{:T(128)}) while((s32[]{:T(128)}, f32[2,24,640]{2,1,0:T(8,128)S(1)}, s32[8,3]{1,0:T(8,128)S(1)}, f32[8,2,8,512]{3,2,0,1:T(8,128)S(1)}, s32[]{:T(128)}) %tuple.267), condition=%wide.while_cond.6, body=%wide.while_body.6.sunk | while | flops 2 | bytes 65653 | solution.py:128
  61.2 1.3 bitcast_dynamic-update-slice_fusion.17
  63.2 1.3 bitcast_dynamic-update-slice_fusion.17
  65.2 1.3 bitcast_dynamic-update-slice_fusion.17
  67.2 1.3 bitcast_dynamic-update-slice_fusion.17
  69.2 1.3 bitcast_dynamic-update-slice_fusion.17
  71.2 1.3 bitcast_dynamic-update-slice_fusion.17
  73.2 1.3 bitcast_dynamic-update-slice_fusion.17
  75.2 1.3 bitcast_dynamic-update-slice_fusion.17
  76.6 16.1 %while.51 = (s32[]{:T(128)}, f32[2,24,640]{2,1,0:T(8,128)S(1)}, s32[8,3]{1,0:T(8,128)S(1)}, f32[8,2,8,512]{3,2,0,1:T(8,128)S(1)}, s32[]{:T(128)}) while((s32[]{:T(128)}, f32[2,24,640]{2,1,0:T(8,128)S(1)}, s32[8,3]{1,0:T(8,128)S(1)}, f32[8,2,8,512]{3,2,0,1:T(8,128)S(1)}, s32[]{:T(128)}) %tuple.270), condition=%wide.while_cond.5, body=%wide.while_body.5.sunk | while | flops 2 | bytes 65653 | solution.py:128
  77.3 1.3 bitcast_dynamic-update-slice_fusion.18
  79.3 1.3 bitcast_dynamic-update-slice_fusion.18
  81.3 1.3 bitcast_dynamic-update-slice_fusion.18
  83.3 1.3 bitcast_dynamic-update-slice_fusion.18
  87.3 1.3 bitcast_dynamic-update-slice_fusion.18
  89.3 1.3 bitcast_dynamic-update-slice_fusion.18
  91.3 1.3 bitcast_dynamic-update-slice_fusion.18
  92.7 16.1 %while.52 = (s32[]{:T(128)}, f32[2,24,640]{2,1,0:T(8,128)S(1)}, s32[8,3]{1,0:T(8,128)S(1)}, f32[8,2,8,512]{3,2,0,1:T(8,128)S(1)}, s32[]{:T(128)}) while((s32[]{:T(128)}, f32[2,24,640]{2,1,0:T(8,128)S(1)}, s32[8,3]{1,0:T(8,128)S(1)}, f32[8,2,8,512]{3,2,0,1:T(8,128)S(1)}, s32[]{:T(128)}) %tuple.273), condition=%wide.while_cond.4, body=%wide.while_body.4.sunk | while | flops 2 | bytes 65653 | solution.py:128
  93.4 1.3 bitcast_dynamic-update-slice_fusion.19
  95.4 1.3 bitcast_dynamic-update-slice_fusion.19
  97.4 1.3 bitcast_dynamic-update-slice_fusion.19
  99.4 1.3 bitcast_dynamic-update-slice_fusion.19
  101.4 1.3 bitcast_dynamic-update-slice_fusion.19
  103.4 1.3 bitcast_dynamic-update-slice_fusion.19
  105.4 1.3 bitcast_dynamic-update-slice_fusion.19
  107.4 1.3 bitcast_dynamic-update-slice_fusion.19
  108.8 16.1 %while.53 = (s32[]{:T(128)}, f32[2,24,640]{2,1,0:T(8,128)S(1)}, s32[8,3]{1,0:T(8,128)S(1)}, f32[8,2,8,512]{3,2,0,1:T(8,128)S(1)}, s32[]{:T(128)}) while((s32[]{:T(128)}, f32[2,24,640]{2,1,0:T(8,128)S(1)}, s32[8,3]{1,0:T(8,128)S(1)}, f32[8,2,8,512]{3,2,0,1:T(8,128)S(1)}, s32[]{:T(128)}) %tuple.276), condition=%wide.while_cond.3, body=%wide.while_body.3.sunk | while | flops 2 | bytes 65653 | solution.py:128
  109.5 1.3 bitcast_dynamic-update-slice_fusion.20
  113.5 1.3 bitcast_dynamic-update-slice_fusion.20
  115.5 1.3 bitcast_dynamic-update-slice_fusion.20
  117.5 1.3 bitcast_dynamic-update-slice_fusion.20
  119.5 1.3 bitcast_dynamic-update-slice_fusion.20
  121.5 1.3 bitcast_dynamic-update-slice_fusion.20
  123.6 1.3 bitcast_dynamic-update-slice_fusion.20
  124.9 16.1 %while.56 = (s32[]{:T(128)}, f32[2,24,640]{2,1,0:T(8,128)S(1)}, s32[8,3]{1,0:T(8,128)S(1)}, f32[8,2,8,512]{3,2,0,1:T(8,128)S(1)}, s32[]{:T(128)}) while((s32[]{:T(128)}, f32[2,24,640]{2,1,0:T(8,128)S(1)}, s32[8,3]{1,0:T(8,128)S(1)}, f32[8,2,8,512]{3,2,0,1:T(8,128)S(1)}, s32[]{:T(128)}) %tuple.285), condition=%wide.while_cond.1, body=%wide.while_body.1.sunk | while | flops 2 | bytes 65653 | solution.py:128
  125.6 1.3 bitcast_dynamic-update-slice_fusion.23
  127.6 1.3 bitcast_dynamic-update-slice_fusion.23
  129.6 1.3 bitcast_dynamic-update-slice_fusion.23
  131.6 1.3 bitcast_dynamic-update-slice_fusion.23
  133.6 1.3 bitcast_dynamic-update-slice_fusion.23
  141.0 16.1 %while.49 = (s32[]{:T(128)}, f32[2,24,640]{2,1,0:T(8,128)S(1)}, s32[8,3]{1,0:T(8,128)S(1)}, f32[8,2,8,512]{3,2,0,1:T(8,128)S(1)}, s32[]{:T(128)}) while((s32[]{:T(128)}, f32[2,24,640]{2,1,0:T(8,128)S(1)}, s32[8,3]{1,0:T(8,128)S(1)}, f32[8,2,8,512]{3,2,0,1:T(8,128)S(1)}, s32[]{:T(128)}) %tuple.264), condition=%wide.while_cond.7, body=%wide.while_body.7.sunk | while | flops 2 | bytes 65653 | solution.py:128
  157.2 16.1 %while.54 = (s32[]{:T(128)}, f32[2,24,640]{2,1,0:T(8,128)S(1)}, s32[8,3]{1,0:T(8,128)S(1)}, f32[8,2,8,512]{3,2,0,1:T(8,128)S(1)}, s32[]{:T(128)}) while((s32[]{:T(128)}, f32[2,24,640]{2,1,0:T(8,128)S(1)}, s32[8,3]{1,0:T(8,128)S(1)}, f32[8,2,8,512]{3,2,0,1:T(8,128)S(1)}, s32[]{:T(128)}) %tuple.279), condition=%wide.while_cond.2, body=%wide.while_body.2.sunk | while | flops 2 | bytes 65653 | solution.py:128
  173.3 16.1 %while.55 = (s32[]{:T(128)}, f32[2,24,640]{2,1,0:T(8,128)S(1)}, s32[8,3]{1,0:T(8,128)S(1)}, f32[8,2,8,512]{3,2,0,1:T(8,128)S(1)}, s32[]{:T(128)}) while((s32[]{:T(128)}, f32[2,24,640]{2,1,0:T(8,128)S(1)}, s32[8,3]{1,0:T(8,128)S(1)}, f32[8,2,8,512]{3,2,0,1:T(8,128)S(1)}, s32[]{:T(128)}) %tuple.282), condition=%wide.while_cond, body=%wide.while_body.sunk | while | flops 2 | bytes 65653 | solution.py:128
  190.1 16.1 %while.50 = (s32[]{:T(128)}, f32[2,24,640]{2,1,0:T(8,128)S(1)}, s32[8,3]{1,0:T(8,128)S(1)}, f32[8,2,8,512]{3,2,0,1:T(8,128)S(1)}, s32[]{:T(128)}) while((s32[]{:T(128)}, f32[2,24,640]{2,1,0:T(8,128)S(1)}, s32[8,3]{1,0:T(8,128)S(1)}, f32[8,2,8,512]{3,2,0,1:T(8,128)S(1)}, s32[]{:T(128)}) %tuple.267), condition=%wide.while_cond.6, body=%wide.while_body.6.sunk | while | flops 2 | bytes 65653 | solution.py:128
  206.2 16.1 %while.51 = (s32[]{:T(128)}, f32[2,24,640]{2,1,0:T(8,128)S(1)}, s32[8,3]{1,0:T(8,128)S(1)}, f32[8,2,8,512]{3,2,0,1:T(8,128)S(1)}, s32[]{:T(128)}) while((s32[]{:T(128)}, f32[2,24,640]{2,1,0:T(8,128)S(1)}, s32[8,3]{1,0:T(8,128)S(1)}, f32[8,2,8,512]{3,2,0,1:T(8,128)S(1)}, s32[]{:T(128)}) %tuple.270), condition=%wide.while_cond.5, body=%wide.while_body.5.sunk | while | flops 2 | bytes 65653 | solution.py:128
  222.3 16.1 %while.52 = (s32[]{:T(128)}, f32[2,24,640]{2,1,0:T(8,128)S(1)}, s32[8,3]{1,0:T(8,128)S(1)}, f32[8,2,8,512]{3,2,0,1:T(8,128)S(1)}, s32[]{:T(128)}) while((s32[]{:T(128)}, f32[2,24,640]{2,1,0:T(8,128)S(1)}, s32[8,3]{1,0:T(8,128)S(1)}, f32[8,2,8,512]{3,2,0,1:T(8,128)S(1)}, s32[]{:T(128)}) %tuple.273), condition=%wide.while_cond.4, body=%wide.while_body.4.sunk | while | flops 2 | bytes 65653 | solution.py:128
  238.4 16.1 %while.53 = (s32[]{:T(128)}, f32[2,24,640]{2,1,0:T(8,128)S(1)}, s32[8,3]{1,0:T(8,128)S(1)}, f32[8,2,8,512]{3,2,0,1:T(8,128)S(1)}, s32[]{:T(128)}) while((s32[]{:T(128)}, f32[2,24,640]{2,1,0:T(8,128)S(1)}, s32[8,3]{1,0:T(8,128)S(1)}, f32[8,2,8,512]{3,2,0,1:T(8,128)S(1)}, s32[]{:T(128)}) %tuple.276), condition=%wide.while_cond.3, body=%wide.while_body.3.sunk | while | flops 2 | bytes 65653 | solution.py:128
  254.5 16.1 %while.56 = (s32[]{:T(128)}, f32[2,24,640]{2,1,0:T(8,128)S(1)}, s32[8,3]{1,0:T(8,128)S(1)}, f32[8,2,8,512]{3,2,0,1:T(8,128)S(1)}, s32[]{:T(128)}) while((s32[]{:T(128)}, f32[2,24,640]{2,1,0:T(8,128)S(1)}, s32[8,3]{1,0:T(8,128)S(1)}, f32[8,2,8,512]{3,2,0,1:T(8,128)S(1)}, s32[]{:T(128)}) %tuple.285), condition=%wide.while_cond.1, body=%wide.while_body.1.sunk | while | flops 2 | bytes 65653 | solution.py:128
  270.6 16.1 %while.49 = (s32[]{:T(128)}, f32[2,24,640]{2,1,0:T(8,128)S(1)}, s32[8,3]{1,0:T(8,128)S(1)}, f32[8,2,8,512]{3,2,0,1:T(8,128)S(1)}, s32[]{:T(128)}) while((s32[]{:T(128)}, f32[2,24,640]{2,1,0:T(8,128)S(1)}, s32[8,3]{1,0:T(8,128)S(1)}, f32[8,2,8,512]{3,2,0,1:T(8,128)S(1)}, s32[]{:T(128)}) %tuple.264), condition=%wide.while_cond.7, body=%wide.while_body.7.sunk | while | flops 2 | bytes 65653 | solution.py:128
  286.8 16.1 %while.54 = (s32[]{:T(128)}, f32[2,24,640]{2,1,0:T(8,128)S(1)}, s32[8,3]{1,0:T(8,128)S(1)}, f32[8,2,8,512]{3,2,0,1:T(8,128)S(1)}, s32[]{:T(128)}) while((s32[]{:T(128)}, f32[2,24,640]{2,1,0:T(8,128)S(1)}, s32[8,3]{1,0:T(8,128)S(1)}, f32[8,2,8,512]{3,2,0,1:T(8,128)S(1)}, s32[]{:T(128)}) %tuple.279), condition=%wide.while_cond.2, body=%wide.while_body.2.sunk | while | flops 2 | bytes 65653 | solution.py:128
  302.9 16.1 %while.55 = (s32[]{:T(128)}, f32[2,24,640]{2,1,0:T(8,128)S(1)}, s32[8,3]{1,0:T(8,128)S(1)}, f32[8,2,8,512]{3,2,0,1:T(8,128)S(1)}, s32[]{:T(128)}) while((s32[]{:T(128)}, f32[2,24,640]{2,1,0:T(8,128)S(1)}, s32[8,3]{1,0:T(8,128)S(1)}, f32[8,2,8,512]{3,2,0,1:T(8,128)S(1)}, s32[]{:T(128)}) %tuple.282), condition=%wide.while_cond, body=%wide.while_body.sunk | while | flops 2 | bytes 65653 | solution.py:128
  (436 shorter events, 224.6 us)
Async XLA Ops:
  0.0 40.2 %copy-start = (f32[8,128,128]{2,1,0:T(8,128)S(1)}, f32[8,128,128]{2,1,0:T(8,128)}, u32[]{:S(2)}) copy-start(f32[8,128,128]{2,1,0:T(8,128)} %param.19) | copy-start | bytes 1572868
  7.1 13.3 %all-to-all-start = ((f32[16,4,3]{1,2,0:T(4,128)}), f32[16,4,3]{1,2,0:T(4,128)S(1)}, u32[]{:S(2)}, u32[]{:S(2)}) async-start(f32[16,4,3]{1,2,0:T(4,128)} %copy.92), calls=%async_computation | async-start | bytes 65536 | tf_op jit(solution)/shard_map/all_to_all | solution.py:111
  20.4 19.9 %all-to-all-start.1 = ((f32[16,4,2,8,128]{4,3,2,1,0:T(8,128)}), f32[16,4,2,8,128]{4,3,2,1,0:T(8,128)S(1)}, u32[]{:S(2)}, u32[]{:S(2)}) async-start(f32[16,4,2,8,128]{4,3,2,1,0:T(8,128)} %bitcast.26), calls=%async_computation.1 | async-start | bytes 1048576 | tf_op jit(solution)/shard_map/all_to_all | solution.py:110
  46.8 7.0 %copy-start.1 = (s32[8,16]{1,0:T(8,128)S(1)}, s32[8,16]{1,0:T(8,128)}, u32[]{:S(2)}) copy-start(s32[8,16]{1,0:T(8,128)} %param.20) | copy-start | bytes 1540
  46.8 7.1 %copy-start.2 = (s32[8,16]{1,0:T(8,128)S(1)}, s32[8,16]{1,0:T(8,128)}, u32[]{:S(2)}) copy-start(s32[8,16]{1,0:T(8,128)} %param.21) | copy-start | bytes 1540
  49.5 5.7 %collective-permute-start = (f32[2,8,8,512]{3,2,1,0:T(8,128)S(1)}, f32[2,8,8,512]{3,2,1,0:T(8,128)S(1)}, u32[]{:S(2)}, u32[]{:S(2)}) collective-permute-start(f32[2,8,8,512]{3,2,1,0:T(8,128)S(1)} %bitcast.237), channel_id=1, source_target_pairs={{0,1},{1,2},{2,3},{3,4},{4,5},{5,6},{6,7},{7,8},{8,9},{9,10},{10,1... | collective-permute-start | bytes 786440 | tf_op jit(solution)/shard_map/ppermute | solution.py:18
  51.9 7.7 %collective-permute-start.1 = (f32[2,8,8,512]{3,2,1,0:T(8,128)S(1)}, f32[2,8,8,512]{3,2,1,0:T(8,128)S(1)}, u32[]{:S(2)}, u32[]{:S(2)}) collective-permute-start(f32[2,8,8,512]{3,2,1,0:T(8,128)S(1)} %bitcast.238), channel_id=1, source_target_pairs={{1,0},{2,1},{3,2},{4,3},{5,4},{6,5},{7,6},{8,7},{9,8},{10,9},{11,1... | collective-permute-start | bytes 786440 | tf_op jit(solution)/shard_map/ppermute | solution.py:21
where the time goes:
time: 324 us; the launch traced here: 320 us
  local copies, waits for them, and re-layouts  269 us (83%)
  waiting for transfers between devices  19.6 us (6%)
  starting transfers between devices  17.5 us (5%)
  other arithmetic  7.42 us (2%)
  matrix products  5.13 us (2%)
    gather x384, local copies, waits for them, and re-layouts  256 us
    all_to_all x1, waiting for transfers between devices, body(): lax.all_to_all(outgoing, 'tile', split_axis=0, concat_axis=0, tiled=True)  13.8 us
    all_to_all x1, starting transfers between devices, body(): lax.all_to_all(send_meta, 'tile', split_axis=0, concat_axis=0, tiled=True)  7.35 us
  transfers between devices with their start and end apart: 4, of which 4 were waited for; matrix products, arithmetic and copies ran while one was open for 2% of the time, Pallas kernels for 0%

commit v1 on v0

v1 whole, which is shorter than its diff:
```python
import functools

import jax
import jax.numpy as jnp
from jax import lax
from jax.experimental import pallas as pl
from jax.experimental.pallas import tpu as pltpu
from jax.sharding import PartitionSpec as P

XREACH = 64
RREACH = 8
LANES = 128
VMEM = pl.BlockSpec(memory_space=pltpu.VMEM)
SMEM = pl.BlockSpec(memory_space=pltpu.SMEM)
LIMIT = pltpu.CompilerParams(vmem_limit_bytes=32 * 1024 * 1024)


def pack_kernel(
    capacity, tile_ref, cell_ref, id_ref, weight_ref, psi_ref, phi_ref, table_ref, out_ref, diag_ref, used_ref
):
    cells, epochs = psi_ref.shape[:2]
    tiles, width = out_ref.shape[0], psi_ref.shape[3]

    source = lax.broadcasted_iota(jnp.int32, (width, width), 0)
    target = lax.broadcasted_iota(jnp.int32, (width, width), 1)
    for place in range(3):
        mask = source == target + (place - 1)
        for index in range(table_ref.shape[0]):
            row = jnp.sum(jnp.where(mask, table_ref[index], 0.0), axis=0, keepdims=True)
            diag_ref[index, place : place + 1, :] = row

    def clear(tile, carry):
        used_ref[tile] = 0
        out_ref[tile, 2 * capacity] = jnp.zeros(out_ref.shape[2:], jnp.float32)
        return carry

    lax.fori_loop(0, tiles, clear, 0)
    lane = lax.broadcasted_iota(jnp.int32, (1, LANES), 1)
    for block in range(cells):
        for epoch in range(epochs):
            tile = tile_ref[block, epoch, 0]
            slot = used_ref[tile]
            used_ref[tile] = slot + 1
            bands = diag_ref[id_ref[block, epoch]] * weight_ref[block, epoch]
            for kind, ref in enumerate((psi_ref, phi_ref)):
                values = ref[block, epoch]
                out_ref[tile, 2 * slot + kind] = (
                    values * bands[1:2]
                    + pltpu.roll(values, 1, 1) * bands[0:1]
                    + pltpu.roll(values, width - 1, 1) * bands[2:3]
                )
            place = (epoch * 2 * cells + cell_ref[block, epoch] + 1).astype(jnp.float32)
            note = out_ref[tile, 2 * capacity, 0:1, :]
            out_ref[tile, 2 * capacity, 0:1, :] = jnp.where(lane == slot, place, note)


def sum_kernel(capacity, cells, in_ref, sky_ref):
    for index in range(sky_ref.shape[0]):
        sky_ref[index] = jnp.zeros(sky_ref.shape[1:], jnp.float32)

    def one_source(source, carry):
        notes = in_ref[source, 2 * capacity].astype(jnp.int32)
        for slot in range(capacity):
            place = notes[0, slot] - 1
            there = place >= 0
            base = jnp.maximum(place, 0)
            for kind in range(2):
                value = jnp.where(there, in_ref[source, 2 * slot + kind], 0.0)
                sky_ref[base + kind * cells] = sky_ref[base + kind * cells] + value
        return carry

    lax.fori_loop(0, in_ref.shape[0], one_source, 0, unroll=4)


def stack_kernel(cells, row_ref, col_ref, odd_ref, own_ref, twin_ref, far_ref, best_ref, wide_ref):
    epochs, vels = row_ref.shape
    rows = own_ref.shape[1]
    odd = odd_ref[0]
    twin_row = pl.multiple_of((1 - odd) * 2 * rows, rows)
    far_row = pl.multiple_of(odd * 2 * rows, rows)
    for epoch in range(epochs):
        for kind in range(2):
            zeros = jnp.zeros(wide_ref.shape[3:], jnp.float32)
            wide_ref[epoch, kind, 0] = zeros
            wide_ref[epoch, kind, cells + 1] = zeros
            for cell in range(cells):
                index = (epoch * 2 + kind) * cells + cell
                wide_ref[epoch, kind, cell + 1, rows : 2 * rows, :] = own_ref[index]
                wide_ref[epoch, kind, cell + 1, pl.ds(twin_row, rows), :] = twin_ref[index]
                wide_ref[epoch, kind, cell + 1, pl.ds(far_row, rows), :] = far_ref[index]
    lane = lax.broadcasted_iota(jnp.int32, (rows, LANES), 1)

    def one_velocity(vel, highest):
        sums = [[jnp.zeros((rows, LANES), jnp.float32) for _ in range(cells)] for _ in range(2)]
        for epoch in range(epochs):
            start_row = rows + row_ref[epoch, vel]
            start_col = LANES + col_ref[epoch, vel]
            first = lax.shift_right_logical(start_col, 7)
            shift = start_col & (LANES - 1)
            mask = lane >= shift
            turn = (LANES - shift) & (LANES - 1)
            for kind in range(2):
                parts = [
                    wide_ref[epoch, kind, first + step, pl.ds(start_row, rows), :]
                    for step in range(cells + 1)
                ]
                for cell in range(cells):
                    merged = jnp.where(mask, parts[cell], parts[cell + 1])
                    sums[kind][cell] = sums[kind][cell] + pltpu.roll(merged, turn, 1)
        return [
            jnp.maximum(highest[cell], sums[0][cell] / jnp.sqrt(jnp.maximum(sums[1][cell], 1.0)))
            for cell in range(cells)
        ]

    start = [jnp.full((rows, LANES), -jnp.inf, jnp.float32) for _ in range(cells)]
    highest = lax.fori_loop(0, vels, one_velocity, start)
    for cell in range(cells):
        best_ref[:, cell * LANES : (cell + 1) * LANES] = highest[cell]


def body(psi, phi, dest_tile, dest_cell, kernel_id, weight, kernels, row_offsets, col_offsets):
    tiles = lax.axis_size("tile")
    cells, epochs, rows, width = psi.shape
    capacity = max(2, 2 * cells * epochs // tiles)
    message = (tiles, 2 * capacity + 1, rows, width)
    outgoing = pl.pallas_call(
        functools.partial(pack_kernel, capacity),
        out_shape=jax.ShapeDtypeStruct(message, jnp.float32),
        in_specs=[SMEM] * 4 + [VMEM] * 3,
        out_specs=VMEM,
        scratch_shapes=[
            pltpu.VMEM((kernels.shape[0], 3, width), jnp.float32),
            pltpu.SMEM((tiles,), jnp.int32),
        ],
        compiler_params=LIMIT,
        name="pack",
    )(dest_tile, dest_cell, kernel_id, weight, psi, phi, kernels)
    incoming = lax.all_to_all(outgoing, "tile", split_axis=0, concat_axis=0, tiled=True)
    sky = pl.pallas_call(
        functools.partial(sum_kernel, capacity, cells),
        out_shape=jax.ShapeDtypeStruct((epochs * 2 * cells, rows, width), jnp.float32),
        in_specs=[VMEM],
        out_specs=VMEM,
        compiler_params=LIMIT,
        name="sum_slots",
    )(incoming)
    twin = lax.ppermute(sky, "tile", [(i, i ^ 1) for i in range(tiles)])
    far = lax.ppermute(
        sky, "tile", [pair for i in range(1, tiles - 1, 2) for pair in ((i, i + 1), (i + 1, i))]
    )
    odd = (lax.axis_index("tile") & 1).reshape(1)
    return pl.pallas_call(
        functools.partial(stack_kernel, cells),
        out_shape=jax.ShapeDtypeStruct((rows, cells * width), jnp.float32),
        in_specs=[SMEM] * 3 + [VMEM] * 3,
        out_specs=VMEM,
        scratch_shapes=[pltpu.VMEM((epochs, 2, cells + 2, 3 * rows, width), jnp.float32)],
        compiler_params=LIMIT,
        name="stack",
    )(row_offsets, col_offsets, odd, sky, twin, far)


def solution(mesh):
    placed = (
        P(("field", "tile"), None, None, None),
        P(("field", "tile"), None, None, None),
        P(("field", "tile"), None, None),
        P(("field", "tile"), None),
        P(("field", "tile"), None),
        P(("field", "tile"), None),
        P(),
        P("field", None),
        P("field", None),
    )
    return jax.shard_map(
        body, mesh=mesh, in_specs=placed, out_specs=P(("field", "tile"), None), check_vma=False
    )
```

time: 324 us -> 43.1 us (0.13); the launches traced: 320 us -> 42.4 us
  local copies, waits for them, and re-layouts: 269 us -> 3.68 us
  blocking collectives: 0 us -> 24.1 us
  starting transfers between devices: 17.5 us -> 2.72 us
  waiting for transfers between devices: 19.6 us -> 6.07 us
  other arithmetic: 7.42 us -> 0 us
  Pallas kernels: 0 us -> 5.76 us
  matrix products: 5.13 us -> 0 us
    gather x386 -> x0, local copies, waits for them, and re-layouts: 258 us -> none
    all_to_all x0 -> x1, blocking collectives: none -> 24.1 us  [body(): lax.all_to_all(outgoing, 'tile', split_axis=0, concat_axis=0, tiled=True)]
    all_to_all x2 -> x0, waiting for transfers between devices: 14 us -> none  [the longest x1 13.8 us: body(): lax.all_to_all(outgoing, 'tile', split_axis=0, concat_axis=0, tiled=True)]
    all_to_all x2 -> x0, starting transfers between devices: 13.1 us -> none  [the longest x1 7.35 us: body(): lax.all_to_all(send_meta, 'tile', split_axis=0, concat_axis=0, tiled=True)]
    pallas_call x0 -> x3, Pallas kernels: none -> 5.76 us  [the longest x1 3.65 us: body(): pl.pallas_call(functools.partial(stack_kernel, cells), out_shape=jax.Shap...]
    dot_general x2 -> x0, matrix products: 5.13 us -> none  [one_group(): jnp.einsum('ncrb,nbk->ncrk', pieces, chosen, precision=lax.Precision.HIGH...]
    scatter x2 -> x0, local copies, waits for them, and re-layouts: 4.53 us -> none  [the longest x1 3.84 us: pack_rows(): outgoing = jnp.zeros((tile_count * capacity,) + payload.shape[1:], payloa...]
  transfers between devices with their start and end apart: 4 -> 2, of which waited for: 4 -> 1; matrix products, arithmetic and copies ran while one was open for 2% -> 0% of each run, Pallas kernels for 0% -> 0%
where the time goes in v1:
time: 43.1 us; the launch traced here: 42.4 us
  blocking collectives  24.1 us (56%)
  waiting for transfers between devices  6.07 us (14%)
  Pallas kernels  5.76 us (13%)
  local copies, waits for them, and re-layouts  3.68 us (9%)
  starting transfers between devices  2.72 us (6%)
    all_to_all x1, blocking collectives, body(): lax.all_to_all(outgoing, 'tile', split_axis=0, concat_axis=0, tiled=True)  24.1 us
    ppermute x1, waiting for transfers between devices, body(): lax.ppermute(sky, 'tile', [pair for i in range(1, tiles - 1, 2) for pair...  6.07 us
    unnamed x17, local copies, waits for them, and re-layouts  3.68 us
    pallas_call x1, Pallas kernels, body(): pl.pallas_call(functools.partial(stack_kernel, cells), out_shape=jax.Shap...  3.65 us
    ppermute x1, starting transfers between devices, body(): lax.ppermute(sky, 'tile', [pair for i in range(1, tiles - 1, 2) for pair...  2.28 us
    pallas_call x1, Pallas kernels, body(): pl.pallas_call(functools.partial(pack_kernel, capacity), out_shape=jax.Sh...  1.38 us
  transfers between devices with their start and end apart: 2, of which 1 were waited for; matrix products, arithmetic and copies ran while one was open for 0% of the time, Pallas kernels for 0%

profile of v1, /device:TPU:1, one launch (start us, length us, event | category | flops | bytes accessed | tf_op | source)
XLA Modules:
  0.0 42.4 jit_solution(17643654945119748102)
XLA Ops:
  0.0 0.0 copy-start.5
  0.0 0.0 copy-start.6
  0.0 0.0 copy-start.7
  0.0 0.8 %copy.10.tile_ref = s32[4,8,1]{2,1,0:T(8,128)S(1)} copy(s32[4,8,1]{1,2,0:T(1,128)} %param.11) | data formatting | bytes 256 | tf_op args[2]
  0.8 0.0 copy-done.5
  0.8 0.0 copy-done.6
  0.8 0.0 copy-done.7
  0.8 0.0 copy-start
  0.8 1.0 %copy-done = f32[8,128,128]{2,1,0:T(8,128)S(1)} copy-done((f32[8,128,128]{2,1,0:T(8,128)S(1)}, f32[8,128,128]{2,1,0:T(8,128)}, u32[]{:S(2)}) %copy-start) | copy-done | bytes 524312
  1.9 0.0 copy-start.1
  1.9 0.9 %copy-done.1 = f32[4,8,8,128]{3,2,1,0:T(8,128)S(1)} copy-done((f32[4,8,8,128]{3,2,1,0:T(8,128)S(1)}, f32[4,8,8,128]{3,2,1,0:T(8,128)}, u32[]{:S(2)}) %copy-start.1) | copy-done | bytes 131096
  2.8 0.0 copy-start.2
  2.8 0.9 %copy-done.2 = f32[4,8,8,128]{3,2,1,0:T(8,128)S(1)} copy-done((f32[4,8,8,128]{3,2,1,0:T(8,128)S(1)}, f32[4,8,8,128]{3,2,1,0:T(8,128)}, u32[]{:S(2)}) %copy-start.2) | copy-done | bytes 131096
  3.7 1.4 %pack.1 = f32[16,9,8,128]{3,2,1,0:T(8,128)S(1)} custom-call(s32[4,8,1]{2,1,0:T(8,128)S(1)} %copy.10.tile_ref, s32[4,8]{1,0:T(4,128)S(1)} %copy-done.5, s32[4,8]{1,0:T(4,128)S(1)} %copy-done.6, f32[4,8]{1,0:T(4,128)S(1)} %copy-done.7, f32[4,8,8,128]{3,2,1,0:T(8,128)S(1)} %copy-done.1, f32[4,8,8,128]{3,2,1,0:T(8,128)S(1)} %copy-done.2, f32[8,128,128]{2,1,0:T(8,128)S(1)} %copy-done), custom_call_target="tpu_custom_call" | custom-call | tf_op jit(solution)/shard_map/pack/pallas_call | solution.py:126
  5.1 24.1 %all_to_all.5.in_ref = f32[16,9,8,128]{3,2,1,0:T(8,128)S(1)} all-to-all(f32[16,9,8,128]{3,2,1,0:T(8,128)S(1)} %pack.1), channel_id=1, replica_groups=mesh['field'=2,'tile'=16] {'tile'}, dimensions={0} | all-to-all | bytes 1179648 | tf_op jit(solution)/shard_map/all_to_all | solution.py:138
  29.2 0.7 %sum_slots.1.own_ref = f32[64,8,128]{2,1,0:T(8,128)S(1)} custom-call(f32[16,9,8,128]{3,2,1,0:T(8,128)S(1)} %all_to_all.5.in_ref), custom_call_target="tpu_custom_call" | custom-call | tf_op jit(solution)/shard_map/sum_slots/pallas_call | solution.py:139
  29.9 0.4 %collective-permute-start = (f32[64,8,128]{2,1,0:T(8,128)S(1)}, f32[64,8,128]{2,1,0:T(8,128)S(1)}, u32[]{:S(2)}, u32[]{:S(2)}) collective-permute-start(f32[64,8,128]{2,1,0:T(8,128)S(1)} %sum_slots.1.own_ref), channel_id=1, source_target_pairs={{0,1},{1,0},{2,3},{3,2},{4,5},{5,4},{6,7},{7,6},{8,9},{9,8},{10,11... | collective-permute-start | bytes 786440 | tf_op jit(solution)/shard_map/ppermute | solution.py:147
  30.4 2.3 %collective-permute-start.1 = (f32[64,8,128]{2,1,0:T(8,128)S(1)}, f32[64,8,128]{2,1,0:T(8,128)S(1)}, u32[]{:S(2)}, u32[]{:S(2)}) collective-permute-start(f32[64,8,128]{2,1,0:T(8,128)S(1)} %sum_slots.1.own_ref), channel_id=1, source_target_pairs={{1,2},{2,1},{3,4},{4,3},{5,6},{6,5},{7,8},{8,7},{9,10},{10,9},{11,... | collective-permute-start | bytes 786440 | tf_op jit(solution)/shard_map/ppermute | solution.py:148
  32.7 0.0 copy-start.4
  32.7 0.0 copy-start.3
  32.7 0.0 collective-permute-done.twin_ref
  32.7 6.1 %collective-permute-done.1.far_ref = f32[64,8,128]{2,1,0:T(8,128)S(1)} collective-permute-done((f32[64,8,128]{2,1,0:T(8,128)S(1)}, f32[64,8,128]{2,1,0:T(8,128)S(1)}, u32[]{:S(2)}, u32[]{:S(2)}) %collective-permute-start.1) | collective-permute-done | bytes 262176 | tf_op jit(solution)/shard_map/ppermute | solution.py:148
  38.8 0.0 copy-done.4
  38.8 0.0 copy-done.3
  38.8 3.6 %stack.1 = f32[8,512]{1,0:T(8,128)} custom-call(s32[8,16]{1,0:T(8,128)S(1)} %copy-done.3, s32[8,16]{1,0:T(8,128)S(1)} %copy-done.4, s32[1]{0:T(128)} %bitcast.odd_ref, f32[64,8,128]{2,1,0:T(8,128)S(1)} %sum_slots.1.own_ref, f32[64,8,128]{2,1,0:T(8,128)S(1)} %collective-permute-done.twin_ref, f32[64,8,128]{2,1,0:T(8,128)S(1)} %collective-permute-done.1.far_ref), custom_call_target="tpu_custom_call" | custom-call | tf_op jit(solution)/shard_map/stack/pallas_call | solution.py:152
Async XLA Ops:
  0.0 0.8 %copy-start.5 = (s32[4,8]{1,0:T(4,128)S(1)}, s32[4,8]{1,0:T(4,128)}, u32[]{:S(2)}) copy-start(s32[4,8]{1,0:T(4,128)} %cell_ref.1) | copy-start | bytes 388
  0.0 0.8 %copy-start.6 = (s32[4,8]{1,0:T(4,128)S(1)}, s32[4,8]{1,0:T(4,128)}, u32[]{:S(2)}) copy-start(s32[4,8]{1,0:T(4,128)} %id_ref.1) | copy-start | bytes 388
  0.0 0.8 %copy-start.7 = (f32[4,8]{1,0:T(4,128)S(1)}, f32[4,8]{1,0:T(4,128)}, u32[]{:S(2)}) copy-start(f32[4,8]{1,0:T(4,128)} %weight_ref.1) | copy-start | bytes 388
  0.8 1.0 %copy-start = (f32[8,128,128]{2,1,0:T(8,128)S(1)}, f32[8,128,128]{2,1,0:T(8,128)}, u32[]{:S(2)}) copy-start(f32[8,128,128]{2,1,0:T(8,128)} %table_ref.1) | copy-start | bytes 1572868
  1.9 0.9 %copy-start.1 = (f32[4,8,8,128]{3,2,1,0:T(8,128)S(1)}, f32[4,8,8,128]{3,2,1,0:T(8,128)}, u32[]{:S(2)}) copy-start(f32[4,8,8,128]{3,2,1,0:T(8,128)} %psi_ref.1) | copy-start | bytes 393220
  2.8 0.9 %copy-start.2 = (f32[4,8,8,128]{3,2,1,0:T(8,128)S(1)}, f32[4,8,8,128]{3,2,1,0:T(8,128)}, u32[]{:S(2)}) copy-start(f32[4,8,8,128]{3,2,1,0:T(8,128)} %phi_ref.1) | copy-start | bytes 393220
  29.9 2.8 %collective-permute-start = (f32[64,8,128]{2,1,0:T(8,128)S(1)}, f32[64,8,128]{2,1,0:T(8,128)S(1)}, u32[]{:S(2)}, u32[]{:S(2)}) collective-permute-start(f32[64,8,128]{2,1,0:T(8,128)S(1)} %sum_slots.1.own_ref), channel_id=1, source_target_pairs={{0,1},{1,0},{2,3},{3,2},{4,5},{5,4},{6,7},{7,6},{8,9},{9,8},{10,11... | collective-permute-start | bytes 786440 | tf_op jit(solution)/shard_map/ppermute | solution.py:147
  30.4 8.4 %collective-permute-start.1 = (f32[64,8,128]{2,1,0:T(8,128)S(1)}, f32[64,8,128]{2,1,0:T(8,128)S(1)}, u32[]{:S(2)}, u32[]{:S(2)}) collective-permute-start(f32[64,8,128]{2,1,0:T(8,128)S(1)} %sum_slots.1.own_ref), channel_id=1, source_target_pairs={{1,2},{2,1},{3,4},{4,3},{5,6},{6,5},{7,8},{8,7},{9,10},{10,9},{11,... | collective-permute-start | bytes 786440 | tf_op jit(solution)/shard_map/ppermute | solution.py:148
  32.7 6.1 %copy-start.4 = (s32[8,16]{1,0:T(8,128)S(1)}, s32[8,16]{1,0:T(8,128)}, u32[]{:S(2)}) copy-start(s32[8,16]{1,0:T(8,128)} %col_ref.1) | copy-start | bytes 1540
  32.7 6.1 %copy-start.3 = (s32[8,16]{1,0:T(8,128)S(1)}, s32[8,16]{1,0:T(8,128)}, u32[]{:S(2)}) copy-start(s32[8,16]{1,0:T(8,128)} %row_ref.1) | copy-start | bytes 1540

commit v2 on v1

--- a/solution.py
+++ b/solution.py
@@ -15,11 +15,26 @@
 LIMIT = pltpu.CompilerParams(vmem_limit_bytes=32 * 1024 * 1024)
 
 
-def pack_kernel(
-    capacity, tile_ref, cell_ref, id_ref, weight_ref, psi_ref, phi_ref, table_ref, out_ref, diag_ref, used_ref
-):
+def pack_kernel(capacity, *refs):
+    given, out_ref, (diag_ref, used_ref), held, sems = refs[:7], refs[7], refs[8:10], refs[10:17], refs[17]
+    copies = [
+        pltpu.make_async_copy(source, target, sems.at[index])
+        for index, (source, target) in enumerate(zip(given, held, strict=True))
+    ]
+    for copy in copies:
+        copy.start()
+    tile_ref, cell_ref, id_ref, weight_ref, psi_ref, phi_ref, table_ref = held
     cells, epochs = psi_ref.shape[:2]
     tiles, width = out_ref.shape[0], psi_ref.shape[3]
+
+    def clear(tile, carry):
+        used_ref[tile] = 0
+        out_ref[tile, 2 * capacity] = jnp.zeros(out_ref.shape[2:], jnp.float32)
+        return carry
+
+    lax.fori_loop(0, tiles, clear, 0)
+    for copy in copies:
+        copy.wait()
 
     source = lax.broadcasted_iota(jnp.int32, (width, width), 0)
     target = lax.broadcasted_iota(jnp.int32, (width, width), 1)
@@ -29,16 +44,10 @@
             row = jnp.sum(jnp.where(mask, table_ref[index], 0.0), axis=0, keepdims=True)
             diag_ref[index, place : place + 1, :] = row
 
-    def clear(tile, carry):
-        used_ref[tile] = 0
-        out_ref[tile, 2 * capacity] = jnp.zeros(out_ref.shape[2:], jnp.float32)
-        return carry
-
-    lax.fori_loop(0, tiles, clear, 0)
     lane = lax.broadcasted_iota(jnp.int32, (1, LANES), 1)
     for block in range(cells):
         for epoch in range(epochs):
-            tile = tile_ref[block, epoch, 0]
+            tile = tile_ref[block, 0, epoch]
             slot = used_ref[tile]
             used_ref[tile] = slot + 1
             bands = diag_ref[id_ref[block, epoch]] * weight_ref[block, epoch]
@@ -113,7 +122,7 @@
         ]
 
     start = [jnp.full((rows, LANES), -jnp.inf, jnp.float32) for _ in range(cells)]
-    highest = lax.fori_loop(0, vels, one_velocity, start)
+    highest = lax.fori_loop(0, vels, one_velocity, start, unroll=4)
     for cell in range(cells):
         best_ref[:, cell * LANES : (cell + 1) * LANES] = highest[cell]
 
@@ -123,18 +132,22 @@
     cells, epochs, rows, width = psi.shape
     capacity = max(2, 2 * cells * epochs // tiles)
     message = (tiles, 2 * capacity + 1, rows, width)
+    given = (jnp.swapaxes(dest_tile, 1, 2), dest_cell, kernel_id, weight, psi, phi, kernels)
     outgoing = pl.pallas_call(
         functools.partial(pack_kernel, capacity),
         out_shape=jax.ShapeDtypeStruct(message, jnp.float32),
-        in_specs=[SMEM] * 4 + [VMEM] * 3,
+        in_specs=[pl.BlockSpec(memory_space=pl.ANY)] * 7,
         out_specs=VMEM,
         scratch_shapes=[
             pltpu.VMEM((kernels.shape[0], 3, width), jnp.float32),
             pltpu.SMEM((tiles,), jnp.int32),
-        ],
-        compiler_params=LIMIT,
+        ]
+        + [pltpu.SMEM(array.shape, array.dtype) for array in given[:4]]
+        + [pltpu.VMEM(array.shape, array.dtype) for array in given[4:]]
+        + [pltpu.SemaphoreType.DMA((7,))],
+        compiler_params=pltpu.CompilerParams(vmem_limit_bytes=60 * 1024 * 1024),
         name="pack",
-    )(dest_tile, dest_cell, kernel_id, weight, psi, phi, kernels)
+    )(*given)
     incoming = lax.all_to_all(outgoing, "tile", split_axis=0, concat_axis=0, tiled=True)
     sky = pl.pallas_call(
         functools.partial(sum_kernel, capacity, cells),

time: 43.1 us -> 39.7 us (0.921)
  local copies, waits for them, and re-layouts: 3.68 us -> 0.01 us
    unnamed x17 -> x4, local copies, waits for them, and re-layouts: 3.68 us -> 0.01 us
    pallas_call x1, Pallas kernels: 1.38 us -> 2.39 us  [body(): pl.pallas_call(functools.partial(pack_kernel, capacity), out_shape=jax.Sh...]
    pallas_call x1, Pallas kernels: 3.65 us -> 2.78 us  [body(): pl.pallas_call(functools.partial(stack_kernel, cells), out_shape=jax.Shap...]
where the time goes in v2:
time: 39.7 us; the launch traced here: 39.1 us
  blocking collectives  24.3 us (61%)
  waiting for transfers between devices  6.07 us (15%)
  Pallas kernels  5.89 us (15%)
  starting transfers between devices  2.73 us (7%)
    all_to_all x1, blocking collectives, body(): lax.all_to_all(outgoing, 'tile', split_axis=0, concat_axis=0, tiled=True)  24.3 us
    ppermute x1, waiting for transfers between devices, body(): lax.ppermute(sky, 'tile', [pair for i in range(1, tiles - 1, 2) for pair...  6.07 us
    pallas_call x1, Pallas kernels, body(): pl.pallas_call(functools.partial(stack_kernel, cells), out_shape=jax.Shap...  2.78 us
    pallas_call x1, Pallas kernels, body(): pl.pallas_call(functools.partial(pack_kernel, capacity), out_shape=jax.Sh...  2.39 us
    ppermute x1, starting transfers between devices, body(): lax.ppermute(sky, 'tile', [pair for i in range(1, tiles - 1, 2) for pair...  2.27 us
  transfers between devices with their start and end apart: 2, of which 1 were waited for; matrix products, arithmetic and copies ran while one was open for 0% of the time, Pallas kernels for 0%

profile of v2, /device:TPU:1, one launch (start us, length us, event | category | flops | bytes accessed | tf_op | source)
XLA Modules:
  0.0 39.1 jit_solution(11064568928012277592)
XLA Ops:
  0.0 2.4 %pack.1 = f32[16,9,8,128]{3,2,1,0:T(8,128)} custom-call(s32[4,1,8]{2,1,0:T(1,128)} %bitcast.4, s32[4,8]{1,0:T(4,128)} %refs_1_.1, s32[4,8]{1,0:T(4,128)} %refs_2_.1, f32[4,8]{1,0:T(4,128)} %refs_3_.1, f32[4,8,8,128]{3,2,1,0:T(8,128)} %refs_4_.1, f32[4,8,8,128]{3,2,1,0:T(8,128)} %refs_5_.1, f32[8,128,128]{2,1,0:T(8,128)} %refs_6_.1), custom_call_target="tpu_custom_call" | custom-call | tf_op jit(solution)/shard_map/pack/pallas_call | solution.py:136
  2.4 24.3 %all_to_all.5.in_ref = f32[16,9,8,128]{3,2,1,0:T(8,128)S(1)} all-to-all(f32[16,9,8,128]{3,2,1,0:T(8,128)} %pack.1), channel_id=1, replica_groups=mesh['field'=2,'tile'=16] {'tile'}, dimensions={0} | all-to-all | bytes 1179648 | tf_op jit(solution)/shard_map/all_to_all | solution.py:151
  26.7 0.7 %sum_slots.1.own_ref = f32[64,8,128]{2,1,0:T(8,128)S(1)} custom-call(f32[16,9,8,128]{3,2,1,0:T(8,128)S(1)} %all_to_all.5.in_ref), custom_call_target="tpu_custom_call" | custom-call | tf_op jit(solution)/shard_map/sum_slots/pallas_call | solution.py:152
  27.5 0.5 %collective-permute-start = (f32[64,8,128]{2,1,0:T(8,128)S(1)}, f32[64,8,128]{2,1,0:T(8,128)S(1)}, u32[]{:S(2)}, u32[]{:S(2)}) collective-permute-start(f32[64,8,128]{2,1,0:T(8,128)S(1)} %sum_slots.1.own_ref), channel_id=1, source_target_pairs={{0,1},{1,0},{2,3},{3,2},{4,5},{5,4},{6,7},{7,6},{8,9},{9,8},{10,11... | collective-permute-start | bytes 786440 | tf_op jit(solution)/shard_map/ppermute | solution.py:160
  27.9 2.3 %collective-permute-start.1 = (f32[64,8,128]{2,1,0:T(8,128)S(1)}, f32[64,8,128]{2,1,0:T(8,128)S(1)}, u32[]{:S(2)}, u32[]{:S(2)}) collective-permute-start(f32[64,8,128]{2,1,0:T(8,128)S(1)} %sum_slots.1.own_ref), channel_id=1, source_target_pairs={{1,2},{2,1},{3,4},{4,3},{5,6},{6,5},{7,8},{8,7},{9,10},{10,9},{11,... | collective-permute-start | bytes 786440 | tf_op jit(solution)/shard_map/ppermute | solution.py:161
  30.2 0.0 copy-start.1
  30.2 0.0 copy-start
  30.2 0.0 collective-permute-done.twin_ref
  30.2 6.1 %collective-permute-done.1.far_ref = f32[64,8,128]{2,1,0:T(8,128)S(1)} collective-permute-done((f32[64,8,128]{2,1,0:T(8,128)S(1)}, f32[64,8,128]{2,1,0:T(8,128)S(1)}, u32[]{:S(2)}, u32[]{:S(2)}) %collective-permute-start.1) | collective-permute-done | bytes 262176 | tf_op jit(solution)/shard_map/ppermute | solution.py:161
  36.3 0.0 copy-done.1
  36.3 0.0 copy-done
  36.3 2.8 %stack.1 = f32[8,512]{1,0:T(8,128)} custom-call(s32[8,16]{1,0:T(8,128)S(1)} %copy-done, s32[8,16]{1,0:T(8,128)S(1)} %copy-done.1, s32[1]{0:T(128)} %bitcast.odd_ref, f32[64,8,128]{2,1,0:T(8,128)S(1)} %sum_slots.1.own_ref, f32[64,8,128]{2,1,0:T(8,128)S(1)} %collective-permute-done.twin_ref, f32[64,8,128]{2,1,0:T(8,128)S(1)} %collective-permute-done.1.far_ref), custom_call_target="tpu_custom_call" | custom-call | tf_op jit(solution)/shard_map/stack/pallas_call | solution.py:165
Async XLA Ops:
  27.5 2.8 %collective-permute-start = (f32[64,8,128]{2,1,0:T(8,128)S(1)}, f32[64,8,128]{2,1,0:T(8,128)S(1)}, u32[]{:S(2)}, u32[]{:S(2)}) collective-permute-start(f32[64,8,128]{2,1,0:T(8,128)S(1)} %sum_slots.1.own_ref), channel_id=1, source_target_pairs={{0,1},{1,0},{2,3},{3,2},{4,5},{5,4},{6,7},{7,6},{8,9},{9,8},{10,11... | collective-permute-start | bytes 786440 | tf_op jit(solution)/shard_map/ppermute | solution.py:160
  27.9 8.4 %collective-permute-start.1 = (f32[64,8,128]{2,1,0:T(8,128)S(1)}, f32[64,8,128]{2,1,0:T(8,128)S(1)}, u32[]{:S(2)}, u32[]{:S(2)}) collective-permute-start(f32[64,8,128]{2,1,0:T(8,128)S(1)} %sum_slots.1.own_ref), channel_id=1, source_target_pairs={{1,2},{2,1},{3,4},{4,3},{5,6},{6,5},{7,8},{8,7},{9,10},{10,9},{11,... | collective-permute-start | bytes 786440 | tf_op jit(solution)/shard_map/ppermute | solution.py:161
  30.2 6.1 %copy-start.1 = (s32[8,16]{1,0:T(8,128)S(1)}, s32[8,16]{1,0:T(8,128)}, u32[]{:S(2)}) copy-start(s32[8,16]{1,0:T(8,128)} %col_ref.1) | copy-start | bytes 1540
  30.2 6.1 %copy-start = (s32[8,16]{1,0:T(8,128)S(1)}, s32[8,16]{1,0:T(8,128)}, u32[]{:S(2)}) copy-start(s32[8,16]{1,0:T(8,128)} %row_ref.1) | copy-start | bytes 1540

commit v3 on v2

--- a/solution.py
+++ b/solution.py
@@ -78,10 +78,21 @@
                 sky_ref[base + kind * cells] = sky_ref[base + kind * cells] + value
         return carry
 
-    lax.fori_loop(0, in_ref.shape[0], one_source, 0, unroll=4)
-
-
-def stack_kernel(cells, row_ref, col_ref, odd_ref, own_ref, twin_ref, far_ref, best_ref, wide_ref):
+    lax.fori_loop(0, in_ref.shape[0], one_source, 0, unroll=16)
+
+
+def shift_kernel(row_ref, col_ref, odd_ref, after_ref, row_out, col_out, odd_out):
+    def one_epoch(epoch, carry):
+        for vel in range(row_ref.shape[1]):
+            row_out[epoch, vel] = row_ref[epoch, vel]
+            col_out[epoch, vel] = col_ref[epoch, vel]
+        return carry
+
+    lax.fori_loop(0, row_ref.shape[0], one_epoch, 0)
+    odd_out[0] = odd_ref[0]
+
+
+def stack_kernel(cells, row_ref, col_ref, odd_ref, own_ref, far_ref, twin_ref, best_ref, wide_ref):
     epochs, vels = row_ref.shape
     rows = own_ref.shape[1]
     odd = odd_ref[0]
@@ -145,9 +156,9 @@
         + [pltpu.SMEM(array.shape, array.dtype) for array in given[:4]]
         + [pltpu.VMEM(array.shape, array.dtype) for array in given[4:]]
         + [pltpu.SemaphoreType.DMA((7,))],
-        compiler_params=pltpu.CompilerParams(vmem_limit_bytes=60 * 1024 * 1024),
+        compiler_params=pltpu.CompilerParams(vmem_limit_bytes=32 * 1024 * 1024),
         name="pack",
-    )(*given)
+    )(*(pltpu.with_memory_space_constraint(array, pltpu.HBM) for array in given))
     incoming = lax.all_to_all(outgoing, "tile", split_axis=0, concat_axis=0, tiled=True)
     sky = pl.pallas_call(
         functools.partial(sum_kernel, capacity, cells),
@@ -157,11 +168,20 @@
         compiler_params=LIMIT,
         name="sum_slots",
     )(incoming)
-    twin = lax.ppermute(sky, "tile", [(i, i ^ 1) for i in range(tiles)])
     far = lax.ppermute(
         sky, "tile", [pair for i in range(1, tiles - 1, 2) for pair in ((i, i + 1), (i + 1, i))]
     )
+    twin = lax.ppermute(sky, "tile", [(i, i ^ 1) for i in range(tiles)])
     odd = (lax.axis_index("tile") & 1).reshape(1)
+    scalars = (row_offsets, col_offsets, odd)
+    scalars = pl.pallas_call(
+        shift_kernel,
+        out_shape=[pltpu.SMEM(array.shape, array.dtype) for array in scalars],
+        in_specs=[SMEM] * 3 + [pl.BlockSpec(memory_space=pl.ANY)],
+        out_specs=[SMEM] * 3,
+        compiler_params=LIMIT,
+        name="shifts",
+    )(*scalars, sky)
     return pl.pallas_call(
         functools.partial(stack_kernel, cells),
         out_shape=jax.ShapeDtypeStruct((rows, cells * width), jnp.float32),
@@ -170,7 +190,7 @@
         scratch_shapes=[pltpu.VMEM((epochs, 2, cells + 2, 3 * rows, width), jnp.float32)],
         compiler_params=LIMIT,
         name="stack",
-    )(row_offsets, col_offsets, odd, sky, twin, far)
+    )(*scalars, sky, far, twin)
 
 
 def solution(mesh):

time: 39.7 us -> 37.2 us (0.937)
  waiting for transfers between devices: 6.07 us -> 4.37 us
  Pallas kernels: 5.89 us -> 5.03 us
  local copies, waits for them, and re-layouts: 0.01 us -> 0.69 us
    ppermute x1, waiting for transfers between devices: 6.07 us -> 4.36 us  [body(): lax.ppermute(sky, 'tile', [pair for i in range(1, tiles - 1, 2) for pair...]
    pallas_call x0 -> x1, Pallas kernels: none -> 0.95 us  [body(): pl.pallas_call(shift_kernel, out_shape=[pltpu.SMEM(array.shape, array.dty...]
    pallas_call x1, Pallas kernels: 2.39 us -> 1.56 us  [body(): pl.pallas_call(functools.partial(pack_kernel, capacity), out_shape=jax.Sh...]
    unnamed x4, local copies, waits for them, and re-layouts: 0.01 us -> 0.69 us
    pallas_call x1, Pallas kernels: 2.78 us -> 2.12 us  [body(): pl.pallas_call(functools.partial(stack_kernel, cells), out_shape=jax.Shap...]
  transfers between devices with their start and end apart: 2 -> 2, of which waited for: 1 -> 1; matrix products, arithmetic and copies ran while one was open for 0% -> 0% of each run, Pallas kernels for 0% -> 3%
where the time goes in v3:
time: 37.2 us; the launch traced here: 36.9 us
  blocking collectives  24.1 us (65%)
  Pallas kernels  5.03 us (14%)
  waiting for transfers between devices  4.37 us (12%)
  starting transfers between devices  2.62 us (7%)
  local copies, waits for them, and re-layouts  0.69 us (2%)
    all_to_all x1, blocking collectives, body(): lax.all_to_all(outgoing, 'tile', split_axis=0, concat_axis=0, tiled=True)  24.1 us
    ppermute x1, waiting for transfers between devices, body(): lax.ppermute(sky, 'tile', [pair for i in range(1, tiles - 1, 2) for pair...  4.36 us
    ppermute x1, starting transfers between devices, body(): lax.ppermute(sky, 'tile', [pair for i in range(1, tiles - 1, 2) for pair...  2.55 us
    pallas_call x1, Pallas kernels, body(): pl.pallas_call(functools.partial(stack_kernel, cells), out_shape=jax.Shap...  2.12 us
    pallas_call x1, Pallas kernels, body(): pl.pallas_call(functools.partial(pack_kernel, capacity), out_shape=jax.Sh...  1.56 us
    pallas_call x1, Pallas kernels, body(): pl.pallas_call(shift_kernel, out_shape=[pltpu.SMEM(array.shape, array.dty...  0.95 us
  transfers between devices with their start and end apart: 2, of which 1 were waited for; matrix products, arithmetic and copies ran while one was open for 0% of the time, Pallas kernels for 3%

profile of v3, /device:TPU:1, one launch (start us, length us, event | category | flops | bytes accessed | tf_op | source)
XLA Modules:
  0.0 36.9 jit_solution(10941581732629757197)
XLA Ops:
  0.0 1.6 %pack.1 = f32[16,9,8,128]{3,2,1,0:T(8,128)S(1)} custom-call(s32[4,1,8]{2,1,0:T(1,128)} %bitcast.4, s32[4,8]{1,0:T(4,128)} %refs_1_.1, s32[4,8]{1,0:T(4,128)} %refs_2_.1, f32[4,8]{1,0:T(4,128)} %refs_3_.1, f32[4,8,8,128]{3,2,1,0:T(8,128)} %refs_4_.1, f32[4,8,8,128]{3,2,1,0:T(8,128)} %refs_5_.1, f32[8,128,128]{2,1,0:T(8,128)} %refs_6_.1), custom_call_target="tpu_custom_call" | custom-call | tf_op jit(solution)/shard_map/pack/pallas_call | solution.py:147
  1.6 24.1 %all_to_all.5.in_ref = f32[16,9,8,128]{3,2,1,0:T(8,128)S(1)} all-to-all(f32[16,9,8,128]{3,2,1,0:T(8,128)S(1)} %pack.1), channel_id=1, replica_groups=mesh['field'=2,'tile'=16] {'tile'}, dimensions={0} | all-to-all | bytes 1179648 | tf_op jit(solution)/shard_map/all_to_all | solution.py:162
  25.7 0.4 %sum_slots.1.after_ref.own_ref = f32[64,8,128]{2,1,0:T(8,128)S(1)} custom-call(f32[16,9,8,128]{3,2,1,0:T(8,128)S(1)} %all_to_all.5.in_ref), custom_call_target="tpu_custom_call" | custom-call | tf_op jit(solution)/shard_map/sum_slots/pallas_call | solution.py:163
  26.1 2.5 %collective-permute-start = (f32[64,8,128]{2,1,0:T(8,128)S(1)}, f32[64,8,128]{2,1,0:T(8,128)S(1)}, u32[]{:S(2)}, u32[]{:S(2)}) collective-permute-start(f32[64,8,128]{2,1,0:T(8,128)S(1)} %sum_slots.1.after_ref.own_ref), channel_id=1, source_target_pairs={{1,2},{2,1},{3,4},{4,3},{5,6},{6,5},{7,8},{8,7},{9,10},{10,9},{11,... | collective-permute-start | bytes 786440 | tf_op jit(solution)/shard_map/ppermute | solution.py:171
  28.7 0.1 collective-permute-start.1
  28.7 0.0 copy-start.1
  28.8 0.0 copy-start
  28.8 0.7 %copy-done.1 = s32[8,16]{1,0:T(8,128)S(1)} copy-done((s32[8,16]{1,0:T(8,128)S(1)}, s32[8,16]{1,0:T(8,128)}, u32[]{:S(2)}) %copy-start.1) | copy-done | bytes 536
  29.4 0.0 copy-done
  29.4 0.9 %shifts.1 = (s32[8,16]{1,0:T(8,128)S(4)}, s32[8,16]{1,0:T(8,128)S(4)}, s32[1]{0:T(128)S(4)}) custom-call(s32[8,16]{1,0:T(8,128)S(1)} %copy-done, s32[8,16]{1,0:T(8,128)S(1)} %copy-done.1, s32[1]{0:T(128)} %bitcast.odd_ref, f32[64,8,128]{2,1,0:T(8,128)S(1)} %sum_slots.1.after_ref.own_ref), custom_call_target="tpu_custom_call" | custom-call | tf_op jit(solution)/shard_map/shifts/pallas_call | solution.py:177
  30.4 4.4 %collective-permute-done.far_ref = f32[64,8,128]{2,1,0:T(8,128)S(1)} collective-permute-done((f32[64,8,128]{2,1,0:T(8,128)S(1)}, f32[64,8,128]{2,1,0:T(8,128)S(1)}, u32[]{:S(2)}, u32[]{:S(2)}) %collective-permute-start) | collective-permute-done | bytes 262176 | tf_op jit(solution)/shard_map/ppermute | solution.py:171
  34.8 0.0 collective-permute-done.1.twin_ref
  34.8 2.1 %stack.1 = f32[8,512]{1,0:T(8,128)} custom-call(s32[8,16]{1,0:T(8,128)S(4)} %get-tuple-element.8.row_ref, s32[8,16]{1,0:T(8,128)S(4)} %get-tuple-element.9.col_ref, s32[1]{0:T(128)S(4)} %get-tuple-element.10.odd_ref, f32[64,8,128]{2,1,0:T(8,128)S(1)} %sum_slots.1.after_ref.own_ref, f32[64,8,128]{2,1,0:T(8,128)S(1)} %collective-permute-done.far_ref, ...), custom_call_target="tpu_custom_call" | custom-call | tf_op jit(solution)/shard_map/stack/pallas_call | solution.py:185
Async XLA Ops:
  26.1 8.7 %collective-permute-start = (f32[64,8,128]{2,1,0:T(8,128)S(1)}, f32[64,8,128]{2,1,0:T(8,128)S(1)}, u32[]{:S(2)}, u32[]{:S(2)}) collective-permute-start(f32[64,8,128]{2,1,0:T(8,128)S(1)} %sum_slots.1.after_ref.own_ref), channel_id=1, source_target_pairs={{1,2},{2,1},{3,4},{4,3},{5,6},{6,5},{7,8},{8,7},{9,10},{10,9},{11,... | collective-permute-start | bytes 786440 | tf_op jit(solution)/shard_map/ppermute | solution.py:171
  28.7 6.1 %collective-permute-start.1 = (f32[64,8,128]{2,1,0:T(8,128)S(1)}, f32[64,8,128]{2,1,0:T(8,128)S(1)}, u32[]{:S(2)}, u32[]{:S(2)}) collective-permute-start(f32[64,8,128]{2,1,0:T(8,128)S(1)} %sum_slots.1.after_ref.own_ref), channel_id=1, source_target_pairs={{0,1},{1,0},{2,3},{3,2},{4,5},{5,4},{6,7},{7,6},{8,9},{9,8},{10,11... | collective-permute-start | bytes 786440 | tf_op jit(solution)/shard_map/ppermute | solution.py:174
  28.7 0.7 %copy-start.1 = (s32[8,16]{1,0:T(8,128)S(1)}, s32[8,16]{1,0:T(8,128)}, u32[]{:S(2)}) copy-start(s32[8,16]{1,0:T(8,128)} %col_ref.1) | copy-start | bytes 1540
  28.8 0.7 %copy-start = (s32[8,16]{1,0:T(8,128)S(1)}, s32[8,16]{1,0:T(8,128)}, u32[]{:S(2)}) copy-start(s32[8,16]{1,0:T(8,128)} %row_ref.1) | copy-start | bytes 1540

commit v4 on v2

v4 whole, which is shorter than its diff:
```python
import functools

import jax
import jax.numpy as jnp
from jax import lax
from jax.experimental import pallas as pl
from jax.experimental.pallas import tpu as pltpu
from jax.sharding import PartitionSpec as P

XREACH = 64
RREACH = 8
LANES = 128
GROUP = 24
VMEM = pl.BlockSpec(memory_space=pltpu.VMEM)
SMEM = pl.BlockSpec(memory_space=pltpu.SMEM)
LIMIT = pltpu.CompilerParams(vmem_limit_bytes=32 * 1024 * 1024)


def pack_kernel(capacity, *refs):
    given, out_ref, (diag_ref, note_ref, used_ref, spot_ref), held, sems = (
        refs[:7], refs[7], refs[8:12], refs[12:19], refs[19]
    )
    copies = [
        pltpu.make_async_copy(source, target, sems.at[index])
        for index, (source, target) in enumerate(zip(given, held, strict=True))
    ]
    for copy in copies[::-1]:
        copy.start()
    tile_ref, cell_ref, id_ref, weight_ref, psi_ref, phi_ref, table_ref = held
    cells, epochs = psi_ref.shape[:2]
    tiles, width = used_ref.shape[0], psi_ref.shape[3]
    stride = 2 * capacity + 1

    def clear(tile, carry):
        used_ref[tile] = 0
        note_ref[tile] = jnp.zeros(note_ref.shape[1:], jnp.float32)
        return carry

    lax.fori_loop(0, tiles, clear, 0, unroll=16)
    for copy in copies[:4]:
        copy.wait()

    lane = lax.broadcasted_iota(jnp.int32, (1, LANES), 1)
    for block in range(cells):
        for epoch in range(epochs):
            tile = tile_ref[block, 0, epoch]
            slot = used_ref[tile]
            used_ref[tile] = slot + 1
            spot_ref[block, epoch] = tile * stride + 2 * slot
            place = (epoch * 2 * cells + cell_ref[block, epoch] + 1).astype(jnp.float32)
            note_ref[tile] = jnp.where(lane == slot, place, note_ref[tile])
    for copy in copies[4:]:
        copy.wait()

    source = lax.broadcasted_iota(jnp.int32, (width, width), 0)
    target = lax.broadcasted_iota(jnp.int32, (width, width), 1)
    for place in range(3):
        mask = source == target + (place - 1)
        for index in range(table_ref.shape[0]):
            row = jnp.sum(jnp.where(mask, table_ref[index], 0.0), axis=0, keepdims=True)
            diag_ref[index, place : place + 1, :] = row

    def write_note(tile, carry):
        out_ref[tile * stride + 2 * capacity, 0:1, :] = note_ref[tile]
        return carry

    lax.fori_loop(0, tiles, write_note, 0, unroll=16)
    for block in range(cells):
        for epoch in range(epochs):
            spot = spot_ref[block, epoch]
            bands = diag_ref[id_ref[block, epoch]] * weight_ref[block, epoch]
            for kind, ref in enumerate((psi_ref, phi_ref)):
                values = ref[block, epoch]
                out_ref[spot + kind] = (
                    values * bands[1:2]
                    + pltpu.roll(values, 1, 1) * bands[0:1]
                    + pltpu.roll(values, width - 1, 1) * bands[2:3]
                )


def sum_kernel(capacity, cells, in_ref, sky_ref, *half_refs):
    for index in range(sky_ref.shape[0]):
        sky_ref[index] = jnp.zeros(sky_ref.shape[1:], jnp.float32)

    def one_source(source, carry):
        notes = in_ref[source, 2 * capacity].astype(jnp.int32)
        for slot in range(capacity):
            place = notes[0, slot] - 1
            there = place >= 0
            base = jnp.maximum(place, 0)
            for kind in range(2):
                value = jnp.where(there, in_ref[source, 2 * slot + kind], 0.0)
                sky_ref[base + kind * cells] = sky_ref[base + kind * cells] + value
        return carry

    lax.fori_loop(0, in_ref.shape[0], one_source, 0, unroll=16)
    for half, ref in enumerate(half_refs):
        for index in range(ref.shape[0]):
            ref[index] = sky_ref[half * ref.shape[0] + index]


def windows_at(ref, epoch, start_row, start_col, rows):
    first = lax.shift_right_logical(start_col, 7)
    shift = start_col & (LANES - 1)
    turn = (LANES - shift) & (LANES - 1)
    mask = lax.broadcasted_iota(jnp.int32, (rows, LANES), 1) >= shift
    windows = []
    for kind in range(2):
        parts = [
            ref[epoch, kind, first + step, pl.ds(start_row, rows), :]
            for step in range(ref.shape[2] - 1)
        ]
        windows.append(
            [
                pltpu.roll(jnp.where(mask, parts[cell], parts[cell + 1]), turn, 1)
                for cell in range(len(parts) - 1)
            ]
        )
    return windows


def clear_sides(ref, epoch, kind):
    for side in (0, ref.shape[2] - 1):
        ref[epoch, kind, side] = jnp.zeros(ref.shape[3:], jnp.float32)


def near_kernel(
    cells, group, row_ref, col_ref, odd_ref, own_ref, low_ref, high_ref, sums_ref, list_ref, count_ref, wide_ref
):
    epochs, vels = row_ref.shape
    rows = own_ref.shape[1]
    odd = odd_ref[0]
    twin_row = pl.multiple_of((1 - odd) * 2 * rows, rows)
    far_row = pl.multiple_of(odd * 2 * rows, rows)
    for epoch in range(epochs):
        for kind in range(2):
            clear_sides(wide_ref, epoch, kind)
            for cell in range(cells):
                index = (epoch * 2 + kind) * cells + cell
                wide_ref[epoch, kind, cell + 1, rows : 2 * rows, :] = own_ref[index]
                half, place = divmod(index, low_ref.shape[0])
                wide_ref[epoch, kind, cell + 1, pl.ds(twin_row, rows), :] = (low_ref, high_ref)[half][place]
                wide_ref[epoch, kind, cell + 1, pl.ds(far_row, rows), :] = jnp.zeros(
                    (rows, LANES), jnp.float32
                )

    def one_velocity(vel, count):
        sums = [[jnp.zeros((rows, LANES), jnp.float32) for _ in range(cells)] for _ in range(2)]
        for epoch in range(epochs):
            row = row_ref[epoch, vel]
            start_col = LANES + col_ref[epoch, vel]
            windows = windows_at(wide_ref, epoch, rows + row, start_col, rows)
            for kind in range(2):
                for cell in range(cells):
                    sums[kind][cell] = sums[kind][cell] + windows[kind][cell]
            reach = row * (2 * odd - 1)
            start_row = row + (1 - odd) * rows
            list_ref[count] = (vel << 24) | (epoch << 16) | (start_row << 10) | start_col
            count = count + jnp.where(reach > 0, 1, 0)
        for kind in range(2):
            for cell in range(cells):
                sums_ref[vel, kind, cell] = sums[kind][cell]
        return count

    count = lax.fori_loop(0, vels, one_velocity, jnp.int32(0), unroll=4)
    for index in range(group):
        list_ref[count + index] = (((1 - odd) * rows) << 10) | LANES
    count_ref[0] = count
    count_ref[1] = odd


def far_kernel(cells, group, list_ref, count_ref, far_ref, given_ref, sums_ref, best_ref, wide_ref):
    vels = sums_ref.shape[0]
    rows = far_ref.shape[1]
    epochs = wide_ref.shape[0]
    far_row = pl.multiple_of(count_ref[1] * rows, rows)
    zero_row = pl.multiple_of((1 - count_ref[1]) * rows, rows)
    for epoch in range(epochs):
        for kind in range(2):
            clear_sides(wide_ref, epoch, kind)
            for cell in range(cells):
                index = (epoch * 2 + kind) * cells + cell
                wide_ref[epoch, kind, cell + 1, pl.ds(far_row, rows), :] = far_ref[index]
                wide_ref[epoch, kind, cell + 1, pl.ds(zero_row, rows), :] = jnp.zeros(
                    (rows, LANES), jnp.float32
                )

    def one_group(turn, carry):
        found = []
        for index in range(group):
            code = list_ref[turn * group + index]
            start_col = code & 1023
            start_row = (code >> 10) & 63
            epoch = (code >> 16) & 255
            found.append((code >> 24, windows_at(wide_ref, epoch, start_row, start_col, rows)))
        for vel, windows in found:
            for kind in range(2):
                for cell in range(cells):
                    sums_ref[vel, kind, cell] = sums_ref[vel, kind, cell] + windows[kind][cell]
        return carry

    lax.fori_loop(0, lax.div(count_ref[0] + group - 1, group), one_group, 0)
    highest = [jnp.full((rows, LANES), -jnp.inf, jnp.float32) for _ in range(cells)]
    for vel in range(vels):
        for cell in range(cells):
            scale = lax.rsqrt(jnp.maximum(sums_ref[vel, 1, cell], 1.0))
            highest[cell] = jnp.maximum(highest[cell], sums_ref[vel, 0, cell] * scale)
    for cell in range(cells):
        best_ref[:, cell * LANES : (cell + 1) * LANES] = highest[cell]


def body(psi, phi, dest_tile, dest_cell, kernel_id, weight, kernels, row_offsets, col_offsets):
    tiles = lax.axis_size("tile")
    cells, epochs, rows, width = psi.shape
    capacity = max(2, 2 * cells * epochs // tiles)
    message = (tiles * (2 * capacity + 1), rows, width)
    given = (jnp.swapaxes(dest_tile, 1, 2), dest_cell, kernel_id, weight, psi, phi, kernels)
    outgoing = pl.pallas_call(
        functools.partial(pack_kernel, capacity),
        out_shape=jax.ShapeDtypeStruct(message, jnp.float32),
        in_specs=[pl.BlockSpec(memory_space=pl.ANY)] * 7,
        out_specs=VMEM,
        scratch_shapes=[
            pltpu.VMEM((kernels.shape[0], 3, width), jnp.float32),
            pltpu.VMEM((tiles, 1, LANES), jnp.float32),
            pltpu.SMEM((tiles,), jnp.int32),
            pltpu.SMEM((cells, epochs), jnp.int32),
        ]
        + [pltpu.SMEM(array.shape, array.dtype) for array in given[:4]]
        + [pltpu.VMEM(array.shape, array.dtype) for array in given[4:]]
        + [pltpu.SemaphoreType.DMA((7,))],
        compiler_params=pltpu.CompilerParams(vmem_limit_bytes=32 * 1024 * 1024),
        name="pack",
    )(*(pltpu.with_memory_space_constraint(array, pltpu.HBM) for array in given))
    outgoing = outgoing.reshape(tiles, 2 * capacity + 1, rows, width)
    incoming = lax.all_to_all(outgoing, "tile", split_axis=0, concat_axis=0, tiled=True)
    sky, *halves = pl.pallas_call(
        functools.partial(sum_kernel, capacity, cells),
        out_shape=[
            jax.ShapeDtypeStruct((epochs * 2 * cells // parts, rows, width), jnp.float32)
            for parts in (1, 2, 2)
        ],
        in_specs=[VMEM],
        out_specs=[VMEM] * 3,
        compiler_params=LIMIT,
        name="sum_slots",
    )(incoming)
    far = lax.ppermute(
        sky, "tile", [pair for i in range(1, tiles - 1, 2) for pair in ((i, i + 1), (i + 1, i))]
    )
    twins = [lax.ppermute(half, "tile", [(i, i ^ 1) for i in range(tiles)]) for half in halves]
    odd = (lax.axis_index("tile") & 1).reshape(1)
    vels = row_offsets.shape[1]
    sums_shape = jax.ShapeDtypeStruct((vels, 2, cells, rows, width), jnp.float32)
    sums, listed, count = pl.pallas_call(
        functools.partial(near_kernel, cells, GROUP),
        out_shape=[
            sums_shape,
            pltpu.SMEM((vels * epochs + GROUP,), jnp.int32),
            pltpu.SMEM((2,), jnp.int32),
        ],
        in_specs=[SMEM] * 3 + [VMEM] * 3,
        out_specs=[VMEM, SMEM, SMEM],
        scratch_shapes=[pltpu.VMEM((epochs, 2, cells + 2, 3 * rows, width), jnp.float32)],
        compiler_params=LIMIT,
        name="stack_near",
    )(row_offsets, col_offsets, odd, sky, *twins)
    _, best = pl.pallas_call(
        functools.partial(far_kernel, cells, GROUP),
        out_shape=[sums_shape, jax.ShapeDtypeStruct((rows, cells * width), jnp.float32)],
        in_specs=[SMEM] * 2 + [VMEM] * 2,
        out_specs=[VMEM, VMEM],
        input_output_aliases={3: 0},
        scratch_shapes=[pltpu.VMEM((epochs, 2, cells + 2, 2 * rows, width), jnp.float32)],
        compiler_params=LIMIT,
        name="stack_far",
    )(listed, count, far, sums)
    return best


def solution(mesh):
    placed = (
        P(("field", "tile"), None, None, None),
        P(("field", "tile"), None, None, None),
        P(("field", "tile"), None, None),
        P(("field", "tile"), None),
        P(("field", "tile"), None),
        P(("field", "tile"), None),
        P(),
        P("field", None),
        P("field", None),
    )
    return jax.shard_map(
        body, mesh=mesh, in_specs=placed, out_specs=P(("field", "tile"), None), check_vma=False
    )
```

time: 39.7 us -> 36.6 us (0.922)
  waiting for transfers between devices: 6.07 us -> 3.28 us
    ppermute x1, waiting for transfers between devices: 6.07 us -> 2.26 us  [body(): lax.ppermute(sky, 'tile', [pair for i in range(1, tiles - 1, 2) for pair...]
    pallas_call x1 -> x2, Pallas kernels: 2.78 us -> 3.84 us  [the longest x1 2.23 us: body(): pl.pallas_call(functools.partial(near_kernel, cells, GROUP), out_shape=[s...]
    ppermute x1 -> x2, waiting for transfers between devices: 0.01 us -> 1.02 us  [body(): lax.ppermute(half, 'tile', [(i, i ^ 1) for i in range(tiles)])]
    pallas_call x1, Pallas kernels: 2.39 us -> 1.43 us  [body(): pl.pallas_call(functools.partial(pack_kernel, capacity), out_shape=jax.Sh...]
  transfers between devices with their start and end apart: 2 -> 3, of which waited for: 1 -> 3; matrix products, arithmetic and copies ran while one was open for 0% -> 0% of each run, Pallas kernels for 0% -> 6%
where the time goes in v4:
time: 36.6 us; the launch traced here: 36.2 us
  blocking collectives  24.1 us (66%)
  Pallas kernels  5.7 us (16%)
  waiting for transfers between devices  3.28 us (9%)
  starting transfers between devices  3.09 us (8%)
    all_to_all x1, blocking collectives, body(): lax.all_to_all(outgoing, 'tile', split_axis=0, concat_axis=0, tiled=True)  24.1 us
    ppermute x1, starting transfers between devices, body(): lax.ppermute(sky, 'tile', [pair for i in range(1, tiles - 1, 2) for pair...  2.52 us
    ppermute x1, waiting for transfers between devices, body(): lax.ppermute(sky, 'tile', [pair for i in range(1, tiles - 1, 2) for pair...  2.26 us
    pallas_call x1, Pallas kernels, body(): pl.pallas_call(functools.partial(near_kernel, cells, GROUP), out_shape=[s...  2.23 us
    pallas_call x1, Pallas kernels, body(): pl.pallas_call(functools.partial(far_kernel, cells, GROUP), out_shape=[su...  1.61 us
    pallas_call x1, Pallas kernels, body(): pl.pallas_call(functools.partial(pack_kernel, capacity), out_shape=jax.Sh...  1.43 us
    ppermute x2, waiting for transfers between devices, body(): lax.ppermute(half, 'tile', [(i, i ^ 1) for i in range(tiles)])  1.02 us
  transfers between devices with their start and end apart: 3, of which 3 were waited for; matrix products, arithmetic and copies ran while one was open for 0% of the time, Pallas kernels for 6%

profile of v4, /device:TPU:1, one launch (start us, length us, event | category | flops | bytes accessed | tf_op | source)
XLA Modules:
  0.0 36.2 jit_solution(4140421960669477216)
XLA Ops:
  0.0 1.4 %pack.1 = f32[144,8,128]{2,1,0:T(8,128)S(1)} custom-call(s32[4,1,8]{2,1,0:T(1,128)} %bitcast.6, s32[4,8]{1,0:T(4,128)} %refs_1_.1, s32[4,8]{1,0:T(4,128)} %refs_2_.1, f32[4,8]{1,0:T(4,128)} %refs_3_.1, f32[4,8,8,128]{3,2,1,0:T(8,128)} %refs_4_.1, f32[4,8,8,128]{3,2,1,0:T(8,128)} %refs_5_.1, f32[8,128,128]{2,1,0:T(8,128)} %refs_6_.1), custom_call_target="tpu_custom_call" | custom-call | tf_op jit(solution)/shard_map/pack/pallas_call | solution.py:218
  1.4 24.1 %all_to_all.5.in_ref = f32[16,9,8,128]{3,2,1,0:T(8,128)S(1)} all-to-all(f32[16,9,8,128]{3,2,1,0:T(8,128)S(1)} %bitcast.5), channel_id=1, replica_groups=mesh['field'=2,'tile'=16] {'tile'}, dimensions={0} | all-to-all | bytes 1179648 | tf_op jit(solution)/shard_map/all_to_all | solution.py:236
  25.6 0.4 %sum_slots.1 = (f32[64,8,128]{2,1,0:T(8,128)S(1)}, f32[32,8,128]{2,1,0:T(8,128)S(1)}, f32[32,8,128]{2,1,0:T(8,128)S(1)}) custom-call(f32[16,9,8,128]{3,2,1,0:T(8,128)S(1)} %all_to_all.5.in_ref), custom_call_target="tpu_custom_call" | custom-call | tf_op jit(solution)/shard_map/sum_slots/pallas_call | solution.py:237
  26.0 2.5 %collective-permute-start.2 = (f32[64,8,128]{2,1,0:T(8,128)S(1)}, f32[64,8,128]{2,1,0:T(8,128)S(1)}, u32[]{:S(2)}, u32[]{:S(2)}) collective-permute-start(f32[64,8,128]{2,1,0:T(8,128)S(1)} %get-tuple-element.12.own_ref), channel_id=1, source_target_pairs={{1,2},{2,1},{3,4},{4,3},{5,6},{6,5},{7,8},{8,7},{9,10},{10,9},{11,... | collective-permute-start | bytes 786440 | tf_op jit(solution)/shard_map/ppermute | solution.py:248
  28.5 0.1 collective-permute-start
  28.6 0.5 %collective-permute-start.1 = (f32[32,8,128]{2,1,0:T(8,128)S(1)}, f32[32,8,128]{2,1,0:T(8,128)S(1)}, u32[]{:S(2)}, u32[]{:S(2)}) collective-permute-start(f32[32,8,128]{2,1,0:T(8,128)S(1)} %get-tuple-element.14), channel_id=1, source_target_pairs={{0,1},{1,0},{2,3},{3,2},{4,5},{5,4},{6,7},{7,6},{8,9},{9,8},{10,11... | collective-permute-start | bytes 393224 | tf_op jit(solution)/shard_map/ppermute | solution.py:251
  29.1 0.0 copy-start.1
  29.1 0.0 copy-start
  29.1 0.8 %collective-permute-done.low_ref = f32[32,8,128]{2,1,0:T(8,128)S(1)} collective-permute-done((f32[32,8,128]{2,1,0:T(8,128)S(1)}, f32[32,8,128]{2,1,0:T(8,128)S(1)}, u32[]{:S(2)}, u32[]{:S(2)}) %collective-permute-start) | collective-permute-done | bytes 131104 | tf_op jit(solution)/shard_map/ppermute | solution.py:251
  29.9 0.2 collective-permute-done.1.high_ref
  30.1 0.0 copy-done.1
  30.1 0.0 copy-done
  30.1 2.2 %stack_near.1 = (f32[16,2,4,8,128]{4,3,2,1,0:T(8,128)S(1)}, s32[152]{0:T(256)S(4)}, s32[2]{0:T(128)S(4)}) custom-call(s32[8,16]{1,0:T(8,128)S(1)} %copy-done, s32[8,16]{1,0:T(8,128)S(1)} %copy-done.1, s32[1]{0:T(128)} %bitcast.odd_ref, f32[64,8,128]{2,1,0:T(8,128)S(1)} %get-tuple-element.12.own_ref, f32[32,8,128]{2,1,0:T(8,128)S(1)} %collective-permute-done.low_ref, ...), custom_call_target="tpu_custom_call" | custom-call | tf_op jit(solution)/shard_map/stack_near/pallas_call | solution.py:255
  32.4 2.3 %collective-permute-done.2.far_ref = f32[64,8,128]{2,1,0:T(8,128)S(1)} collective-permute-done((f32[64,8,128]{2,1,0:T(8,128)S(1)}, f32[64,8,128]{2,1,0:T(8,128)S(1)}, u32[]{:S(2)}, u32[]{:S(2)}) %collective-permute-start.2) | collective-permute-done | bytes 262176 | tf_op jit(solution)/shard_map/ppermute | solution.py:248
  34.6 1.6 %stack_far.1 = (f32[16,2,4,8,128]{4,3,2,1,0:T(8,128)S(1)}, f32[8,512]{1,0:T(8,128)}) custom-call(s32[152]{0:T(256)S(4)} %get-tuple-element.15.list_ref, s32[2]{0:T(128)S(4)} %get-tuple-element.16.count_ref, f32[64,8,128]{2,1,0:T(8,128)S(1)} %collective-permute-done.2.far_ref, ...), custom_call_target="tpu_custom_call", output_to_operand_aliasing={{0}: (3, {})} | custom-call | tf_op jit(solution)/shard_map/stack_far/pallas_call | solution.py:268
Async XLA Ops:
  26.0 8.6 %collective-permute-start.2 = (f32[64,8,128]{2,1,0:T(8,128)S(1)}, f32[64,8,128]{2,1,0:T(8,128)S(1)}, u32[]{:S(2)}, u32[]{:S(2)}) collective-permute-start(f32[64,8,128]{2,1,0:T(8,128)S(1)} %get-tuple-element.12.own_ref), channel_id=1, source_target_pairs={{1,2},{2,1},{3,4},{4,3},{5,6},{6,5},{7,8},{8,7},{9,10},{10,9},{11,... | collective-permute-start | bytes 786440 | tf_op jit(solution)/shard_map/ppermute | solution.py:248
  28.5 1.4 %collective-permute-start = (f32[32,8,128]{2,1,0:T(8,128)S(1)}, f32[32,8,128]{2,1,0:T(8,128)S(1)}, u32[]{:S(2)}, u32[]{:S(2)}) collective-permute-start(f32[32,8,128]{2,1,0:T(8,128)S(1)} %get-tuple-element.13), channel_id=1, source_target_pairs={{0,1},{1,0},{2,3},{3,2},{4,5},{5,4},{6,7},{7,6},{8,9},{9,8},{10,11... | collective-permute-start | bytes 393224 | tf_op jit(solution)/shard_map/ppermute | solution.py:251
  28.6 1.5 %collective-permute-start.1 = (f32[32,8,128]{2,1,0:T(8,128)S(1)}, f32[32,8,128]{2,1,0:T(8,128)S(1)}, u32[]{:S(2)}, u32[]{:S(2)}) collective-permute-start(f32[32,8,128]{2,1,0:T(8,128)S(1)} %get-tuple-element.14), channel_id=1, source_target_pairs={{0,1},{1,0},{2,3},{3,2},{4,5},{5,4},{6,7},{7,6},{8,9},{9,8},{10,11... | collective-permute-start | bytes 393224 | tf_op jit(solution)/shard_map/ppermute | solution.py:251
  29.1 1.0 %copy-start.1 = (s32[8,16]{1,0:T(8,128)S(1)}, s32[8,16]{1,0:T(8,128)}, u32[]{:S(2)}) copy-start(s32[8,16]{1,0:T(8,128)} %col_ref.1) | copy-start | bytes 1540
  29.1 1.0 %copy-start = (s32[8,16]{1,0:T(8,128)S(1)}, s32[8,16]{1,0:T(8,128)}, u32[]{:S(2)}) copy-start(s32[8,16]{1,0:T(8,128)} %row_ref.1) | copy-start | bytes 1540

commit v5 on v4

--- a/solution.py
+++ b/solution.py
@@ -29,7 +29,8 @@
     tile_ref, cell_ref, id_ref, weight_ref, psi_ref, phi_ref, table_ref = held
     cells, epochs = psi_ref.shape[:2]
     tiles, width = used_ref.shape[0], psi_ref.shape[3]
-    stride = 2 * capacity + 1
+    rows = psi_ref.shape[2]
+    stride = 2 * capacity * rows + 1
 
     def clear(tile, carry):
         used_ref[tile] = 0
@@ -46,7 +47,7 @@
             tile = tile_ref[block, 0, epoch]
             slot = used_ref[tile]
             used_ref[tile] = slot + 1
-            spot_ref[block, epoch] = tile * stride + 2 * slot
+            spot_ref[block, epoch] = tile * stride + 2 * rows * slot
             place = (epoch * 2 * cells + cell_ref[block, epoch] + 1).astype(jnp.float32)
             note_ref[tile] = jnp.where(lane == slot, place, note_ref[tile])
     for copy in copies[4:]:
@@ -61,7 +62,7 @@
             diag_ref[index, place : place + 1, :] = row
 
     def write_note(tile, carry):
-        out_ref[tile * stride + 2 * capacity, 0:1, :] = note_ref[tile]
+        out_ref[pl.ds(tile * stride + stride - 1, 1), :] = note_ref[tile]
         return carry
 
     lax.fori_loop(0, tiles, write_note, 0, unroll=16)
@@ -71,7 +72,7 @@
             bands = diag_ref[id_ref[block, epoch]] * weight_ref[block, epoch]
             for kind, ref in enumerate((psi_ref, phi_ref)):
                 values = ref[block, epoch]
-                out_ref[spot + kind] = (
+                out_ref[pl.ds(spot + kind * rows, rows), :] = (
                     values * bands[1:2]
                     + pltpu.roll(values, 1, 1) * bands[0:1]
                     + pltpu.roll(values, width - 1, 1) * bands[2:3]
@@ -79,21 +80,25 @@
 
 
 def sum_kernel(capacity, cells, in_ref, sky_ref, *half_refs):
+    rows = sky_ref.shape[1]
+    stride = 2 * capacity * rows + 1
     for index in range(sky_ref.shape[0]):
         sky_ref[index] = jnp.zeros(sky_ref.shape[1:], jnp.float32)
 
     def one_source(source, carry):
-        notes = in_ref[source, 2 * capacity].astype(jnp.int32)
+        first = source * stride
+        notes = in_ref[pl.ds(first + stride - 1, 1), :].astype(jnp.int32)
         for slot in range(capacity):
             place = notes[0, slot] - 1
             there = place >= 0
             base = jnp.maximum(place, 0)
             for kind in range(2):
-                value = jnp.where(there, in_ref[source, 2 * slot + kind], 0.0)
+                value = in_ref[pl.ds(first + (2 * slot + kind) * rows, rows), :]
+                value = jnp.where(there, value, 0.0)
                 sky_ref[base + kind * cells] = sky_ref[base + kind * cells] + value
         return carry
 
-    lax.fori_loop(0, in_ref.shape[0], one_source, 0, unroll=16)
+    lax.fori_loop(0, in_ref.shape[0] // stride, one_source, 0, unroll=16)
     for half, ref in enumerate(half_refs):
         for index in range(ref.shape[0]):
             ref[index] = sky_ref[half * ref.shape[0] + index]
@@ -213,7 +218,8 @@
     tiles = lax.axis_size("tile")
     cells, epochs, rows, width = psi.shape
     capacity = max(2, 2 * cells * epochs // tiles)
-    message = (tiles * (2 * capacity + 1), rows, width)
+    stride = 2 * capacity * rows + 1
+    message = (tiles * stride, width)
     given = (jnp.swapaxes(dest_tile, 1, 2), dest_cell, kernel_id, weight, psi, phi, kernels)
     outgoing = pl.pallas_call(
         functools.partial(pack_kernel, capacity),
@@ -232,8 +238,9 @@
         compiler_params=pltpu.CompilerParams(vmem_limit_bytes=32 * 1024 * 1024),
         name="pack",
     )(*(pltpu.with_memory_space_constraint(array, pltpu.HBM) for array in given))
-    outgoing = outgoing.reshape(tiles, 2 * capacity + 1, rows, width)
+    outgoing = outgoing.reshape(tiles, stride, 1, width)
     incoming = lax.all_to_all(outgoing, "tile", split_axis=0, concat_axis=0, tiled=True)
+    incoming = incoming.reshape(message)
     sky, *halves = pl.pallas_call(
         functools.partial(sum_kernel, capacity, cells),
         out_shape=[

time: 36.6 us -> 35.4 us (0.967)
  blocking collectives: 24.1 us -> 22.9 us
    all_to_all x1, blocking collectives: 24.1 us -> 22.9 us  [body(): lax.all_to_all(outgoing, 'tile', split_axis=0, concat_axis=0, tiled=True)]
where the time goes in v5:
time: 35.4 us; the launch traced here: 35.2 us
  blocking collectives  22.9 us (65%)
  Pallas kernels  5.71 us (16%)
  starting transfers between devices  3.31 us (9%)
  waiting for transfers between devices  3.28 us (9%)
    all_to_all x1, blocking collectives, body(): lax.all_to_all(outgoing, 'tile', split_axis=0, concat_axis=0, tiled=True)  22.9 us
    ppermute x1, starting transfers between devices, body(): lax.ppermute(sky, 'tile', [pair for i in range(1, tiles - 1, 2) for pair...  2.75 us
    ppermute x1, waiting for transfers between devices, body(): lax.ppermute(sky, 'tile', [pair for i in range(1, tiles - 1, 2) for pair...  2.26 us
    pallas_call x1, Pallas kernels, body(): pl.pallas_call(functools.partial(near_kernel, cells, GROUP), out_shape=[s...  2.23 us
    pallas_call x1, Pallas kernels, body(): pl.pallas_call(functools.partial(far_kernel, cells, GROUP), out_shape=[su...  1.61 us
    pallas_call x1, Pallas kernels, body(): pl.pallas_call(functools.partial(pack_kernel, capacity), out_shape=jax.Sh...  1.43 us
    ppermute x2, waiting for transfers between devices, body(): lax.ppermute(half, 'tile', [(i, i ^ 1) for i in range(tiles)])  1.02 us
  transfers between devices with their start and end apart: 3, of which 3 were waited for; matrix products, arithmetic and copies ran while one was open for 0% of the time, Pallas kernels for 6%

profile of v5, /device:TPU:1, one launch (start us, length us, event | category | flops | bytes accessed | tf_op | source)
XLA Modules:
  0.0 35.2 jit_solution(5951200949056551026)
XLA Ops:
  0.0 1.4 %pack.1 = f32[1040,128]{1,0:T(8,128)S(1)} custom-call(s32[4,1,8]{2,1,0:T(1,128)} %bitcast.8, s32[4,8]{1,0:T(4,128)} %refs_1_.1, s32[4,8]{1,0:T(4,128)} %refs_2_.1, f32[4,8]{1,0:T(4,128)} %refs_3_.1, f32[4,8,8,128]{3,2,1,0:T(8,128)} %refs_4_.1, f32[4,8,8,128]{3,2,1,0:T(8,128)} %refs_5_.1, f32[8,128,128]{2,1,0:T(8,128)} %refs_6_.1), custom_call_target="tpu_custom_call" | custom-call | tf_op jit(solution)/shard_map/pack/pallas_call | solution.py:224
  1.4 22.9 %all_to_all.5 = f32[16,65,1,128]{3,2,1,0:T(1,128)S(1)} all-to-all(f32[16,65,1,128]{3,2,1,0:T(1,128)S(1)} %bitcast.7), channel_id=1, replica_groups=mesh['field'=2,'tile'=16] {'tile'}, dimensions={0} | all-to-all | bytes 1064960 | tf_op jit(solution)/shard_map/all_to_all | solution.py:242
  24.3 0.4 %sum_slots.1 = (f32[64,8,128]{2,1,0:T(8,128)S(1)}, f32[32,8,128]{2,1,0:T(8,128)S(1)}, f32[32,8,128]{2,1,0:T(8,128)S(1)}) custom-call(f32[1040,128]{1,0:T(8,128)S(1)} %bitcast.6), custom_call_target="tpu_custom_call" | custom-call | tf_op jit(solution)/shard_map/sum_slots/pallas_call | solution.py:244
  24.7 2.7 %collective-permute-start.2 = (f32[64,8,128]{2,1,0:T(8,128)S(1)}, f32[64,8,128]{2,1,0:T(8,128)S(1)}, u32[]{:S(2)}, u32[]{:S(2)}) collective-permute-start(f32[64,8,128]{2,1,0:T(8,128)S(1)} %get-tuple-element.12.own_ref), channel_id=1, source_target_pairs={{1,2},{2,1},{3,4},{4,3},{5,6},{6,5},{7,8},{8,7},{9,10},{10,9},{11,... | collective-permute-start | bytes 786440 | tf_op jit(solution)/shard_map/ppermute | solution.py:255
  27.5 0.1 collective-permute-start
  27.6 0.5 %collective-permute-start.1 = (f32[32,8,128]{2,1,0:T(8,128)S(1)}, f32[32,8,128]{2,1,0:T(8,128)S(1)}, u32[]{:S(2)}, u32[]{:S(2)}) collective-permute-start(f32[32,8,128]{2,1,0:T(8,128)S(1)} %get-tuple-element.14), channel_id=1, source_target_pairs={{0,1},{1,0},{2,3},{3,2},{4,5},{5,4},{6,7},{7,6},{8,9},{9,8},{10,11... | collective-permute-start | bytes 393224 | tf_op jit(solution)/shard_map/ppermute | solution.py:258
  28.1 0.0 copy-start.1
  28.1 0.0 copy-start
  28.1 0.8 %collective-permute-done.low_ref = f32[32,8,128]{2,1,0:T(8,128)S(1)} collective-permute-done((f32[32,8,128]{2,1,0:T(8,128)S(1)}, f32[32,8,128]{2,1,0:T(8,128)S(1)}, u32[]{:S(2)}, u32[]{:S(2)}) %collective-permute-start) | collective-permute-done | bytes 131104 | tf_op jit(solution)/shard_map/ppermute | solution.py:258
  28.9 0.2 collective-permute-done.1.high_ref
  29.1 0.0 copy-done.1
  29.1 0.0 copy-done
  29.1 2.2 %stack_near.1 = (f32[16,2,4,8,128]{4,3,2,1,0:T(8,128)S(1)}, s32[152]{0:T(256)S(4)}, s32[2]{0:T(128)S(4)}) custom-call(s32[8,16]{1,0:T(8,128)S(1)} %copy-done, s32[8,16]{1,0:T(8,128)S(1)} %copy-done.1, s32[1]{0:T(128)} %bitcast.odd_ref, f32[64,8,128]{2,1,0:T(8,128)S(1)} %get-tuple-element.12.own_ref, f32[32,8,128]{2,1,0:T(8,128)S(1)} %collective-permute-done.low_ref, ...), custom_call_target="tpu_custom_call" | custom-call | tf_op jit(solution)/shard_map/stack_near/pallas_call | solution.py:262
  31.3 2.3 %collective-permute-done.2.far_ref = f32[64,8,128]{2,1,0:T(8,128)S(1)} collective-permute-done((f32[64,8,128]{2,1,0:T(8,128)S(1)}, f32[64,8,128]{2,1,0:T(8,128)S(1)}, u32[]{:S(2)}, u32[]{:S(2)}) %collective-permute-start.2) | collective-permute-done | bytes 262176 | tf_op jit(solution)/shard_map/ppermute | solution.py:255
  33.6 1.6 %stack_far.1 = (f32[16,2,4,8,128]{4,3,2,1,0:T(8,128)S(1)}, f32[8,512]{1,0:T(8,128)}) custom-call(s32[152]{0:T(256)S(4)} %get-tuple-element.15.list_ref, s32[2]{0:T(128)S(4)} %get-tuple-element.16.count_ref, f32[64,8,128]{2,1,0:T(8,128)S(1)} %collective-permute-done.2.far_ref, ...), custom_call_target="tpu_custom_call", output_to_operand_aliasing={{0}: (3, {})} | custom-call | tf_op jit(solution)/shard_map/stack_far/pallas_call | solution.py:275
Async XLA Ops:
  24.7 8.9 %collective-permute-start.2 = (f32[64,8,128]{2,1,0:T(8,128)S(1)}, f32[64,8,128]{2,1,0:T(8,128)S(1)}, u32[]{:S(2)}, u32[]{:S(2)}) collective-permute-start(f32[64,8,128]{2,1,0:T(8,128)S(1)} %get-tuple-element.12.own_ref), channel_id=1, source_target_pairs={{1,2},{2,1},{3,4},{4,3},{5,6},{6,5},{7,8},{8,7},{9,10},{10,9},{11,... | collective-permute-start | bytes 786440 | tf_op jit(solution)/shard_map/ppermute | solution.py:255
  27.5 1.4 %collective-permute-start = (f32[32,8,128]{2,1,0:T(8,128)S(1)}, f32[32,8,128]{2,1,0:T(8,128)S(1)}, u32[]{:S(2)}, u32[]{:S(2)}) collective-permute-start(f32[32,8,128]{2,1,0:T(8,128)S(1)} %get-tuple-element.13), channel_id=1, source_target_pairs={{0,1},{1,0},{2,3},{3,2},{4,5},{5,4},{6,7},{7,6},{8,9},{9,8},{10,11... | collective-permute-start | bytes 393224 | tf_op jit(solution)/shard_map/ppermute | solution.py:258
  27.6 1.5 %collective-permute-start.1 = (f32[32,8,128]{2,1,0:T(8,128)S(1)}, f32[32,8,128]{2,1,0:T(8,128)S(1)}, u32[]{:S(2)}, u32[]{:S(2)}) collective-permute-start(f32[32,8,128]{2,1,0:T(8,128)S(1)} %get-tuple-element.14), channel_id=1, source_target_pairs={{0,1},{1,0},{2,3},{3,2},{4,5},{5,4},{6,7},{7,6},{8,9},{9,8},{10,11... | collective-permute-start | bytes 393224 | tf_op jit(solution)/shard_map/ppermute | solution.py:258
  28.1 1.0 %copy-start.1 = (s32[8,16]{1,0:T(8,128)S(1)}, s32[8,16]{1,0:T(8,128)}, u32[]{:S(2)}) copy-start(s32[8,16]{1,0:T(8,128)} %col_ref.1) | copy-start | bytes 1540
  28.1 1.0 %copy-start = (s32[8,16]{1,0:T(8,128)S(1)}, s32[8,16]{1,0:T(8,128)}, u32[]{:S(2)}) copy-start(s32[8,16]{1,0:T(8,128)} %row_ref.1) | copy-start | bytes 1540

commit v6 on v5

--- a/solution.py
+++ b/solution.py
@@ -130,11 +130,12 @@
 
 
 def near_kernel(
-    cells, group, row_ref, col_ref, odd_ref, own_ref, low_ref, high_ref, sums_ref, list_ref, count_ref, wide_ref
+    cells, tiles, group, row_ref, col_ref, me_ref, own_ref, low_ref, high_ref, sums_ref, list_ref, count_ref, wide_ref
 ):
     epochs, vels = row_ref.shape
     rows = own_ref.shape[1]
-    odd = odd_ref[0]
+    odd = me_ref[0] & 1
+    towards = jnp.where((me_ref[0] == 0) | (me_ref[0] == tiles - 1), 0, 2 * odd - 1)
     twin_row = pl.multiple_of((1 - odd) * 2 * rows, rows)
     far_row = pl.multiple_of(odd * 2 * rows, rows)
     for epoch in range(epochs):
@@ -158,7 +159,7 @@
             for kind in range(2):
                 for cell in range(cells):
                     sums[kind][cell] = sums[kind][cell] + windows[kind][cell]
-            reach = row * (2 * odd - 1)
+            reach = row * towards
             start_row = row + (1 - odd) * rows
             list_ref[count] = (vel << 24) | (epoch << 16) | (start_row << 10) | start_col
             count = count + jnp.where(reach > 0, 1, 0)
@@ -252,15 +253,20 @@
         compiler_params=LIMIT,
         name="sum_slots",
     )(incoming)
+    fields = lax.axis_size("field")
+    pairs = [(f * tiles + i, f * tiles + i + 1) for f in range(fields) for i in range(1, tiles - 1, 2)]
+    pairs += [
+        (f * tiles + i, (f + 1) * tiles + i) for f in range(0, fields - 1, 2) for i in (0, tiles - 1)
+    ]
     far = lax.ppermute(
-        sky, "tile", [pair for i in range(1, tiles - 1, 2) for pair in ((i, i + 1), (i + 1, i))]
+        sky, ("field", "tile"), [way for a, b in pairs for way in ((a, b), (b, a))]
     )
     twins = [lax.ppermute(half, "tile", [(i, i ^ 1) for i in range(tiles)]) for half in halves]
-    odd = (lax.axis_index("tile") & 1).reshape(1)
+    me = lax.axis_index("tile").reshape(1)
     vels = row_offsets.shape[1]
     sums_shape = jax.ShapeDtypeStruct((vels, 2, cells, rows, width), jnp.float32)
     sums, listed, count = pl.pallas_call(
-        functools.partial(near_kernel, cells, GROUP),
+        functools.partial(near_kernel, cells, tiles, GROUP),
         out_shape=[
             sums_shape,
             pltpu.SMEM((vels * epochs + GROUP,), jnp.int32),
@@ -271,7 +277,7 @@
         scratch_shapes=[pltpu.VMEM((epochs, 2, cells + 2, 3 * rows, width), jnp.float32)],
         compiler_params=LIMIT,
         name="stack_near",
-    )(row_offsets, col_offsets, odd, sky, *twins)
+    )(row_offsets, col_offsets, me, sky, *twins)
     _, best = pl.pallas_call(
         functools.partial(far_kernel, cells, GROUP),
         out_shape=[sums_shape, jax.ShapeDtypeStruct((rows, cells * width), jnp.float32)],

time: 35.4 us -> 33.6 us (0.949)
  starting transfers between devices: 3.31 us -> 2.23 us
  waiting for transfers between devices: 3.28 us -> 2.63 us
    ppermute x1, starting transfers between devices: 2.75 us -> 0.94 us  [body(): lax.ppermute(sky, ('field', 'tile'), [way for a, b in pairs for way in ((...]
    ppermute x1, waiting for transfers between devices: 2.26 us -> 1.28 us  [body(): lax.ppermute(sky, ('field', 'tile'), [way for a, b in pairs for way in ((...]
    ppermute x2, starting transfers between devices: 0.57 us -> 1.29 us  [body(): lax.ppermute(half, 'tile', [(i, i ^ 1) for i in range(tiles)])]
  transfers between devices with their start and end apart: 3 -> 3, of which waited for: 3 -> 3; matrix products, arithmetic and copies ran while one was open for 0% -> 0% of each run, Pallas kernels for 6% -> 7%
where the time goes in v6:
time: 33.6 us; the launch traced here: 33.4 us
  blocking collectives  22.9 us (68%)
  Pallas kernels  5.66 us (17%)
  waiting for transfers between devices  2.63 us (8%)
  starting transfers between devices  2.23 us (7%)
    all_to_all x1, blocking collectives, body(): lax.all_to_all(outgoing, 'tile', split_axis=0, concat_axis=0, tiled=True)  22.9 us
    pallas_call x1, Pallas kernels, body(): pl.pallas_call(functools.partial(near_kernel, cells, tiles, GROUP), out_s...  2.19 us
    pallas_call x1, Pallas kernels, body(): pl.pallas_call(functools.partial(far_kernel, cells, GROUP), out_shape=[su...  1.61 us
    pallas_call x1, Pallas kernels, body(): pl.pallas_call(functools.partial(pack_kernel, capacity), out_shape=jax.Sh...  1.43 us
    ppermute x2, waiting for transfers between devices, body(): lax.ppermute(half, 'tile', [(i, i ^ 1) for i in range(tiles)])  1.34 us
    ppermute x2, starting transfers between devices, body(): lax.ppermute(half, 'tile', [(i, i ^ 1) for i in range(tiles)])  1.29 us
    ppermute x1, waiting for transfers between devices, body(): lax.ppermute(sky, ('field', 'tile'), [way for a, b in pairs for way in ((...  1.28 us
    ppermute x1, starting transfers between devices, body(): lax.ppermute(sky, ('field', 'tile'), [way for a, b in pairs for way in ((...  0.94 us
  transfers between devices with their start and end apart: 3, of which 3 were waited for; matrix products, arithmetic and copies ran while one was open for 0% of the time, Pallas kernels for 7%

profile of v6, /device:TPU:1, one launch (start us, length us, event | category | flops | bytes accessed | tf_op | source)
XLA Modules:
  0.0 33.4 jit_solution(2504938732856830944)
XLA Ops:
  0.0 1.4 %pack.1 = f32[1040,128]{1,0:T(8,128)S(1)} custom-call(s32[4,1,8]{2,1,0:T(1,128)} %bitcast.8, s32[4,8]{1,0:T(4,128)} %refs_1_.1, s32[4,8]{1,0:T(4,128)} %refs_2_.1, f32[4,8]{1,0:T(4,128)} %refs_3_.1, f32[4,8,8,128]{3,2,1,0:T(8,128)} %refs_4_.1, f32[4,8,8,128]{3,2,1,0:T(8,128)} %refs_5_.1, f32[8,128,128]{2,1,0:T(8,128)} %refs_6_.1), custom_call_target="tpu_custom_call" | custom-call | tf_op jit(solution)/shard_map/pack/pallas_call | solution.py:225
  1.4 22.9 %all_to_all.5 = f32[16,65,1,128]{3,2,1,0:T(1,128)S(1)} all-to-all(f32[16,65,1,128]{3,2,1,0:T(1,128)S(1)} %bitcast.7), channel_id=1, replica_groups=mesh['field'=2,'tile'=16] {'tile'}, dimensions={0} | all-to-all | bytes 1064960 | tf_op jit(solution)/shard_map/all_to_all | solution.py:243
  24.3 0.4 %sum_slots.1 = (f32[64,8,128]{2,1,0:T(8,128)S(1)}, f32[32,8,128]{2,1,0:T(8,128)S(1)}, f32[32,8,128]{2,1,0:T(8,128)S(1)}) custom-call(f32[1040,128]{1,0:T(8,128)S(1)} %bitcast.6), custom_call_target="tpu_custom_call" | custom-call | tf_op jit(solution)/shard_map/sum_slots/pallas_call | solution.py:245
  24.7 0.9 %collective-permute-start.2 = (f32[64,8,128]{2,1,0:T(8,128)S(1)}, f32[64,8,128]{2,1,0:T(8,128)S(1)}, u32[]{:S(2)}, u32[]{:S(2)}) collective-permute-start(f32[64,8,128]{2,1,0:T(8,128)S(1)} %get-tuple-element.12.own_ref), channel_id=1, source_target_pairs={{1,2},{2,1},{3,4},{4,3},{5,6},{6,5},{7,8},{8,7},{9,10},{10,9},{11,... | collective-permute-start | bytes 786440 | tf_op jit(solution)/shard_map/ppermute | solution.py:261
  25.7 1.3 %collective-permute-start = (f32[32,8,128]{2,1,0:T(8,128)S(1)}, f32[32,8,128]{2,1,0:T(8,128)S(1)}, u32[]{:S(2)}, u32[]{:S(2)}) collective-permute-start(f32[32,8,128]{2,1,0:T(8,128)S(1)} %get-tuple-element.13), channel_id=1, source_target_pairs={{0,1},{1,0},{2,3},{3,2},{4,5},{5,4},{6,7},{7,6},{8,9},{9,8},{10,11... | collective-permute-start | bytes 393224 | tf_op jit(solution)/shard_map/ppermute | solution.py:264
  27.0 0.0 copy-start.1
  27.0 0.0 copy-start
  27.0 0.0 collective-permute-start.1
  27.0 1.0 %collective-permute-done.low_ref = f32[32,8,128]{2,1,0:T(8,128)S(1)} collective-permute-done((f32[32,8,128]{2,1,0:T(8,128)S(1)}, f32[32,8,128]{2,1,0:T(8,128)S(1)}, u32[]{:S(2)}, u32[]{:S(2)}) %collective-permute-start) | collective-permute-done | bytes 131104 | tf_op jit(solution)/shard_map/ppermute | solution.py:264
  28.0 0.4 %collective-permute-done.1.high_ref = f32[32,8,128]{2,1,0:T(8,128)S(1)} collective-permute-done((f32[32,8,128]{2,1,0:T(8,128)S(1)}, f32[32,8,128]{2,1,0:T(8,128)S(1)}, u32[]{:S(2)}, u32[]{:S(2)}) %collective-permute-start.1) | collective-permute-done | bytes 131104 | tf_op jit(solution)/shard_map/ppermute | solution.py:264
  28.3 0.0 copy-done.1
  28.3 0.0 copy-done
  28.3 2.2 %stack_near.1 = (f32[16,2,4,8,128]{4,3,2,1,0:T(8,128)S(1)}, s32[152]{0:T(256)S(4)}, s32[2]{0:T(128)S(4)}) custom-call(s32[8,16]{1,0:T(8,128)S(1)} %copy-done, s32[8,16]{1,0:T(8,128)S(1)} %copy-done.1, s32[1]{0:T(128)} %bitcast.me_ref, f32[64,8,128]{2,1,0:T(8,128)S(1)} %get-tuple-element.12.own_ref, f32[32,8,128]{2,1,0:T(8,128)S(1)} %collective-permute-done.low_ref, ...), custom_call_target="tpu_custom_call" | custom-call | tf_op jit(solution)/shard_map/stack_near/pallas_call | solution.py:268
  30.5 1.3 %collective-permute-done.2.far_ref = f32[64,8,128]{2,1,0:T(8,128)S(1)} collective-permute-done((f32[64,8,128]{2,1,0:T(8,128)S(1)}, f32[64,8,128]{2,1,0:T(8,128)S(1)}, u32[]{:S(2)}, u32[]{:S(2)}) %collective-permute-start.2) | collective-permute-done | bytes 262176 | tf_op jit(solution)/shard_map/ppermute | solution.py:261
  31.8 1.6 %stack_far.1 = (f32[16,2,4,8,128]{4,3,2,1,0:T(8,128)S(1)}, f32[8,512]{1,0:T(8,128)}) custom-call(s32[152]{0:T(256)S(4)} %get-tuple-element.15.list_ref, s32[2]{0:T(128)S(4)} %get-tuple-element.16.count_ref, f32[64,8,128]{2,1,0:T(8,128)S(1)} %collective-permute-done.2.far_ref, ...), custom_call_target="tpu_custom_call", output_to_operand_aliasing={{0}: (3, {})} | custom-call | tf_op jit(solution)/shard_map/stack_far/pallas_call | solution.py:281
Async XLA Ops:
  24.7 7.1 %collective-permute-start.2 = (f32[64,8,128]{2,1,0:T(8,128)S(1)}, f32[64,8,128]{2,1,0:T(8,128)S(1)}, u32[]{:S(2)}, u32[]{:S(2)}) collective-permute-start(f32[64,8,128]{2,1,0:T(8,128)S(1)} %get-tuple-element.12.own_ref), channel_id=1, source_target_pairs={{1,2},{2,1},{3,4},{4,3},{5,6},{6,5},{7,8},{8,7},{9,10},{10,9},{11,... | collective-permute-start | bytes 786440 | tf_op jit(solution)/shard_map/ppermute | solution.py:261
  25.7 2.3 %collective-permute-start = (f32[32,8,128]{2,1,0:T(8,128)S(1)}, f32[32,8,128]{2,1,0:T(8,128)S(1)}, u32[]{:S(2)}, u32[]{:S(2)}) collective-permute-start(f32[32,8,128]{2,1,0:T(8,128)S(1)} %get-tuple-element.13), channel_id=1, source_target_pairs={{0,1},{1,0},{2,3},{3,2},{4,5},{5,4},{6,7},{7,6},{8,9},{9,8},{10,11... | collective-permute-start | bytes 393224 | tf_op jit(solution)/shard_map/ppermute | solution.py:264
  27.0 1.4 %copy-start.1 = (s32[8,16]{1,0:T(8,128)S(1)}, s32[8,16]{1,0:T(8,128)}, u32[]{:S(2)}) copy-start(s32[8,16]{1,0:T(8,128)} %col_ref.1) | copy-start | bytes 1540
  27.0 1.4 %copy-start = (s32[8,16]{1,0:T(8,128)S(1)}, s32[8,16]{1,0:T(8,128)}, u32[]{:S(2)}) copy-start(s32[8,16]{1,0:T(8,128)} %row_ref.1) | copy-start | bytes 1540
  27.0 1.3 %collective-permute-start.1 = (f32[32,8,128]{2,1,0:T(8,128)S(1)}, f32[32,8,128]{2,1,0:T(8,128)S(1)}, u32[]{:S(2)}, u32[]{:S(2)}) collective-permute-start(f32[32,8,128]{2,1,0:T(8,128)S(1)} %get-tuple-element.14), channel_id=1, source_target_pairs={{0,1},{1,0},{2,3},{3,2},{4,5},{5,4},{6,7},{7,6},{8,9},{9,8},{10,11... | collective-permute-start | bytes 393224 | tf_op jit(solution)/shard_map/ppermute | solution.py:264

commit v7 on v6

--- a/solution.py
+++ b/solution.py
@@ -10,7 +10,9 @@
 XREACH = 64
 RREACH = 8
 LANES = 128
-GROUP = 24
+GROUP = 16
+PARTS = 2
+PIECES = 2
 VMEM = pl.BlockSpec(memory_space=pltpu.VMEM)
 SMEM = pl.BlockSpec(memory_space=pltpu.SMEM)
 LIMIT = pltpu.CompilerParams(vmem_limit_bytes=32 * 1024 * 1024)
@@ -79,7 +81,8 @@
                 )
 
 
-def sum_kernel(capacity, cells, in_ref, sky_ref, *half_refs):
+def sum_kernel(capacity, cells, in_ref, *refs):
+    part_refs, sky_ref = refs[:-1], refs[-1]
     rows = sky_ref.shape[1]
     stride = 2 * capacity * rows + 1
     for index in range(sky_ref.shape[0]):
@@ -99,9 +102,11 @@
         return carry
 
     lax.fori_loop(0, in_ref.shape[0] // stride, one_source, 0, unroll=16)
-    for half, ref in enumerate(half_refs):
+    first = 0
+    for ref in part_refs:
         for index in range(ref.shape[0]):
-            ref[index] = sky_ref[half * ref.shape[0] + index]
+            ref[index] = sky_ref[(first + index) % sky_ref.shape[0]]
+        first += ref.shape[0]
 
 
 def windows_at(ref, epoch, start_row, start_col, rows):
@@ -129,11 +134,18 @@
         ref[epoch, kind, side] = jnp.zeros(ref.shape[3:], jnp.float32)
 
 
-def near_kernel(
-    cells, tiles, group, row_ref, col_ref, me_ref, own_ref, low_ref, high_ref, sums_ref, list_ref, count_ref, wide_ref
-):
+def tile_of(refs, index):
+    for ref in refs:
+        if index < ref.shape[0]:
+            return ref[index]
+        index -= ref.shape[0]
+
+
+def near_kernel(tiles, group, split, pieces, row_ref, col_ref, me_ref, *refs):
+    own_refs, twin_refs = refs[:PARTS], refs[PARTS : PARTS + pieces]
+    sums_ref, *list_refs, count_ref, wide_ref = refs[PARTS + pieces :]
     epochs, vels = row_ref.shape
-    rows = own_ref.shape[1]
+    cells, rows = sums_ref.shape[2:4]
     odd = me_ref[0] & 1
     towards = jnp.where((me_ref[0] == 0) | (me_ref[0] == tiles - 1), 0, 2 * odd - 1)
     twin_row = pl.multiple_of((1 - odd) * 2 * rows, rows)
@@ -143,14 +155,13 @@
             clear_sides(wide_ref, epoch, kind)
             for cell in range(cells):
                 index = (epoch * 2 + kind) * cells + cell
-                wide_ref[epoch, kind, cell + 1, rows : 2 * rows, :] = own_ref[index]
-                half, place = divmod(index, low_ref.shape[0])
-                wide_ref[epoch, kind, cell + 1, pl.ds(twin_row, rows), :] = (low_ref, high_ref)[half][place]
-                wide_ref[epoch, kind, cell + 1, pl.ds(far_row, rows), :] = jnp.zeros(
-                    (rows, LANES), jnp.float32
-                )
-
-    def one_velocity(vel, count):
+                at = wide_ref.at[epoch, kind, cell + 1]
+                at[rows : 2 * rows, :] = tile_of(own_refs, index)
+                at[pl.ds(twin_row, rows), :] = tile_of(twin_refs, index)
+                at[pl.ds(far_row, rows), :] = jnp.zeros((rows, LANES), jnp.float32)
+
+    def one_velocity(vel, counts):
+        counts = list(counts)
         sums = [[jnp.zeros((rows, LANES), jnp.float32) for _ in range(cells)] for _ in range(2)]
         for epoch in range(epochs):
             row = row_ref[epoch, vel]
@@ -159,37 +170,38 @@
             for kind in range(2):
                 for cell in range(cells):
                     sums[kind][cell] = sums[kind][cell] + windows[kind][cell]
-            reach = row * towards
+            part = int(epoch >= split[0])
+            place = epoch - part * split[0]
             start_row = row + (1 - odd) * rows
-            list_ref[count] = (vel << 24) | (epoch << 16) | (start_row << 10) | start_col
-            count = count + jnp.where(reach > 0, 1, 0)
+            code = (vel << 24) | (place << 16) | (start_row << 10) | start_col
+            list_refs[part][counts[part]] = code
+            counts[part] = counts[part] + jnp.where(row * towards > 0, 1, 0)
         for kind in range(2):
             for cell in range(cells):
                 sums_ref[vel, kind, cell] = sums[kind][cell]
-        return count
-
-    count = lax.fori_loop(0, vels, one_velocity, jnp.int32(0), unroll=4)
-    for index in range(group):
-        list_ref[count + index] = (((1 - odd) * rows) << 10) | LANES
-    count_ref[0] = count
-    count_ref[1] = odd
-
-
-def far_kernel(cells, group, list_ref, count_ref, far_ref, given_ref, sums_ref, best_ref, wide_ref):
-    vels = sums_ref.shape[0]
-    rows = far_ref.shape[1]
-    epochs = wide_ref.shape[0]
-    far_row = pl.multiple_of(count_ref[1] * rows, rows)
-    zero_row = pl.multiple_of((1 - count_ref[1]) * rows, rows)
-    for epoch in range(epochs):
+        return counts
+
+    counts = lax.fori_loop(0, vels, one_velocity, [jnp.int32(0)] * PARTS, unroll=4)
+    for part, count in enumerate(counts):
+        for index in range(group):
+            list_refs[part][count + index] = (((1 - odd) * rows) << 10) | LANES
+        count_ref[part] = count
+    count_ref[PARTS] = odd
+
+
+def far_kernel(part, group, list_ref, count_ref, far_ref, given_ref, sums_ref, *refs):
+    *best_refs, wide_ref = refs
+    vels, _, cells, rows, _ = sums_ref.shape
+    odd = count_ref[PARTS]
+    far_row = pl.multiple_of(odd * rows, rows)
+    zero_row = pl.multiple_of((1 - odd) * rows, rows)
+    for epoch in range(wide_ref.shape[0]):
         for kind in range(2):
             clear_sides(wide_ref, epoch, kind)
             for cell in range(cells):
-                index = (epoch * 2 + kind) * cells + cell
-                wide_ref[epoch, kind, cell + 1, pl.ds(far_row, rows), :] = far_ref[index]
-                wide_ref[epoch, kind, cell + 1, pl.ds(zero_row, rows), :] = jnp.zeros(
-                    (rows, LANES), jnp.float32
-                )
+                at = wide_ref.at[epoch, kind, cell + 1]
+                at[pl.ds(far_row, rows), :] = far_ref[(epoch * 2 + kind) * cells + cell]
+                at[pl.ds(zero_row, rows), :] = jnp.zeros((rows, LANES), jnp.float32)
 
     def one_group(turn, carry):
         found = []
@@ -205,14 +217,15 @@
                     sums_ref[vel, kind, cell] = sums_ref[vel, kind, cell] + windows[kind][cell]
         return carry
 
-    lax.fori_loop(0, lax.div(count_ref[0] + group - 1, group), one_group, 0)
-    highest = [jnp.full((rows, LANES), -jnp.inf, jnp.float32) for _ in range(cells)]
-    for vel in range(vels):
+    lax.fori_loop(0, lax.div(count_ref[part] + group - 1, group), one_group, 0)
+    for best_ref in best_refs:
+        highest = [jnp.full((rows, LANES), -jnp.inf, jnp.float32) for _ in range(cells)]
+        for vel in range(vels):
+            for cell in range(cells):
+                scale = lax.rsqrt(jnp.maximum(sums_ref[vel, 1, cell], 1.0))
+                highest[cell] = jnp.maximum(highest[cell], sums_ref[vel, 0, cell] * scale)
         for cell in range(cells):
-            scale = lax.rsqrt(jnp.maximum(sums_ref[vel, 1, cell], 1.0))
-            highest[cell] = jnp.maximum(highest[cell], sums_ref[vel, 0, cell] * scale)
-    for cell in range(cells):
-        best_ref[:, cell * LANES : (cell + 1) * LANES] = highest[cell]
+            best_ref[:, cell * LANES : (cell + 1) * LANES] = highest[cell]
 
 
 def body(psi, phi, dest_tile, dest_cell, kernel_id, weight, kernels, row_offsets, col_offsets):
@@ -242,53 +255,59 @@
     outgoing = outgoing.reshape(tiles, stride, 1, width)
     incoming = lax.all_to_all(outgoing, "tile", split_axis=0, concat_axis=0, tiled=True)
     incoming = incoming.reshape(message)
-    sky, *halves = pl.pallas_call(
+    total = epochs * 2 * cells
+    split = [epochs - 3 * epochs // 8, 3 * epochs // 8]
+    skies = pl.pallas_call(
         functools.partial(sum_kernel, capacity, cells),
         out_shape=[
-            jax.ShapeDtypeStruct((epochs * 2 * cells // parts, rows, width), jnp.float32)
-            for parts in (1, 2, 2)
+            jax.ShapeDtypeStruct((count * 2 * cells, rows, width), jnp.float32)
+            for count in split + [epochs // PIECES] * PIECES
         ],
         in_specs=[VMEM],
-        out_specs=[VMEM] * 3,
+        out_specs=[VMEM] * (PARTS + PIECES),
+        scratch_shapes=[pltpu.VMEM((total, rows, width), jnp.float32)],
         compiler_params=LIMIT,
         name="sum_slots",
     )(incoming)
+    own, pieces = skies[:PARTS], skies[PARTS:]
     fields = lax.axis_size("field")
     pairs = [(f * tiles + i, f * tiles + i + 1) for f in range(fields) for i in range(1, tiles - 1, 2)]
     pairs += [
         (f * tiles + i, (f + 1) * tiles + i) for f in range(0, fields - 1, 2) for i in (0, tiles - 1)
     ]
-    far = lax.ppermute(
-        sky, ("field", "tile"), [way for a, b in pairs for way in ((a, b), (b, a))]
-    )
-    twins = [lax.ppermute(half, "tile", [(i, i ^ 1) for i in range(tiles)]) for half in halves]
+    both = [way for a, b in pairs for way in ((a, b), (b, a))]
+    far = [lax.ppermute(part, ("field", "tile"), both) for part in own]
+    twin = [lax.ppermute(piece, "tile", [(i, i ^ 1) for i in range(tiles)]) for piece in pieces]
     me = lax.axis_index("tile").reshape(1)
     vels = row_offsets.shape[1]
     sums_shape = jax.ShapeDtypeStruct((vels, 2, cells, rows, width), jnp.float32)
-    sums, listed, count = pl.pallas_call(
-        functools.partial(near_kernel, cells, tiles, GROUP),
-        out_shape=[
-            sums_shape,
-            pltpu.SMEM((vels * epochs + GROUP,), jnp.int32),
-            pltpu.SMEM((2,), jnp.int32),
-        ],
-        in_specs=[SMEM] * 3 + [VMEM] * 3,
-        out_specs=[VMEM, SMEM, SMEM],
+    sums, *lists, count = pl.pallas_call(
+        functools.partial(near_kernel, tiles, GROUP, split, PIECES),
+        out_shape=[sums_shape]
+        + [pltpu.SMEM((vels * count + GROUP,), jnp.int32) for count in split]
+        + [pltpu.SMEM((PARTS + 1,), jnp.int32)],
+        in_specs=[SMEM] * 3 + [VMEM] * (PARTS + PIECES),
+        out_specs=[VMEM] + [SMEM] * (PARTS + 1),
         scratch_shapes=[pltpu.VMEM((epochs, 2, cells + 2, 3 * rows, width), jnp.float32)],
         compiler_params=LIMIT,
         name="stack_near",
-    )(row_offsets, col_offsets, me, sky, *twins)
-    _, best = pl.pallas_call(
-        functools.partial(far_kernel, cells, GROUP),
-        out_shape=[sums_shape, jax.ShapeDtypeStruct((rows, cells * width), jnp.float32)],
-        in_specs=[SMEM] * 2 + [VMEM] * 2,
-        out_specs=[VMEM, VMEM],
-        input_output_aliases={3: 0},
-        scratch_shapes=[pltpu.VMEM((epochs, 2, cells + 2, 2 * rows, width), jnp.float32)],
-        compiler_params=LIMIT,
-        name="stack_far",
-    )(listed, count, far, sums)
-    return best
+    )(row_offsets, col_offsets, me, *own, *twin)
+    for part in range(PARTS):
+        last = part == PARTS - 1
+        sums, *best = pl.pallas_call(
+            functools.partial(far_kernel, part, GROUP),
+            out_shape=[sums_shape]
+            + [jax.ShapeDtypeStruct((rows, cells * width), jnp.float32)] * last,
+            in_specs=[SMEM] * 2 + [VMEM] * 2,
+            out_specs=[VMEM] * (1 + last),
+            input_output_aliases={3: 0},
+            scratch_shapes=[
+                pltpu.VMEM((split[part], 2, cells + 2, 2 * rows, width), jnp.float32)
+            ],
+            compiler_params=LIMIT,
+            name="stack_far",
+        )(lists[part], count, far[part], sums)
+    return best[0]
 
 
 def solution(mesh):

time: 33.6 us -> 33.1 us (0.985)
  waiting for transfers between devices: 2.63 us -> 1.66 us
    ppermute x3 -> x4, waiting for transfers between devices: 2.63 us -> 1.66 us  [the longest x2 1.07 us: body(): lax.ppermute(piece, 'tile', [(i, i ^ 1) for i in range(tiles)])]
    ppermute x3 -> x4, starting transfers between devices: 2.23 us -> 2.49 us  [the longest x2 1.28 us: body(): lax.ppermute(piece, 'tile', [(i, i ^ 1) for i in range(tiles)])]
    pallas_call x2 -> x3, Pallas kernels: 3.8 us -> 4.01 us  [the longest x1 2.2 us: body(): pl.pallas_call(functools.partial(near_kernel, tiles, GROUP, split, PIECES...]
  transfers between devices with their start and end apart: 3 -> 4, of which waited for: 3 -> 4; matrix products, arithmetic and copies ran while one was open for 0% -> 0% of each run, Pallas kernels for 7% -> 9%
where the time goes in v7:
time: 33.1 us; the launch traced here: 32.9 us
  blocking collectives  22.9 us (69%)
  Pallas kernels  5.88 us (18%)
  starting transfers between devices  2.49 us (8%)
  waiting for transfers between devices  1.66 us (5%)
    all_to_all x1, blocking collectives, body(): lax.all_to_all(outgoing, 'tile', split_axis=0, concat_axis=0, tiled=True)  22.9 us
    pallas_call x1, Pallas kernels, body(): pl.pallas_call(functools.partial(near_kernel, tiles, GROUP, split, PIECES...  2.2 us
    pallas_call x2, Pallas kernels, body(): pl.pallas_call(functools.partial(far_kernel, part, GROUP), out_shape=[sum...  1.81 us
    pallas_call x1, Pallas kernels, body(): pl.pallas_call(functools.partial(pack_kernel, capacity), out_shape=jax.Sh...  1.43 us
    ppermute x2, starting transfers between devices, body(): lax.ppermute(piece, 'tile', [(i, i ^ 1) for i in range(tiles)])  1.28 us
    ppermute x2, starting transfers between devices, body(): far = [lax.ppermute(part, ('field', 'tile'), both) for part in own]  1.21 us
    ppermute x2, waiting for transfers between devices, body(): lax.ppermute(piece, 'tile', [(i, i ^ 1) for i in range(tiles)])  1.07 us
  transfers between devices with their start and end apart: 4, of which 4 were waited for; matrix products, arithmetic and copies ran while one was open for 0% of the time, Pallas kernels for 9%

profile of v7, /device:TPU:1, one launch (start us, length us, event | category | flops | bytes accessed | tf_op | source)
XLA Modules:
  0.0 32.9 jit_solution(2115589807229836839)
XLA Ops:
  0.0 1.4 %pack.1 = f32[1040,128]{1,0:T(8,128)S(1)} custom-call(s32[4,1,8]{2,1,0:T(1,128)} %bitcast.8, s32[4,8]{1,0:T(4,128)} %refs_1_.1, s32[4,8]{1,0:T(4,128)} %refs_2_.1, f32[4,8]{1,0:T(4,128)} %refs_3_.1, f32[4,8,8,128]{3,2,1,0:T(8,128)} %refs_4_.1, f32[4,8,8,128]{3,2,1,0:T(8,128)} %refs_5_.1, f32[8,128,128]{2,1,0:T(8,128)} %refs_6_.1), custom_call_target="tpu_custom_call" | custom-call | tf_op jit(solution)/shard_map/pack/pallas_call | solution.py:238
  1.4 22.9 %all_to_all.5 = f32[16,65,1,128]{3,2,1,0:T(1,128)S(1)} all-to-all(f32[16,65,1,128]{3,2,1,0:T(1,128)S(1)} %bitcast.7), channel_id=1, replica_groups=mesh['field'=2,'tile'=16] {'tile'}, dimensions={0} | all-to-all | bytes 1064960 | tf_op jit(solution)/shard_map/all_to_all | solution.py:256
  24.3 0.4 %sum_slots.1 = (f32[40,8,128]{2,1,0:T(8,128)S(1)}, f32[24,8,128]{2,1,0:T(8,128)S(1)}, f32[32,8,128]{2,1,0:T(8,128)S(1)}, f32[32,8,128]{2,1,0:T(8,128)S(1)}) custom-call(f32[1040,128]{1,0:T(8,128)S(1)} %bitcast.6), custom_call_target="tpu_custom_call" | custom-call | tf_op jit(solution)/shard_map/sum_slots/pallas_call | solution.py:260
  24.8 0.9 %collective-permute-start.3 = (f32[40,8,128]{2,1,0:T(8,128)S(1)}, f32[40,8,128]{2,1,0:T(8,128)S(1)}, u32[]{:S(2)}, u32[]{:S(2)}) collective-permute-start(f32[40,8,128]{2,1,0:T(8,128)S(1)} %get-tuple-element.14.refs_0_), channel_id=1, source_target_pairs={{1,2},{2,1},{3,4},{4,3},{5,6},{6,5},{7,8},{8,7},{9,10},{10,9},{11,... | collective-permute-start | bytes 491528 | tf_op jit(solution)/shard_map/ppermute | solution.py:279
  25.7 1.3 %collective-permute-start = (f32[32,8,128]{2,1,0:T(8,128)S(1)}, f32[32,8,128]{2,1,0:T(8,128)S(1)}, u32[]{:S(2)}, u32[]{:S(2)}) collective-permute-start(f32[32,8,128]{2,1,0:T(8,128)S(1)} %get-tuple-element.16), channel_id=1, source_target_pairs={{0,1},{1,0},{2,3},{3,2},{4,5},{5,4},{6,7},{7,6},{8,9},{9,8},{10,11... | collective-permute-start | bytes 393224 | tf_op jit(solution)/shard_map/ppermute | solution.py:280
  27.0 0.0 collective-permute-start.1
  27.0 0.0 copy-start.1
  27.0 0.0 copy-start
  27.0 0.3 collective-permute-start.2
  27.3 0.7 %collective-permute-done.refs_2_ = f32[32,8,128]{2,1,0:T(8,128)S(1)} collective-permute-done((f32[32,8,128]{2,1,0:T(8,128)S(1)}, f32[32,8,128]{2,1,0:T(8,128)S(1)}, u32[]{:S(2)}, u32[]{:S(2)}) %collective-permute-start) | collective-permute-done | bytes 131104 | tf_op jit(solution)/shard_map/ppermute | solution.py:280
  28.0 0.4 %collective-permute-done.1.refs_3_ = f32[32,8,128]{2,1,0:T(8,128)S(1)} collective-permute-done((f32[32,8,128]{2,1,0:T(8,128)S(1)}, f32[32,8,128]{2,1,0:T(8,128)S(1)}, u32[]{:S(2)}, u32[]{:S(2)}) %collective-permute-start.1) | collective-permute-done | bytes 131104 | tf_op jit(solution)/shard_map/ppermute | solution.py:280
  28.3 0.0 copy-done.1
  28.3 0.0 copy-done
  28.3 2.2 %stack_near.1 = (f32[16,2,4,8,128]{4,3,2,1,0:T(8,128)S(1)}, s32[96]{0:T(128)S(4)}, s32[64]{0:T(128)S(4)}, s32[3]{0:T(128)S(4)}) custom-call(s32[8,16]{1,0:T(8,128)S(1)} %copy-done, s32[8,16]{1,0:T(8,128)S(1)} %copy-done.1, s32[1]{0:T(128)} %bitcast.me_ref, f32[40,8,128]{2,1,0:T(8,128)S(1)} %get-tuple-element.14.refs_0_, ...), custom_call_target="tpu_custom_call" | custom-call | tf_op jit(solution)/shard_map/stack_near/pallas_call | solution.py:284
  30.5 0.2 collective-permute-done.3.far_ref
  30.8 0.7 %stack_far.2.given_ref = f32[16,2,4,8,128]{4,3,2,1,0:T(8,128)S(1)} custom-call(s32[96]{0:T(128)S(4)} %get-tuple-element.20.list_ref, s32[3]{0:T(128)S(4)} %get-tuple-element.19.count_ref, f32[40,8,128]{2,1,0:T(8,128)S(1)} %collective-permute-done.3.far_ref, f32[16,2,4,8,128]{4,3,2,1,0:T(8,128)S(1)} %get-tuple-element.21.given_ref), custom_call_target="tpu_custom_call", output_to_operand_aliasing={{}: (3, {})} | custom-call | tf_op jit(solution)/shard_map/stack_far/pallas_call | solution.py:297
  31.5 0.4 %collective-permute-done.2.far_ref = f32[24,8,128]{2,1,0:T(8,128)S(1)} collective-permute-done((f32[24,8,128]{2,1,0:T(8,128)S(1)}, f32[24,8,128]{2,1,0:T(8,128)S(1)}, u32[]{:S(2)}, u32[]{:S(2)}) %collective-permute-start.2) | collective-permute-done | bytes 98336 | tf_op jit(solution)/shard_map/ppermute | solution.py:279
  31.8 1.1 %stack_far.3 = (f32[16,2,4,8,128]{4,3,2,1,0:T(8,128)S(1)}, f32[8,512]{1,0:T(8,128)}) custom-call(s32[64]{0:T(128)S(4)} %get-tuple-element.18.list_ref, s32[3]{0:T(128)S(4)} %get-tuple-element.19.count_ref, f32[24,8,128]{2,1,0:T(8,128)S(1)} %collective-permute-done.2.far_ref, ...), custom_call_target="tpu_custom_call", output_to_operand_aliasing={{0}: (3, {})} | custom-call | tf_op jit(solution)/shard_map/stack_far/pallas_call | solution.py:297
Async XLA Ops:
  24.8 6.0 %collective-permute-start.3 = (f32[40,8,128]{2,1,0:T(8,128)S(1)}, f32[40,8,128]{2,1,0:T(8,128)S(1)}, u32[]{:S(2)}, u32[]{:S(2)}) collective-permute-start(f32[40,8,128]{2,1,0:T(8,128)S(1)} %get-tuple-element.14.refs_0_), channel_id=1, source_target_pairs={{1,2},{2,1},{3,4},{4,3},{5,6},{6,5},{7,8},{8,7},{9,10},{10,9},{11,... | collective-permute-start | bytes 491528 | tf_op jit(solution)/shard_map/ppermute | solution.py:279
  25.7 2.3 %collective-permute-start = (f32[32,8,128]{2,1,0:T(8,128)S(1)}, f32[32,8,128]{2,1,0:T(8,128)S(1)}, u32[]{:S(2)}, u32[]{:S(2)}) collective-permute-start(f32[32,8,128]{2,1,0:T(8,128)S(1)} %get-tuple-element.16), channel_id=1, source_target_pairs={{0,1},{1,0},{2,3},{3,2},{4,5},{5,4},{6,7},{7,6},{8,9},{9,8},{10,11... | collective-permute-start | bytes 393224 | tf_op jit(solution)/shard_map/ppermute | solution.py:280
  27.0 1.3 %collective-permute-start.1 = (f32[32,8,128]{2,1,0:T(8,128)S(1)}, f32[32,8,128]{2,1,0:T(8,128)S(1)}, u32[]{:S(2)}, u32[]{:S(2)}) collective-permute-start(f32[32,8,128]{2,1,0:T(8,128)S(1)} %get-tuple-element.17), channel_id=1, source_target_pairs={{0,1},{1,0},{2,3},{3,2},{4,5},{5,4},{6,7},{7,6},{8,9},{9,8},{10,11... | collective-permute-start | bytes 393224 | tf_op jit(solution)/shard_map/ppermute | solution.py:280
  27.0 1.3 %copy-start.1 = (s32[8,16]{1,0:T(8,128)S(1)}, s32[8,16]{1,0:T(8,128)}, u32[]{:S(2)}) copy-start(s32[8,16]{1,0:T(8,128)} %col_ref.1) | copy-start | bytes 1540
  27.0 1.3 %copy-start = (s32[8,16]{1,0:T(8,128)S(1)}, s32[8,16]{1,0:T(8,128)}, u32[]{:S(2)}) copy-start(s32[8,16]{1,0:T(8,128)} %row_ref.1) | copy-start | bytes 1540
  27.0 4.8 %collective-permute-start.2 = (f32[24,8,128]{2,1,0:T(8,128)S(1)}, f32[24,8,128]{2,1,0:T(8,128)S(1)}, u32[]{:S(2)}, u32[]{:S(2)}) collective-permute-start(f32[24,8,128]{2,1,0:T(8,128)S(1)} %get-tuple-element.15.refs_1_), channel_id=1, source_target_pairs={{1,2},{2,1},{3,4},{4,3},{5,6},{6,5},{7,8},{8,7},{9,10},{10,9},{11,... | collective-permute-start | bytes 294920 | tf_op jit(solution)/shard_map/ppermute | solution.py:279

commit v8 on v7

--- a/solution.py
+++ b/solution.py
@@ -12,47 +12,48 @@
 LANES = 128
 GROUP = 16
 PARTS = 2
+ORDER = (4, 5, 2, 3, 7, 6, 1)
 PIECES = 2
 VMEM = pl.BlockSpec(memory_space=pltpu.VMEM)
 SMEM = pl.BlockSpec(memory_space=pltpu.SMEM)
 LIMIT = pltpu.CompilerParams(vmem_limit_bytes=32 * 1024 * 1024)
 
 
-def pack_kernel(capacity, *refs):
-    given, out_ref, (diag_ref, note_ref, used_ref, spot_ref), held, sems = (
-        refs[:7], refs[7], refs[8:12], refs[12:19], refs[19]
-    )
+def pack_kernel(capacity, outputs, *refs):
+    given, out_refs, rest = refs[:8], refs[8 : 8 + outputs], refs[8 + outputs :]
+    (slots_ref, diag_ref, note_ref, used_ref, spot_ref), held, sems = rest[:5], rest[5:13], rest[13]
     copies = [
         pltpu.make_async_copy(source, target, sems.at[index])
         for index, (source, target) in enumerate(zip(given, held, strict=True))
     ]
     for copy in copies[::-1]:
         copy.start()
-    tile_ref, cell_ref, id_ref, weight_ref, psi_ref, phi_ref, table_ref = held
-    cells, epochs = psi_ref.shape[:2]
-    tiles, width = used_ref.shape[0], psi_ref.shape[3]
-    rows = psi_ref.shape[2]
-    stride = 2 * capacity * rows + 1
+    tile_ref, cell_ref, id_ref, weight_ref, base_ref, psi_ref, phi_ref, table_ref = held
+    cells, epochs, rows, width = psi_ref.shape
+    chips = note_ref.shape[0]
+    stride = 4 * capacity * rows + 1
 
     def clear(tile, carry):
         used_ref[tile] = 0
-        note_ref[tile] = jnp.zeros(note_ref.shape[1:], jnp.float32)
         return carry
 
-    lax.fori_loop(0, tiles, clear, 0, unroll=16)
-    for copy in copies[:4]:
+    lax.fori_loop(0, used_ref.shape[0], clear, 0, unroll=16)
+    note_ref[...] = jnp.zeros(note_ref.shape, jnp.float32)
+    for copy in copies[:5]:
         copy.wait()
 
     lane = lax.broadcasted_iota(jnp.int32, (1, LANES), 1)
     for block in range(cells):
         for epoch in range(epochs):
-            tile = tile_ref[block, 0, epoch]
+            tile = tile_ref[block, 0, epoch] ^ base_ref[0]
+            chip, core = tile >> 1, tile & 1
             slot = used_ref[tile]
             used_ref[tile] = slot + 1
-            spot_ref[block, epoch] = tile * stride + 2 * rows * slot
+            slot = core * capacity + slot
+            spot_ref[block, epoch] = chip * stride + 2 * rows * slot
             place = (epoch * 2 * cells + cell_ref[block, epoch] + 1).astype(jnp.float32)
-            note_ref[tile] = jnp.where(lane == slot, place, note_ref[tile])
-    for copy in copies[4:]:
+            note_ref[chip] = jnp.where(lane == slot, place, note_ref[chip])
+    for copy in copies[5:]:
         copy.wait()
 
     source = lax.broadcasted_iota(jnp.int32, (width, width), 0)
@@ -63,50 +64,71 @@
             row = jnp.sum(jnp.where(mask, table_ref[index], 0.0), axis=0, keepdims=True)
             diag_ref[index, place : place + 1, :] = row
 
-    def write_note(tile, carry):
-        out_ref[pl.ds(tile * stride + stride - 1, 1), :] = note_ref[tile]
+    def write_note(chip, carry):
+        slots_ref[pl.ds(chip * stride + stride - 1, 1), :] = note_ref[chip]
         return carry
 
-    lax.fori_loop(0, tiles, write_note, 0, unroll=16)
+    lax.fori_loop(0, chips, write_note, 0, unroll=8)
     for block in range(cells):
         for epoch in range(epochs):
             spot = spot_ref[block, epoch]
             bands = diag_ref[id_ref[block, epoch]] * weight_ref[block, epoch]
             for kind, ref in enumerate((psi_ref, phi_ref)):
                 values = ref[block, epoch]
-                out_ref[pl.ds(spot + kind * rows, rows), :] = (
+                slots_ref[pl.ds(spot + kind * rows, rows), :] = (
                     values * bands[1:2]
                     + pltpu.roll(values, 1, 1) * bands[0:1]
                     + pltpu.roll(values, width - 1, 1) * bands[2:3]
                 )
-
-
-def sum_kernel(capacity, cells, in_ref, *refs):
-    part_refs, sky_ref = refs[:-1], refs[-1]
-    rows = sky_ref.shape[1]
-    stride = 2 * capacity * rows + 1
-    for index in range(sky_ref.shape[0]):
-        sky_ref[index] = jnp.zeros(sky_ref.shape[1:], jnp.float32)
-
-    def one_source(source, carry):
-        first = source * stride
-        notes = in_ref[pl.ds(first + stride - 1, 1), :].astype(jnp.int32)
-        for slot in range(capacity):
-            place = notes[0, slot] - 1
-            there = place >= 0
-            base = jnp.maximum(place, 0)
-            for kind in range(2):
-                value = in_ref[pl.ds(first + (2 * slot + kind) * rows, rows), :]
-                value = jnp.where(there, value, 0.0)
-                sky_ref[base + kind * cells] = sky_ref[base + kind * cells] + value
-        return carry
-
-    lax.fori_loop(0, in_ref.shape[0] // stride, one_source, 0, unroll=16)
     first = 0
-    for ref in part_refs:
-        for index in range(ref.shape[0]):
-            ref[index] = sky_ref[(first + index) % sky_ref.shape[0]]
-        first += ref.shape[0]
+    for out_ref in out_refs:
+        count = out_ref.shape[0]
+        flat_ref = out_ref.reshape(count, width)
+        for row in range(0, count, rows):
+            size = min(rows, count - row)
+            flat_ref[row : row + size, :] = slots_ref[first + row : first + row + size, :]
+        first += count
+
+
+def sum_kernel(capacity, cells, *refs):
+    in_refs, sky_refs = refs[:-2], refs[-2:]
+    rows, width = sky_refs[0].shape[1:]
+    stride = 4 * capacity * rows + 1
+    for sky_ref in sky_refs:
+        for index in range(sky_ref.shape[0]):
+            sky_ref[index] = jnp.zeros((rows, width), jnp.float32)
+    for in_ref in in_refs:
+        flat_ref = in_ref.reshape(in_ref.shape[0], width)
+
+        def one_message(message, carry, flat_ref=flat_ref):
+            first = message * stride
+            notes = flat_ref[pl.ds(first + stride - 1, 1), :].astype(jnp.int32)
+            for slot in range(2 * capacity):
+                sky_ref = sky_refs[slot // capacity]
+                place = notes[0, slot] - 1
+                there = place >= 0
+                base = jnp.maximum(place, 0)
+                for kind in range(2):
+                    value = flat_ref[pl.ds(first + (2 * slot + kind) * rows, rows), :]
+                    value = jnp.where(there, value, 0.0)
+                    sky_ref[base + kind * cells] = sky_ref[base + kind * cells] + value
+            return carry
+
+        messages = in_ref.shape[0] // stride
+        if messages == 1:
+            one_message(0, 0)
+        else:
+            lax.fori_loop(0, messages, one_message, 0, unroll=8)
+
+
+def join_kernel(mine_ref, other_ref, *part_refs):
+    total = mine_ref.shape[0]
+    first = 0
+    for part_ref in part_refs:
+        for index in range(part_ref.shape[0]):
+            place = (first + index) % total
+            part_ref[index] = mine_ref[place] + other_ref[place]
+        first += part_ref.shape[0]
 
 
 def windows_at(ref, epoch, start_row, start_col, rows):
@@ -232,43 +254,74 @@
     tiles = lax.axis_size("tile")
     cells, epochs, rows, width = psi.shape
     capacity = max(2, 2 * cells * epochs // tiles)
-    stride = 2 * capacity * rows + 1
-    message = (tiles * stride, width)
-    given = (jnp.swapaxes(dest_tile, 1, 2), dest_cell, kernel_id, weight, psi, phi, kernels)
+    chips = tiles // 2
+    stride = 4 * capacity * rows + 1
+    me = lax.axis_index("tile")
+    direct = chips <= len(ORDER) + 1
+    base = me if direct else me & 1
+    given = (jnp.swapaxes(dest_tile, 1, 2), dest_cell, kernel_id, weight, base.reshape(1))
+    given += (psi, phi, kernels)
+    outputs = chips if direct else 1
     outgoing = pl.pallas_call(
-        functools.partial(pack_kernel, capacity),
-        out_shape=jax.ShapeDtypeStruct(message, jnp.float32),
-        in_specs=[pl.BlockSpec(memory_space=pl.ANY)] * 7,
-        out_specs=VMEM,
+        functools.partial(pack_kernel, capacity, outputs),
+        out_shape=[
+            jax.ShapeDtypeStruct((chips * stride // outputs, 1, width), jnp.float32)
+            for _ in range(outputs)
+        ],
+        in_specs=[pl.BlockSpec(memory_space=pl.ANY)] * len(given),
+        out_specs=[VMEM] * outputs,
         scratch_shapes=[
+            pltpu.VMEM((chips * stride, width), jnp.float32),
             pltpu.VMEM((kernels.shape[0], 3, width), jnp.float32),
-            pltpu.VMEM((tiles, 1, LANES), jnp.float32),
+            pltpu.VMEM((chips, 1, LANES), jnp.float32),
             pltpu.SMEM((tiles,), jnp.int32),
             pltpu.SMEM((cells, epochs), jnp.int32),
         ]
-        + [pltpu.SMEM(array.shape, array.dtype) for array in given[:4]]
-        + [pltpu.VMEM(array.shape, array.dtype) for array in given[4:]]
-        + [pltpu.SemaphoreType.DMA((7,))],
-        compiler_params=pltpu.CompilerParams(vmem_limit_bytes=32 * 1024 * 1024),
+        + [pltpu.SMEM(array.shape, array.dtype) for array in given[:5]]
+        + [pltpu.VMEM(array.shape, array.dtype) for array in given[5:]]
+        + [pltpu.SemaphoreType.DMA((len(given),))],
+        compiler_params=LIMIT,
         name="pack",
     )(*(pltpu.with_memory_space_constraint(array, pltpu.HBM) for array in given))
-    outgoing = outgoing.reshape(tiles, stride, 1, width)
-    incoming = lax.all_to_all(outgoing, "tile", split_axis=0, concat_axis=0, tiled=True)
-    incoming = incoming.reshape(message)
+    if direct:
+        incoming = [outgoing[0]] + [
+            lax.ppermute(outgoing[k], "tile", [(i, i ^ (2 * k)) for i in range(tiles)])
+            for k in ORDER
+            if k < chips
+        ]
+    else:
+        incoming = lax.all_to_all(
+            outgoing[0].reshape(chips, stride, 1, width),
+            "tile",
+            split_axis=0,
+            concat_axis=0,
+            axis_index_groups=[list(range(core, tiles, 2)) for core in range(2)],
+            tiled=True,
+        )
+        incoming = [incoming.reshape(chips * stride, 1, width)]
     total = epochs * 2 * cells
+    sky_shape = jax.ShapeDtypeStruct((total, rows, width), jnp.float32)
+    mine, others = pl.pallas_call(
+        functools.partial(sum_kernel, capacity, cells),
+        out_shape=[sky_shape, sky_shape],
+        in_specs=[VMEM] * len(incoming),
+        out_specs=[VMEM, VMEM],
+        compiler_params=LIMIT,
+        name="sum_slots",
+    )(*incoming)
+    other = lax.ppermute(others, "tile", [(i, i ^ 1) for i in range(tiles)])
     split = [epochs - 3 * epochs // 8, 3 * epochs // 8]
     skies = pl.pallas_call(
-        functools.partial(sum_kernel, capacity, cells),
+        join_kernel,
         out_shape=[
             jax.ShapeDtypeStruct((count * 2 * cells, rows, width), jnp.float32)
             for count in split + [epochs // PIECES] * PIECES
         ],
-        in_specs=[VMEM],
+        in_specs=[VMEM, VMEM],
         out_specs=[VMEM] * (PARTS + PIECES),
-        scratch_shapes=[pltpu.VMEM((total, rows, width), jnp.float32)],
         compiler_params=LIMIT,
-        name="sum_slots",
-    )(incoming)
+        name="join",
+    )(mine, other)
     own, pieces = skies[:PARTS], skies[PARTS:]
     fields = lax.axis_size("field")
     pairs = [(f * tiles + i, f * tiles + i + 1) for f in range(fields) for i in range(1, tiles - 1, 2)]
@@ -278,7 +331,6 @@
     both = [way for a, b in pairs for way in ((a, b), (b, a))]
     far = [lax.ppermute(part, ("field", "tile"), both) for part in own]
     twin = [lax.ppermute(piece, "tile", [(i, i ^ 1) for i in range(tiles)]) for piece in pieces]
-    me = lax.axis_index("tile").reshape(1)
     vels = row_offsets.shape[1]
     sums_shape = jax.ShapeDtypeStruct((vels, 2, cells, rows, width), jnp.float32)
     sums, *lists, count = pl.pallas_call(
@@ -291,7 +343,7 @@
         scratch_shapes=[pltpu.VMEM((epochs, 2, cells + 2, 3 * rows, width), jnp.float32)],
         compiler_params=LIMIT,
         name="stack_near",
-    )(row_offsets, col_offsets, me, *own, *twin)
+    )(row_offsets, col_offsets, me.reshape(1), *own, *twin)
     for part in range(PARTS):
         last = part == PARTS - 1
         sums, *best = pl.pallas_call(

time: 33.1 us -> 29.2 us (0.88)
  blocking collectives: 22.9 us -> 0 us
  starting transfers between devices: 2.49 us -> 18.5 us
  waiting for transfers between devices: 1.66 us -> 4.83 us
    all_to_all x1 -> x0, blocking collectives: 22.9 us -> none  [body(): lax.all_to_all(outgoing, 'tile', split_axis=0, concat_axis=0, tiled=True)]
    ppermute x0 -> x8, starting transfers between devices: none -> 16.2 us  [the longest x7 13.1 us: body(): lax.ppermute(outgoing[k], 'tile', [(i, i ^ 2 * k) for i in range(tiles)])]
    ppermute x0 -> x8, waiting for transfers between devices: none -> 3.11 us  [the longest x7 1.95 us: body(): lax.ppermute(outgoing[k], 'tile', [(i, i ^ 2 * k) for i in range(tiles)])]
    pallas_call x1 -> x2, Pallas kernels: 1.43 us -> 1.55 us  [the longest x1 1.51 us: body(): pl.pallas_call(functools.partial(pack_kernel, capacity, outputs), out_sha...]
  transfers between devices with their start and end apart: 4 -> 12, of which waited for: 4 -> 7; matrix products, arithmetic and copies ran while one was open for 0% -> 0% of each run, Pallas kernels for 9% -> 9%
where the time goes in v8:
time: 29.2 us; the launch traced here: 29 us
  starting transfers between devices  18.5 us (63%)
  Pallas kernels  5.64 us (19%)
  waiting for transfers between devices  4.83 us (17%)
    ppermute x7, starting transfers between devices, body(): lax.ppermute(outgoing[k], 'tile', [(i, i ^ 2 * k) for i in range(tiles)])  13.1 us
    ppermute x1, starting transfers between devices, body(): other = lax.ppermute(others, 'tile', [(i, i ^ 1) for i in range(tiles)])  3.07 us
    pallas_call x1, Pallas kernels, body(): pl.pallas_call(functools.partial(near_kernel, tiles, GROUP, split, PIECES...  2.2 us
    ppermute x7, waiting for transfers between devices, body(): lax.ppermute(outgoing[k], 'tile', [(i, i ^ 2 * k) for i in range(tiles)])  1.95 us
    pallas_call x2, Pallas kernels, body(): pl.pallas_call(functools.partial(far_kernel, part, GROUP), out_shape=[sum...  1.59 us
    pallas_call x1, Pallas kernels, body(): pl.pallas_call(functools.partial(pack_kernel, capacity, outputs), out_sha...  1.51 us
    ppermute x2, starting transfers between devices, body(): lax.ppermute(piece, 'tile', [(i, i ^ 1) for i in range(tiles)])  1.32 us
    ppermute x1, waiting for transfers between devices, body(): other = lax.ppermute(others, 'tile', [(i, i ^ 1) for i in range(tiles)])  1.16 us
  transfers between devices with their start and end apart: 12, of which 7 were waited for; matrix products, arithmetic and copies ran while one was open for 0% of the time, Pallas kernels for 9%

profile of v8, /device:TPU:1, one launch (start us, length us, event | category | flops | bytes accessed | tf_op | source)
XLA Modules:
  0.0 29.0 jit_solution(7267716347965240842)
XLA Ops:
  0.0 1.5 %pack.1 = (f32[129,1,128]{2,1,0:T(1,128)S(1)}, f32[129,1,128]{2,1,0:T(1,128)S(1)}, f32[129,1,128]{2,1,0:T(1,128)S(1)}, f32[129,1,128]{2,1,0:T(1,128)S(1)}, f32[1...) custom-call(s32[4,1,8]{2,1,0:T(1,128)} %bitcast.4, ...), custom_call_target="tpu_custom_call" | custom-call | tf_op jit(solution)/shard_map/pack/pallas_call | solution.py:265
  1.5 3.2 %collective-permute-start = (f32[129,1,128]{2,1,0:T(1,128)S(1)}, f32[129,1,128]{2,1,0:T(1,128)S(1)}, u32[]{:S(2)}, u32[]{:S(2)}) collective-permute-start(f32[129,1,128]{2,1,0:T(1,128)S(1)} %get-tuple-element.25), channel_id=1, source_target_pairs={{0,8},{1,9},{2,10},{3,11},{4,12},{5,13},{6,14},{7,15},{8,0},{9,1},... | collective-permute-start | bytes 198152 | tf_op jit(solution)/shard_map/ppermute | solution.py:288
  4.7 1.0 %collective-permute-start.1 = (f32[129,1,128]{2,1,0:T(1,128)S(1)}, f32[129,1,128]{2,1,0:T(1,128)S(1)}, u32[]{:S(2)}, u32[]{:S(2)}) collective-permute-start(f32[129,1,128]{2,1,0:T(1,128)S(1)} %get-tuple-element.26), channel_id=1, source_target_pairs={{0,10},{1,11},{2,8},{3,9},{4,14},{5,15},{6,12},{7,13},{8,2},{9,3},... | collective-permute-start | bytes 198152 | tf_op jit(solution)/shard_map/ppermute | solution.py:288
  5.8 1.3 %collective-permute-start.2 = (f32[129,1,128]{2,1,0:T(1,128)S(1)}, f32[129,1,128]{2,1,0:T(1,128)S(1)}, u32[]{:S(2)}, u32[]{:S(2)}) collective-permute-start(f32[129,1,128]{2,1,0:T(1,128)S(1)} %get-tuple-element.27), channel_id=1, source_target_pairs={{0,4},{1,5},{2,6},{3,7},{4,0},{5,1},{6,2},{7,3},{8,12},{9,13},{10,... | collective-permute-start | bytes 198152 | tf_op jit(solution)/shard_map/ppermute | solution.py:288
  7.1 0.1 collective-permute-start.3
  7.2 4.3 %collective-permute-start.4 = (f32[129,1,128]{2,1,0:T(1,128)S(1)}, f32[129,1,128]{2,1,0:T(1,128)S(1)}, u32[]{:S(2)}, u32[]{:S(2)}) collective-permute-start(f32[129,1,128]{2,1,0:T(1,128)S(1)} %get-tuple-element.29), channel_id=1, source_target_pairs={{0,14},{1,15},{2,12},{3,13},{4,10},{5,11},{6,8},{7,9},{8,6},{9,7},... | collective-permute-start | bytes 198152 | tf_op jit(solution)/shard_map/ppermute | solution.py:288
  11.4 0.0 collective-permute-done.refs_1_
  11.4 1.7 %collective-permute-start.5 = (f32[129,1,128]{2,1,0:T(1,128)S(1)}, f32[129,1,128]{2,1,0:T(1,128)S(1)}, u32[]{:S(2)}, u32[]{:S(2)}) collective-permute-start(f32[129,1,128]{2,1,0:T(1,128)S(1)} %get-tuple-element.30), channel_id=1, source_target_pairs={{0,12},{1,13},{2,14},{3,15},{4,8},{5,9},{6,10},{7,11},{8,4},{9,5},... | collective-permute-start | bytes 198152 | tf_op jit(solution)/shard_map/ppermute | solution.py:288
  13.1 0.0 collective-permute-done.1.refs_2_
  13.1 1.5 %collective-permute-start.6 = (f32[129,1,128]{2,1,0:T(1,128)S(1)}, f32[129,1,128]{2,1,0:T(1,128)S(1)}, u32[]{:S(2)}, u32[]{:S(2)}) collective-permute-start(f32[129,1,128]{2,1,0:T(1,128)S(1)} %get-tuple-element.31), channel_id=1, source_target_pairs={{0,2},{1,3},{2,0},{3,1},{4,6},{5,7},{6,4},{7,5},{8,10},{9,11},{10,... | collective-permute-start | bytes 198152 | tf_op jit(solution)/shard_map/ppermute | solution.py:288
  14.6 0.0 collective-permute-done.2.refs_3_
  14.6 0.0 collective-permute-done.3.refs_4_
  14.6 0.0 collective-permute-done.4.refs_5_
  14.6 1.8 %collective-permute-done.5.refs_6_ = f32[129,1,128]{2,1,0:T(1,128)S(1)} collective-permute-done((f32[129,1,128]{2,1,0:T(1,128)S(1)}, f32[129,1,128]{2,1,0:T(1,128)S(1)}, u32[]{:S(2)}, u32[]{:S(2)}) %collective-permute-start.5) | collective-permute-done | bytes 66080 | tf_op jit(solution)/shard_map/ppermute | solution.py:288
  16.5 0.1 collective-permute-done.6.refs_7_
  16.6 0.3 %sum_slots.1 = (f32[64,8,128]{2,1,0:T(8,128)S(1)}, f32[64,8,128]{2,1,0:T(8,128)S(1)}) custom-call(f32[129,1,128]{2,1,0:T(1,128)S(1)} %get-tuple-element.24.refs_0_, f32[129,1,128]{2,1,0:T(1,128)S(1)} %collective-permute-done.refs_1_, f32[129,1,128]{2,1,0:T(1,128)S(1)} %collective-permute-done.1.refs_2_, f32[129,1,128]{2,1,0:T(1,128)S(1)} %collective-permute-done.2.refs_3_, ...), custom_call_target="tpu_custom_call" | custom-call | tf_op jit(solution)/shard_map/sum_slots/pallas_call | solution.py:304
  16.9 3.1 %collective-permute-start.7 = (f32[64,8,128]{2,1,0:T(8,128)S(1)}, f32[64,8,128]{2,1,0:T(8,128)S(1)}, u32[]{:S(2)}, u32[]{:S(2)}) collective-permute-start(f32[64,8,128]{2,1,0:T(8,128)S(1)} %get-tuple-element.33), channel_id=1, source_target_pairs={{0,1},{1,0},{2,3},{3,2},{4,5},{5,4},{6,7},{7,6},{8,9},{9,8},{10,11... | collective-permute-start | bytes 786440 | tf_op jit(solution)/shard_map/ppermute | solution.py:312
  19.9 1.2 %collective-permute-done.7.other_ref = f32[64,8,128]{2,1,0:T(8,128)S(1)} collective-permute-done((f32[64,8,128]{2,1,0:T(8,128)S(1)}, f32[64,8,128]{2,1,0:T(8,128)S(1)}, u32[]{:S(2)}, u32[]{:S(2)}) %collective-permute-start.7) | collective-permute-done | bytes 262176 | tf_op jit(solution)/shard_map/ppermute | solution.py:312
  21.1 0.0 copy-start.1
  21.1 0.0 copy-start
  21.2 0.6 %collective-permute-start.11 = (f32[40,8,128]{2,1,0:T(8,128)S(1)}, f32[40,8,128]{2,1,0:T(8,128)S(1)}, u32[]{:S(2)}, u32[]{:S(2)}) collective-permute-start(f32[40,8,128]{2,1,0:T(8,128)S(1)} %get-tuple-element.34.refs_0_), channel_id=1, source_target_pairs={{1,2},{2,1},{3,4},{4,3},{5,6},{6,5},{7,8},{8,7},{9,10},{10,9},{11,... | collective-permute-start | bytes 491528 | tf_op jit(solution)/shard_map/ppermute | solution.py:332
  21.8 1.3 %collective-permute-start.8 = (f32[32,8,128]{2,1,0:T(8,128)S(1)}, f32[32,8,128]{2,1,0:T(8,128)S(1)}, u32[]{:S(2)}, u32[]{:S(2)}) collective-permute-start(f32[32,8,128]{2,1,0:T(8,128)S(1)} %get-tuple-element.36), channel_id=1, source_target_pairs={{0,1},{1,0},{2,3},{3,2},{4,5},{5,4},{6,7},{7,6},{8,9},{9,8},{10,11... | collective-permute-start | bytes 393224 | tf_op jit(solution)/shard_map/ppermute | solution.py:333
  23.1 0.0 collective-permute-start.9
  23.1 0.4 %collective-permute-start.10 = (f32[24,8,128]{2,1,0:T(8,128)S(1)}, f32[24,8,128]{2,1,0:T(8,128)S(1)}, u32[]{:S(2)}, u32[]{:S(2)}) collective-permute-start(f32[24,8,128]{2,1,0:T(8,128)S(1)} %get-tuple-element.35.refs_1_), channel_id=1, source_target_pairs={{1,2},{2,1},{3,4},{4,3},{5,6},{6,5},{7,8},{8,7},{9,10},{10,9},{11,... | collective-permute-start | bytes 294920 | tf_op jit(solution)/shard_map/ppermute | solution.py:332
  23.5 0.6 %collective-permute-done.8.refs_2_ = f32[32,8,128]{2,1,0:T(8,128)S(1)} collective-permute-done((f32[32,8,128]{2,1,0:T(8,128)S(1)}, f32[32,8,128]{2,1,0:T(8,128)S(1)}, u32[]{:S(2)}, u32[]{:S(2)}) %collective-permute-start.8) | collective-permute-done | bytes 131104 | tf_op jit(solution)/shard_map/ppermute | solution.py:333
  24.1 0.4 %collective-permute-done.9.refs_3_ = f32[32,8,128]{2,1,0:T(8,128)S(1)} collective-permute-done((f32[32,8,128]{2,1,0:T(8,128)S(1)}, f32[32,8,128]{2,1,0:T(8,128)S(1)}, u32[]{:S(2)}, u32[]{:S(2)}) %collective-permute-start.9) | collective-permute-done | bytes 131104 | tf_op jit(solution)/shard_map/ppermute | solution.py:333
  24.4 0.0 copy-done.1
  24.4 0.0 copy-done
  24.4 2.2 %stack_near.1 = (f32[16,2,4,8,128]{4,3,2,1,0:T(8,128)S(1)}, s32[96]{0:T(128)S(4)}, s32[64]{0:T(128)S(4)}, s32[3]{0:T(128)S(4)}) custom-call(s32[8,16]{1,0:T(8,128)S(1)} %copy-done, s32[8,16]{1,0:T(8,128)S(1)} %copy-done.1, s32[1]{0:T(128)} %bitcast.refs_4_.me_ref, f32[40,8,128]{2,1,0:T(8,128)S(1)} %get-tuple-element.34.refs_0_, ...), custom_call_target="tpu_custom_call" | custom-call | tf_op jit(solution)/shard_map/stack_near/pallas_call | solution.py:336
  26.7 0.2 collective-permute-done.11.far_ref
  26.8 0.5 %stack_far.2.given_ref = f32[16,2,4,8,128]{4,3,2,1,0:T(8,128)S(1)} custom-call(s32[96]{0:T(128)S(4)} %get-tuple-element.40.list_ref, s32[3]{0:T(128)S(4)} %get-tuple-element.39.count_ref, f32[40,8,128]{2,1,0:T(8,128)S(1)} %collective-permute-done.11.far_ref, f32[16,2,4,8,128]{4,3,2,1,0:T(8,128)S(1)} %get-tuple-element.41.given_ref), custom_call_target="tpu_custom_call", output_to_operand_aliasing={{}: (3, {})} | custom-call | tf_op jit(solution)/shard_map/stack_far/pallas_call | solution.py:349
  27.3 0.6 %collective-permute-done.10.far_ref = f32[24,8,128]{2,1,0:T(8,128)S(1)} collective-permute-done((f32[24,8,128]{2,1,0:T(8,128)S(1)}, f32[24,8,128]{2,1,0:T(8,128)S(1)}, u32[]{:S(2)}, u32[]{:S(2)}) %collective-permute-start.10) | collective-permute-done | bytes 98336 | tf_op jit(solution)/shard_map/ppermute | solution.py:332
  27.9 1.1 %stack_far.3 = (f32[16,2,4,8,128]{4,3,2,1,0:T(8,128)S(1)}, f32[8,512]{1,0:T(8,128)}) custom-call(s32[64]{0:T(128)S(4)} %get-tuple-element.38.list_ref, s32[3]{0:T(128)S(4)} %get-tuple-element.39.count_ref, f32[24,8,128]{2,1,0:T(8,128)S(1)} %collective-permute-done.10.far_ref, ...), custom_call_target="tpu_custom_call", output_to_operand_aliasing={{0}: (3, {})} | custom-call | tf_op jit(solution)/shard_map/stack_far/pallas_call | solution.py:349
  (1 shorter events, 0.0 us)
Async XLA Ops:
  1.5 9.9 %collective-permute-start = (f32[129,1,128]{2,1,0:T(1,128)S(1)}, f32[129,1,128]{2,1,0:T(1,128)S(1)}, u32[]{:S(2)}, u32[]{:S(2)}) collective-permute-start(f32[129,1,128]{2,1,0:T(1,128)S(1)} %get-tuple-element.25), channel_id=1, source_target_pairs={{0,8},{1,9},{2,10},{3,11},{4,12},{5,13},{6,14},{7,15},{8,0},{9,1},... | collective-permute-start | bytes 198152 | tf_op jit(solution)/shard_map/ppermute | solution.py:288
  4.7 8.4 %collective-permute-start.1 = (f32[129,1,128]{2,1,0:T(1,128)S(1)}, f32[129,1,128]{2,1,0:T(1,128)S(1)}, u32[]{:S(2)}, u32[]{:S(2)}) collective-permute-start(f32[129,1,128]{2,1,0:T(1,128)S(1)} %get-tuple-element.26), channel_id=1, source_target_pairs={{0,10},{1,11},{2,8},{3,9},{4,14},{5,15},{6,12},{7,13},{8,2},{9,3},... | collective-permute-start | bytes 198152 | tf_op jit(solution)/shard_map/ppermute | solution.py:288
  5.8 8.9 %collective-permute-start.2 = (f32[129,1,128]{2,1,0:T(1,128)S(1)}, f32[129,1,128]{2,1,0:T(1,128)S(1)}, u32[]{:S(2)}, u32[]{:S(2)}) collective-permute-start(f32[129,1,128]{2,1,0:T(1,128)S(1)} %get-tuple-element.27), channel_id=1, source_target_pairs={{0,4},{1,5},{2,6},{3,7},{4,0},{5,1},{6,2},{7,3},{8,12},{9,13},{10,... | collective-permute-start | bytes 198152 | tf_op jit(solution)/shard_map/ppermute | solution.py:288
  7.1 7.6 %collective-permute-start.3 = (f32[129,1,128]{2,1,0:T(1,128)S(1)}, f32[129,1,128]{2,1,0:T(1,128)S(1)}, u32[]{:S(2)}, u32[]{:S(2)}) collective-permute-start(f32[129,1,128]{2,1,0:T(1,128)S(1)} %get-tuple-element.28), channel_id=1, source_target_pairs={{0,6},{1,7},{2,4},{3,5},{4,2},{5,3},{6,0},{7,1},{8,14},{9,15},{10,... | collective-permute-start | bytes 198152 | tf_op jit(solution)/shard_map/ppermute | solution.py:288
  7.2 7.5 %collective-permute-start.4 = (f32[129,1,128]{2,1,0:T(1,128)S(1)}, f32[129,1,128]{2,1,0:T(1,128)S(1)}, u32[]{:S(2)}, u32[]{:S(2)}) collective-permute-start(f32[129,1,128]{2,1,0:T(1,128)S(1)} %get-tuple-element.29), channel_id=1, source_target_pairs={{0,14},{1,15},{2,12},{3,13},{4,10},{5,11},{6,8},{7,9},{8,6},{9,7},... | collective-permute-start | bytes 198152 | tf_op jit(solution)/shard_map/ppermute | solution.py:288
  11.4 5.0 %collective-permute-start.5 = (f32[129,1,128]{2,1,0:T(1,128)S(1)}, f32[129,1,128]{2,1,0:T(1,128)S(1)}, u32[]{:S(2)}, u32[]{:S(2)}) collective-permute-start(f32[129,1,128]{2,1,0:T(1,128)S(1)} %get-tuple-element.30), channel_id=1, source_target_pairs={{0,12},{1,13},{2,14},{3,15},{4,8},{5,9},{6,10},{7,11},{8,4},{9,5},... | collective-permute-start | bytes 198152 | tf_op jit(solution)/shard_map/ppermute | solution.py:288
  13.1 3.5 %collective-permute-start.6 = (f32[129,1,128]{2,1,0:T(1,128)S(1)}, f32[129,1,128]{2,1,0:T(1,128)S(1)}, u32[]{:S(2)}, u32[]{:S(2)}) collective-permute-start(f32[129,1,128]{2,1,0:T(1,128)S(1)} %get-tuple-element.31), channel_id=1, source_target_pairs={{0,2},{1,3},{2,0},{3,1},{4,6},{5,7},{6,4},{7,5},{8,10},{9,11},{10,... | collective-permute-start | bytes 198152 | tf_op jit(solution)/shard_map/ppermute | solution.py:288
  16.9 4.2 %collective-permute-start.7 = (f32[64,8,128]{2,1,0:T(8,128)S(1)}, f32[64,8,128]{2,1,0:T(8,128)S(1)}, u32[]{:S(2)}, u32[]{:S(2)}) collective-permute-start(f32[64,8,128]{2,1,0:T(8,128)S(1)} %get-tuple-element.33), channel_id=1, source_target_pairs={{0,1},{1,0},{2,3},{3,2},{4,5},{5,4},{6,7},{7,6},{8,9},{9,8},{10,11... | collective-permute-start | bytes 786440 | tf_op jit(solution)/shard_map/ppermute | solution.py:312
  21.1 3.3 %copy-start.1 = (s32[8,16]{1,0:T(8,128)S(1)}, s32[8,16]{1,0:T(8,128)}, u32[]{:S(2)}) copy-start(s32[8,16]{1,0:T(8,128)} %col_ref.1) | copy-start | bytes 1540
  21.1 3.3 %copy-start = (s32[8,16]{1,0:T(8,128)S(1)}, s32[8,16]{1,0:T(8,128)}, u32[]{:S(2)}) copy-start(s32[8,16]{1,0:T(8,128)} %row_ref.1) | copy-start | bytes 1540
  21.2 5.7 %collective-permute-start.11 = (f32[40,8,128]{2,1,0:T(8,128)S(1)}, f32[40,8,128]{2,1,0:T(8,128)S(1)}, u32[]{:S(2)}, u32[]{:S(2)}) collective-permute-start(f32[40,8,128]{2,1,0:T(8,128)S(1)} %get-tuple-element.34.refs_0_), channel_id=1, source_target_pairs={{1,2},{2,1},{3,4},{4,3},{5,6},{6,5},{7,8},{8,7},{9,10},{10,9},{11,... | collective-permute-start | bytes 491528 | tf_op jit(solution)/shard_map/ppermute | solution.py:332
  21.8 2.3 %collective-permute-start.8 = (f32[32,8,128]{2,1,0:T(8,128)S(1)}, f32[32,8,128]{2,1,0:T(8,128)S(1)}, u32[]{:S(2)}, u32[]{:S(2)}) collective-permute-start(f32[32,8,128]{2,1,0:T(8,128)S(1)} %get-tuple-element.36), channel_id=1, source_target_pairs={{0,1},{1,0},{2,3},{3,2},{4,5},{5,4},{6,7},{7,6},{8,9},{9,8},{10,11... | collective-permute-start | bytes 393224 | tf_op jit(solution)/shard_map/ppermute | solution.py:333
  23.1 1.3 %collective-permute-start.9 = (f32[32,8,128]{2,1,0:T(8,128)S(1)}, f32[32,8,128]{2,1,0:T(8,128)S(1)}, u32[]{:S(2)}, u32[]{:S(2)}) collective-permute-start(f32[32,8,128]{2,1,0:T(8,128)S(1)} %get-tuple-element.37), channel_id=1, source_target_pairs={{0,1},{1,0},{2,3},{3,2},{4,5},{5,4},{6,7},{7,6},{8,9},{9,8},{10,11... | collective-permute-start | bytes 393224 | tf_op jit(solution)/shard_map/ppermute | solution.py:333
  23.1 4.8 %collective-permute-start.10 = (f32[24,8,128]{2,1,0:T(8,128)S(1)}, f32[24,8,128]{2,1,0:T(8,128)S(1)}, u32[]{:S(2)}, u32[]{:S(2)}) collective-permute-start(f32[24,8,128]{2,1,0:T(8,128)S(1)} %get-tuple-element.35.refs_1_), channel_id=1, source_target_pairs={{1,2},{2,1},{3,4},{4,3},{5,6},{6,5},{7,8},{8,7},{9,10},{10,9},{11,... | collective-permute-start | bytes 294920 | tf_op jit(solution)/shard_map/ppermute | solution.py:332

commit v9 on v8

--- a/solution.py
+++ b/solution.py
@@ -12,8 +12,8 @@
 LANES = 128
 GROUP = 16
 PARTS = 2
-ORDER = (4, 5, 2, 3, 7, 6, 1)
-PIECES = 2
+EARLY = 6
+ORDER = (4, 2, 5, 3, 7, 6, 1)
 VMEM = pl.BlockSpec(memory_space=pltpu.VMEM)
 SMEM = pl.BlockSpec(memory_space=pltpu.SMEM)
 LIMIT = pltpu.CompilerParams(vmem_limit_bytes=32 * 1024 * 1024)
@@ -90,11 +90,11 @@
         first += count
 
 
-def sum_kernel(capacity, cells, *refs):
-    in_refs, sky_refs = refs[:-2], refs[-2:]
+def sum_kernel(capacity, cells, first_call, *refs):
+    in_refs, sky_refs = refs[: -2 if first_call else -4], refs[-2:]
     rows, width = sky_refs[0].shape[1:]
     stride = 4 * capacity * rows + 1
-    for sky_ref in sky_refs:
+    for sky_ref in sky_refs if first_call else ():
         for index in range(sky_ref.shape[0]):
             sky_ref[index] = jnp.zeros((rows, width), jnp.float32)
     for in_ref in in_refs:
@@ -122,12 +122,10 @@
 
 
 def join_kernel(mine_ref, other_ref, *part_refs):
-    total = mine_ref.shape[0]
     first = 0
     for part_ref in part_refs:
         for index in range(part_ref.shape[0]):
-            place = (first + index) % total
-            part_ref[index] = mine_ref[place] + other_ref[place]
+            part_ref[index] = mine_ref[first + index] + other_ref[first + index]
         first += part_ref.shape[0]
 
 
@@ -163,9 +161,9 @@
         index -= ref.shape[0]
 
 
-def near_kernel(tiles, group, split, pieces, row_ref, col_ref, me_ref, *refs):
-    own_refs, twin_refs = refs[:PARTS], refs[PARTS : PARTS + pieces]
-    sums_ref, *list_refs, count_ref, wide_ref = refs[PARTS + pieces :]
+def near_kernel(tiles, group, split, row_ref, col_ref, me_ref, *refs):
+    own_refs, twin_refs = refs[:PARTS], refs[PARTS : PARTS + 2]
+    sums_ref, *list_refs, count_ref, wide_ref = refs[PARTS + 2 :]
     epochs, vels = row_ref.shape
     cells, rows = sums_ref.shape[2:4]
     odd = me_ref[0] & 1
@@ -179,7 +177,7 @@
                 index = (epoch * 2 + kind) * cells + cell
                 at = wide_ref.at[epoch, kind, cell + 1]
                 at[rows : 2 * rows, :] = tile_of(own_refs, index)
-                at[pl.ds(twin_row, rows), :] = tile_of(twin_refs, index)
+                at[pl.ds(twin_row, rows), :] = twin_refs[0][index] + twin_refs[1][index]
                 at[pl.ds(far_row, rows), :] = jnp.zeros((rows, LANES), jnp.float32)
 
     def one_velocity(vel, counts):
@@ -301,28 +299,34 @@
         incoming = [incoming.reshape(chips * stride, 1, width)]
     total = epochs * 2 * cells
     sky_shape = jax.ShapeDtypeStruct((total, rows, width), jnp.float32)
-    mine, others = pl.pallas_call(
-        functools.partial(sum_kernel, capacity, cells),
-        out_shape=[sky_shape, sky_shape],
-        in_specs=[VMEM] * len(incoming),
-        out_specs=[VMEM, VMEM],
-        compiler_params=LIMIT,
-        name="sum_slots",
-    )(*incoming)
-    other = lax.ppermute(others, "tile", [(i, i ^ 1) for i in range(tiles)])
+    skies = []
+    for some in (incoming[:EARLY], incoming[EARLY:]):
+        if some:
+            skies = pl.pallas_call(
+                functools.partial(sum_kernel, capacity, cells, not skies),
+                out_shape=[sky_shape, sky_shape],
+                in_specs=[VMEM] * (len(some) + len(skies)),
+                out_specs=[VMEM, VMEM],
+                input_output_aliases={len(some) + i: i for i in range(len(skies))},
+                compiler_params=LIMIT,
+                name="sum_slots",
+            )(*some, *skies)
+    mine, others = skies
+    across = [(i, i ^ 1) for i in range(tiles)]
+    other = lax.ppermute(others, "tile", across)
+    theirs = lax.ppermute(mine, "tile", across)
     split = [epochs - 3 * epochs // 8, 3 * epochs // 8]
-    skies = pl.pallas_call(
+    own = pl.pallas_call(
         join_kernel,
         out_shape=[
             jax.ShapeDtypeStruct((count * 2 * cells, rows, width), jnp.float32)
-            for count in split + [epochs // PIECES] * PIECES
+            for count in split
         ],
         in_specs=[VMEM, VMEM],
-        out_specs=[VMEM] * (PARTS + PIECES),
+        out_specs=[VMEM] * PARTS,
         compiler_params=LIMIT,
         name="join",
     )(mine, other)
-    own, pieces = skies[:PARTS], skies[PARTS:]
     fields = lax.axis_size("field")
     pairs = [(f * tiles + i, f * tiles + i + 1) for f in range(fields) for i in range(1, tiles - 1, 2)]
     pairs += [
@@ -330,20 +334,19 @@
     ]
     both = [way for a, b in pairs for way in ((a, b), (b, a))]
     far = [lax.ppermute(part, ("field", "tile"), both) for part in own]
-    twin = [lax.ppermute(piece, "tile", [(i, i ^ 1) for i in range(tiles)]) for piece in pieces]
     vels = row_offsets.shape[1]
     sums_shape = jax.ShapeDtypeStruct((vels, 2, cells, rows, width), jnp.float32)
     sums, *lists, count = pl.pallas_call(
-        functools.partial(near_kernel, tiles, GROUP, split, PIECES),
+        functools.partial(near_kernel, tiles, GROUP, split),
         out_shape=[sums_shape]
         + [pltpu.SMEM((vels * count + GROUP,), jnp.int32) for count in split]
         + [pltpu.SMEM((PARTS + 1,), jnp.int32)],
-        in_specs=[SMEM] * 3 + [VMEM] * (PARTS + PIECES),
+        in_specs=[SMEM] * 3 + [VMEM] * (PARTS + 2),
         out_specs=[VMEM] + [SMEM] * (PARTS + 1),
         scratch_shapes=[pltpu.VMEM((epochs, 2, cells + 2, 3 * rows, width), jnp.float32)],
         compiler_params=LIMIT,
         name="stack_near",
-    )(row_offsets, col_offsets, me.reshape(1), *own, *twin)
+    )(row_offsets, col_offsets, me.reshape(1), *own, others, theirs)
     for part in range(PARTS):
         last = part == PARTS - 1
         sums, *best = pl.pallas_call(

time: 29.2 us -> 29 us (level)
  starting transfers between devices: 18.5 us -> 16.5 us
  waiting for transfers between devices: 4.83 us -> 6.28 us
  Pallas kernels: 5.64 us -> 5.99 us
    ppermute x7, starting transfers between devices: 13.1 us -> 11.3 us  [body(): lax.ppermute(outgoing[k], 'tile', [(i, i ^ 2 * k) for i in range(tiles)])]
    ppermute x7, waiting for transfers between devices: 1.95 us -> 3.25 us  [body(): lax.ppermute(outgoing[k], 'tile', [(i, i ^ 2 * k) for i in range(tiles)])]
    ppermute x2, waiting for transfers between devices: 0.77 us -> 1.94 us  [body(): far = [lax.ppermute(part, ('field', 'tile'), both) for part in own]]
    ppermute x3 -> x2, waiting for transfers between devices: 2.12 us -> 1.09 us  [the longest x1 1.08 us: body(): other = lax.ppermute(others, 'tile', across)]
    ppermute x3 -> x2, starting transfers between devices: 4.39 us -> 3.36 us  [the longest x1 3.28 us: body(): other = lax.ppermute(others, 'tile', across)]
    ppermute x2, starting transfers between devices: 1 us -> 1.81 us  [body(): far = [lax.ppermute(part, ('field', 'tile'), both) for part in own]]
    pallas_call x2 -> x3, Pallas kernels: 2.5 us -> 2.63 us  [the longest x1 2.2 us: body(): pl.pallas_call(functools.partial(near_kernel, tiles, GROUP, split), out_s...]
  transfers between devices with their start and end apart: 12 -> 11, of which waited for: 7 -> 5; matrix products, arithmetic and copies ran while one was open for 0% -> 0% of each run, Pallas kernels for 9% -> 11%
where the time goes in v9:
time: 29 us; the launch traced here: 28.8 us
  starting transfers between devices  16.5 us (57%)
  waiting for transfers between devices  6.28 us (22%)
  Pallas kernels  5.99 us (21%)
    ppermute x7, starting transfers between devices, body(): lax.ppermute(outgoing[k], 'tile', [(i, i ^ 2 * k) for i in range(tiles)])  11.3 us
    ppermute x1, starting transfers between devices, body(): other = lax.ppermute(others, 'tile', across)  3.28 us
    ppermute x7, waiting for transfers between devices, body(): lax.ppermute(outgoing[k], 'tile', [(i, i ^ 2 * k) for i in range(tiles)])  3.25 us
    pallas_call x1, Pallas kernels, body(): pl.pallas_call(functools.partial(near_kernel, tiles, GROUP, split), out_s...  2.2 us
    ppermute x2, waiting for transfers between devices, body(): far = [lax.ppermute(part, ('field', 'tile'), both) for part in own]  1.94 us
    ppermute x2, starting transfers between devices, body(): far = [lax.ppermute(part, ('field', 'tile'), both) for part in own]  1.81 us
    pallas_call x2, Pallas kernels, body(): pl.pallas_call(functools.partial(far_kernel, part, GROUP), out_shape=[sum...  1.81 us
    pallas_call x1, Pallas kernels, body(): pl.pallas_call(functools.partial(pack_kernel, capacity, outputs), out_sha...  1.51 us
  transfers between devices with their start and end apart: 11, of which 5 were waited for; matrix products, arithmetic and copies ran while one was open for 0% of the time, Pallas kernels for 11%

profile of v9, /device:TPU:1, one launch (start us, length us, event | category | flops | bytes accessed | tf_op | source)
XLA Modules:
  0.0 28.8 jit_solution(10099795782058275370)
XLA Ops:
  0.0 1.5 %pack.1 = (f32[129,1,128]{2,1,0:T(1,128)S(1)}, f32[129,1,128]{2,1,0:T(1,128)S(1)}, f32[129,1,128]{2,1,0:T(1,128)S(1)}, f32[129,1,128]{2,1,0:T(1,128)S(1)}, f32[1...) custom-call(s32[4,1,8]{2,1,0:T(1,128)} %bitcast.4, ...), custom_call_target="tpu_custom_call" | custom-call | tf_op jit(solution)/shard_map/pack/pallas_call | solution.py:263
  1.5 3.2 %collective-permute-start.2 = (f32[129,1,128]{2,1,0:T(1,128)S(1)}, f32[129,1,128]{2,1,0:T(1,128)S(1)}, u32[]{:S(2)}, u32[]{:S(2)}) collective-permute-start(f32[129,1,128]{2,1,0:T(1,128)S(1)} %get-tuple-element.27), channel_id=1, source_target_pairs={{0,8},{1,9},{2,10},{3,11},{4,12},{5,13},{6,14},{7,15},{8,0},{9,1},... | collective-permute-start | bytes 198152 | tf_op jit(solution)/shard_map/ppermute | solution.py:286
  4.7 1.3 %collective-permute-start.3 = (f32[129,1,128]{2,1,0:T(1,128)S(1)}, f32[129,1,128]{2,1,0:T(1,128)S(1)}, u32[]{:S(2)}, u32[]{:S(2)}) collective-permute-start(f32[129,1,128]{2,1,0:T(1,128)S(1)} %get-tuple-element.28), channel_id=1, source_target_pairs={{0,4},{1,5},{2,6},{3,7},{4,0},{5,1},{6,2},{7,3},{8,12},{9,13},{10,... | collective-permute-start | bytes 198152 | tf_op jit(solution)/shard_map/ppermute | solution.py:286
  6.0 1.0 %collective-permute-start.4 = (f32[129,1,128]{2,1,0:T(1,128)S(1)}, f32[129,1,128]{2,1,0:T(1,128)S(1)}, u32[]{:S(2)}, u32[]{:S(2)}) collective-permute-start(f32[129,1,128]{2,1,0:T(1,128)S(1)} %get-tuple-element.29), channel_id=1, source_target_pairs={{0,10},{1,11},{2,8},{3,9},{4,14},{5,15},{6,12},{7,13},{8,2},{9,3},... | collective-permute-start | bytes 198152 | tf_op jit(solution)/shard_map/ppermute | solution.py:286
  7.1 0.1 collective-permute-start.5
  7.2 4.3 %collective-permute-start.6 = (f32[129,1,128]{2,1,0:T(1,128)S(1)}, f32[129,1,128]{2,1,0:T(1,128)S(1)}, u32[]{:S(2)}, u32[]{:S(2)}) collective-permute-start(f32[129,1,128]{2,1,0:T(1,128)S(1)} %get-tuple-element.31), channel_id=1, source_target_pairs={{0,14},{1,15},{2,12},{3,13},{4,10},{5,11},{6,8},{7,9},{8,6},{9,7},... | collective-permute-start | bytes 198152 | tf_op jit(solution)/shard_map/ppermute | solution.py:286
  11.4 0.0 collective-permute-done.2.refs_1_
  11.4 0.2 collective-permute-start
  11.6 0.0 collective-permute-done.3.refs_2_
  11.6 1.2 %collective-permute-start.1 = (f32[129,1,128]{2,1,0:T(1,128)S(1)}, f32[129,1,128]{2,1,0:T(1,128)S(1)}, u32[]{:S(2)}, u32[]{:S(2)}) collective-permute-start(f32[129,1,128]{2,1,0:T(1,128)S(1)} %get-tuple-element.25), channel_id=1, source_target_pairs={{0,2},{1,3},{2,0},{3,1},{4,6},{5,7},{6,4},{7,5},{8,10},{9,11},{10,... | collective-permute-start | bytes 198152 | tf_op jit(solution)/shard_map/ppermute | solution.py:286
  12.8 0.0 collective-permute-done.4.refs_3_
  12.8 0.0 collective-permute-done.5.refs_4_
  12.8 1.2 %collective-permute-done.6.refs_5_ = f32[129,1,128]{2,1,0:T(1,128)S(1)} collective-permute-done((f32[129,1,128]{2,1,0:T(1,128)S(1)}, f32[129,1,128]{2,1,0:T(1,128)S(1)}, u32[]{:S(2)}, u32[]{:S(2)}) %collective-permute-start.6) | collective-permute-done | bytes 66080 | tf_op jit(solution)/shard_map/ppermute | solution.py:286
  14.1 0.3 sum_slots.2
  14.3 2.0 %collective-permute-done.refs_0_ = f32[129,1,128]{2,1,0:T(1,128)S(1)} collective-permute-done((f32[129,1,128]{2,1,0:T(1,128)S(1)}, f32[129,1,128]{2,1,0:T(1,128)S(1)}, u32[]{:S(2)}, u32[]{:S(2)}) %collective-permute-start) | collective-permute-done | bytes 66080 | tf_op jit(solution)/shard_map/ppermute | solution.py:286
  16.4 0.0 collective-permute-done.1.refs_1_
  16.4 0.2 sum_slots.3
  16.5 3.3 %collective-permute-start.7 = (f32[64,8,128]{2,1,0:T(8,128)S(1)}, f32[64,8,128]{2,1,0:T(8,128)S(1)}, u32[]{:S(2)}, u32[]{:S(2)}) collective-permute-start(f32[64,8,128]{2,1,0:T(8,128)S(1)} %get-tuple-element.35.refs_2_), channel_id=1, source_target_pairs={{0,1},{1,0},{2,3},{3,2},{4,5},{5,4},{6,7},{7,6},{8,9},{9,8},{10,11... | collective-permute-start | bytes 786440 | tf_op jit(solution)/shard_map/ppermute | solution.py:316
  19.8 0.1 collective-permute-start.8
  19.9 1.1 %collective-permute-done.7.other_ref = f32[64,8,128]{2,1,0:T(8,128)S(1)} collective-permute-done((f32[64,8,128]{2,1,0:T(8,128)S(1)}, f32[64,8,128]{2,1,0:T(8,128)S(1)}, u32[]{:S(2)}, u32[]{:S(2)}) %collective-permute-start.7) | collective-permute-done | bytes 262176 | tf_op jit(solution)/shard_map/ppermute | solution.py:316
  21.0 0.0 copy-start
  21.0 0.0 copy-start.1
  21.0 0.5 %collective-permute-start.10 = (f32[40,8,128]{2,1,0:T(8,128)S(1)}, f32[40,8,128]{2,1,0:T(8,128)S(1)}, u32[]{:S(2)}, u32[]{:S(2)}) collective-permute-start(f32[40,8,128]{2,1,0:T(8,128)S(1)} %get-tuple-element.36.refs_0_), channel_id=1, source_target_pairs={{1,2},{2,1},{3,4},{4,3},{5,6},{6,5},{7,8},{8,7},{9,10},{10,9},{11,... | collective-permute-start | bytes 491528 | tf_op jit(solution)/shard_map/ppermute | solution.py:336
  21.6 1.3 %collective-permute-start.9 = (f32[24,8,128]{2,1,0:T(8,128)S(1)}, f32[24,8,128]{2,1,0:T(8,128)S(1)}, u32[]{:S(2)}, u32[]{:S(2)}) collective-permute-start(f32[24,8,128]{2,1,0:T(8,128)S(1)} %get-tuple-element.37.refs_1_), channel_id=1, source_target_pairs={{1,2},{2,1},{3,4},{4,3},{5,6},{6,5},{7,8},{8,7},{9,10},{10,9},{11,... | collective-permute-start | bytes 294920 | tf_op jit(solution)/shard_map/ppermute | solution.py:336
  22.8 0.0 collective-permute-done.8.refs_3_
  22.8 0.0 copy-done
  22.8 0.0 copy-done.1
  22.8 2.2 %stack_near.1 = (f32[16,2,4,8,128]{4,3,2,1,0:T(8,128)S(1)}, s32[96]{0:T(128)S(4)}, s32[64]{0:T(128)S(4)}, s32[3]{0:T(128)S(4)}) custom-call(s32[8,16]{1,0:T(8,128)S(1)} %copy-done, s32[8,16]{1,0:T(8,128)S(1)} %copy-done.1, s32[1]{0:T(128)} %bitcast.refs_4_.me_ref, f32[40,8,128]{2,1,0:T(8,128)S(1)} %get-tuple-element.36.refs_0_, ...), custom_call_target="tpu_custom_call" | custom-call | tf_op jit(solution)/shard_map/stack_near/pallas_call | solution.py:339
  25.0 1.6 %collective-permute-done.10.far_ref = f32[40,8,128]{2,1,0:T(8,128)S(1)} collective-permute-done((f32[40,8,128]{2,1,0:T(8,128)S(1)}, f32[40,8,128]{2,1,0:T(8,128)S(1)}, u32[]{:S(2)}, u32[]{:S(2)}) %collective-permute-start.10) | collective-permute-done | bytes 163872 | tf_op jit(solution)/shard_map/ppermute | solution.py:336
  26.6 0.7 %stack_far.2.given_ref = f32[16,2,4,8,128]{4,3,2,1,0:T(8,128)S(1)} custom-call(s32[96]{0:T(128)S(4)} %get-tuple-element.40.list_ref, s32[3]{0:T(128)S(4)} %get-tuple-element.39.count_ref, f32[40,8,128]{2,1,0:T(8,128)S(1)} %collective-permute-done.10.far_ref, f32[16,2,4,8,128]{4,3,2,1,0:T(8,128)S(1)} %get-tuple-element.41.given_ref), custom_call_target="tpu_custom_call", output_to_operand_aliasing={{}: (3, {})} | custom-call | tf_op jit(solution)/shard_map/stack_far/pallas_call | solution.py:352
  27.3 0.4 %collective-permute-done.9.far_ref = f32[24,8,128]{2,1,0:T(8,128)S(1)} collective-permute-done((f32[24,8,128]{2,1,0:T(8,128)S(1)}, f32[24,8,128]{2,1,0:T(8,128)S(1)}, u32[]{:S(2)}, u32[]{:S(2)}) %collective-permute-start.9) | collective-permute-done | bytes 98336 | tf_op jit(solution)/shard_map/ppermute | solution.py:336
  27.7 1.1 %stack_far.3 = (f32[16,2,4,8,128]{4,3,2,1,0:T(8,128)S(1)}, f32[8,512]{1,0:T(8,128)}) custom-call(s32[64]{0:T(128)S(4)} %get-tuple-element.38.list_ref, s32[3]{0:T(128)S(4)} %get-tuple-element.39.count_ref, f32[24,8,128]{2,1,0:T(8,128)S(1)} %collective-permute-done.9.far_ref, ...), custom_call_target="tpu_custom_call", output_to_operand_aliasing={{0}: (3, {})} | custom-call | tf_op jit(solution)/shard_map/stack_far/pallas_call | solution.py:352
  (1 shorter events, 0.0 us)
Async XLA Ops:
  1.5 9.9 %collective-permute-start.2 = (f32[129,1,128]{2,1,0:T(1,128)S(1)}, f32[129,1,128]{2,1,0:T(1,128)S(1)}, u32[]{:S(2)}, u32[]{:S(2)}) collective-permute-start(f32[129,1,128]{2,1,0:T(1,128)S(1)} %get-tuple-element.27), channel_id=1, source_target_pairs={{0,8},{1,9},{2,10},{3,11},{4,12},{5,13},{6,14},{7,15},{8,0},{9,1},... | collective-permute-start | bytes 198152 | tf_op jit(solution)/shard_map/ppermute | solution.py:286
  4.7 6.9 %collective-permute-start.3 = (f32[129,1,128]{2,1,0:T(1,128)S(1)}, f32[129,1,128]{2,1,0:T(1,128)S(1)}, u32[]{:S(2)}, u32[]{:S(2)}) collective-permute-start(f32[129,1,128]{2,1,0:T(1,128)S(1)} %get-tuple-element.28), channel_id=1, source_target_pairs={{0,4},{1,5},{2,6},{3,7},{4,0},{5,1},{6,2},{7,3},{8,12},{9,13},{10,... | collective-permute-start | bytes 198152 | tf_op jit(solution)/shard_map/ppermute | solution.py:286
  6.0 6.8 %collective-permute-start.4 = (f32[129,1,128]{2,1,0:T(1,128)S(1)}, f32[129,1,128]{2,1,0:T(1,128)S(1)}, u32[]{:S(2)}, u32[]{:S(2)}) collective-permute-start(f32[129,1,128]{2,1,0:T(1,128)S(1)} %get-tuple-element.29), channel_id=1, source_target_pairs={{0,10},{1,11},{2,8},{3,9},{4,14},{5,15},{6,12},{7,13},{8,2},{9,3},... | collective-permute-start | bytes 198152 | tf_op jit(solution)/shard_map/ppermute | solution.py:286
  7.1 5.8 %collective-permute-start.5 = (f32[129,1,128]{2,1,0:T(1,128)S(1)}, f32[129,1,128]{2,1,0:T(1,128)S(1)}, u32[]{:S(2)}, u32[]{:S(2)}) collective-permute-start(f32[129,1,128]{2,1,0:T(1,128)S(1)} %get-tuple-element.30), channel_id=1, source_target_pairs={{0,6},{1,7},{2,4},{3,5},{4,2},{5,3},{6,0},{7,1},{8,14},{9,15},{10,... | collective-permute-start | bytes 198152 | tf_op jit(solution)/shard_map/ppermute | solution.py:286
  7.2 6.9 %collective-permute-start.6 = (f32[129,1,128]{2,1,0:T(1,128)S(1)}, f32[129,1,128]{2,1,0:T(1,128)S(1)}, u32[]{:S(2)}, u32[]{:S(2)}) collective-permute-start(f32[129,1,128]{2,1,0:T(1,128)S(1)} %get-tuple-element.31), channel_id=1, source_target_pairs={{0,14},{1,15},{2,12},{3,13},{4,10},{5,11},{6,8},{7,9},{8,6},{9,7},... | collective-permute-start | bytes 198152 | tf_op jit(solution)/shard_map/ppermute | solution.py:286
  11.4 4.9 %collective-permute-start = (f32[129,1,128]{2,1,0:T(1,128)S(1)}, f32[129,1,128]{2,1,0:T(1,128)S(1)}, u32[]{:S(2)}, u32[]{:S(2)}) collective-permute-start(f32[129,1,128]{2,1,0:T(1,128)S(1)} %get-tuple-element.24), channel_id=1, source_target_pairs={{0,12},{1,13},{2,14},{3,15},{4,8},{5,9},{6,10},{7,11},{8,4},{9,5},... | collective-permute-start | bytes 198152 | tf_op jit(solution)/shard_map/ppermute | solution.py:286
  11.6 4.8 %collective-permute-start.1 = (f32[129,1,128]{2,1,0:T(1,128)S(1)}, f32[129,1,128]{2,1,0:T(1,128)S(1)}, u32[]{:S(2)}, u32[]{:S(2)}) collective-permute-start(f32[129,1,128]{2,1,0:T(1,128)S(1)} %get-tuple-element.25), channel_id=1, source_target_pairs={{0,2},{1,3},{2,0},{3,1},{4,6},{5,7},{6,4},{7,5},{8,10},{9,11},{10,... | collective-permute-start | bytes 198152 | tf_op jit(solution)/shard_map/ppermute | solution.py:286
  16.5 4.4 %collective-permute-start.7 = (f32[64,8,128]{2,1,0:T(8,128)S(1)}, f32[64,8,128]{2,1,0:T(8,128)S(1)}, u32[]{:S(2)}, u32[]{:S(2)}) collective-permute-start(f32[64,8,128]{2,1,0:T(8,128)S(1)} %get-tuple-element.35.refs_2_), channel_id=1, source_target_pairs={{0,1},{1,0},{2,3},{3,2},{4,5},{5,4},{6,7},{7,6},{8,9},{9,8},{10,11... | collective-permute-start | bytes 786440 | tf_op jit(solution)/shard_map/ppermute | solution.py:316
  19.8 3.0 %collective-permute-start.8 = (f32[64,8,128]{2,1,0:T(8,128)S(1)}, f32[64,8,128]{2,1,0:T(8,128)S(1)}, u32[]{:S(2)}, u32[]{:S(2)}) collective-permute-start(f32[64,8,128]{2,1,0:T(8,128)S(1)} %get-tuple-element.34.mine_ref), channel_id=1, source_target_pairs={{0,1},{1,0},{2,3},{3,2},{4,5},{5,4},{6,7},{7,6},{8,9},{9,8},{10,11... | collective-permute-start | bytes 786440 | tf_op jit(solution)/shard_map/ppermute | solution.py:317
  21.0 1.9 %copy-start = (s32[8,16]{1,0:T(8,128)S(1)}, s32[8,16]{1,0:T(8,128)}, u32[]{:S(2)}) copy-start(s32[8,16]{1,0:T(8,128)} %row_ref.1) | copy-start | bytes 1540
  21.0 1.9 %copy-start.1 = (s32[8,16]{1,0:T(8,128)S(1)}, s32[8,16]{1,0:T(8,128)}, u32[]{:S(2)}) copy-start(s32[8,16]{1,0:T(8,128)} %col_ref.1) | copy-start | bytes 1540
  21.0 5.6 %collective-permute-start.10 = (f32[40,8,128]{2,1,0:T(8,128)S(1)}, f32[40,8,128]{2,1,0:T(8,128)S(1)}, u32[]{:S(2)}, u32[]{:S(2)}) collective-permute-start(f32[40,8,128]{2,1,0:T(8,128)S(1)} %get-tuple-element.36.refs_0_), channel_id=1, source_target_pairs={{1,2},{2,1},{3,4},{4,3},{5,6},{6,5},{7,8},{8,7},{9,10},{10,9},{11,... | collective-permute-start | bytes 491528 | tf_op jit(solution)/shard_map/ppermute | solution.py:336
  21.6 6.1 %collective-permute-start.9 = (f32[24,8,128]{2,1,0:T(8,128)S(1)}, f32[24,8,128]{2,1,0:T(8,128)S(1)}, u32[]{:S(2)}, u32[]{:S(2)}) collective-permute-start(f32[24,8,128]{2,1,0:T(8,128)S(1)} %get-tuple-element.37.refs_1_), channel_id=1, source_target_pairs={{1,2},{2,1},{3,4},{4,3},{5,6},{6,5},{7,8},{8,7},{9,10},{10,9},{11,... | collective-permute-start | bytes 294920 | tf_op jit(solution)/shard_map/ppermute | solution.py:336

commit v10 on v9

--- a/solution.py
+++ b/solution.py
@@ -11,7 +11,7 @@
 RREACH = 8
 LANES = 128
 GROUP = 16
-PARTS = 2
+PARTS = 3
 EARLY = 6
 ORDER = (4, 2, 5, 3, 7, 6, 1)
 VMEM = pl.BlockSpec(memory_space=pltpu.VMEM)
@@ -190,8 +190,8 @@
             for kind in range(2):
                 for cell in range(cells):
                     sums[kind][cell] = sums[kind][cell] + windows[kind][cell]
-            part = int(epoch >= split[0])
-            place = epoch - part * split[0]
+            part = sum(epoch >= sum(split[: index + 1]) for index in range(PARTS - 1))
+            place = epoch - sum(split[:part])
             start_row = row + (1 - odd) * rows
             code = (vel << 24) | (place << 16) | (start_row << 10) | start_col
             list_refs[part][counts[part]] = code
@@ -315,7 +315,7 @@
     across = [(i, i ^ 1) for i in range(tiles)]
     other = lax.ppermute(others, "tile", across)
     theirs = lax.ppermute(mine, "tile", across)
-    split = [epochs - 3 * epochs // 8, 3 * epochs // 8]
+    split = [epochs - epochs // 4 - epochs // 8, epochs // 4, epochs // 8]
     own = pl.pallas_call(
         join_kernel,
         out_shape=[

time: 29 us -> 28.7 us (0.990)
  waiting for transfers between devices: 6.28 us -> 5.57 us
  starting transfers between devices: 16.5 us -> 17 us
    ppermute x2 -> x3, waiting for transfers between devices: 1.94 us -> 1.22 us  [body(): far = [lax.ppermute(part, ('field', 'tile'), both) for part in own]]
    ppermute x2 -> x3, starting transfers between devices: 1.81 us -> 2.3 us  [body(): far = [lax.ppermute(part, ('field', 'tile'), both) for part in own]]
    pallas_call x2 -> x3, Pallas kernels: 1.81 us -> 1.81 us  [body(): pl.pallas_call(functools.partial(far_kernel, part, GROUP), out_shape=[sum...]
  transfers between devices with their start and end apart: 11 -> 12, of which waited for: 5 -> 5; matrix products, arithmetic and copies ran while one was open for 0% -> 0% of each run, Pallas kernels for 11% -> 12%
where the time goes in v10:
time: 28.7 us; the launch traced here: 28.6 us
  starting transfers between devices  17 us (59%)
  Pallas kernels  5.96 us (21%)
  waiting for transfers between devices  5.57 us (19%)
    ppermute x7, starting transfers between devices, body(): lax.ppermute(outgoing[k], 'tile', [(i, i ^ 2 * k) for i in range(tiles)])  11.3 us
    ppermute x1, starting transfers between devices, body(): other = lax.ppermute(others, 'tile', across)  3.28 us
    ppermute x7, waiting for transfers between devices, body(): lax.ppermute(outgoing[k], 'tile', [(i, i ^ 2 * k) for i in range(tiles)])  3.26 us
    ppermute x3, starting transfers between devices, body(): far = [lax.ppermute(part, ('field', 'tile'), both) for part in own]  2.3 us
    pallas_call x1, Pallas kernels, body(): pl.pallas_call(functools.partial(near_kernel, tiles, GROUP, split), out_s...  2.19 us
    pallas_call x3, Pallas kernels, body(): pl.pallas_call(functools.partial(far_kernel, part, GROUP), out_shape=[sum...  1.81 us
    pallas_call x1, Pallas kernels, body(): pl.pallas_call(functools.partial(pack_kernel, capacity, outputs), out_sha...  1.51 us
    ppermute x3, waiting for transfers between devices, body(): far = [lax.ppermute(part, ('field', 'tile'), both) for part in own]  1.22 us
  transfers between devices with their start and end apart: 12, of which 5 were waited for; matrix products, arithmetic and copies ran while one was open for 0% of the time, Pallas kernels for 12%

profile of v10, /device:TPU:1, one launch (start us, length us, event | category | flops | bytes accessed | tf_op | source)
XLA Modules:
  0.0 28.6 jit_solution(13865996302877013967)
XLA Ops:
  0.0 1.5 %pack.1 = (f32[129,1,128]{2,1,0:T(1,128)S(1)}, f32[129,1,128]{2,1,0:T(1,128)S(1)}, f32[129,1,128]{2,1,0:T(1,128)S(1)}, f32[129,1,128]{2,1,0:T(1,128)S(1)}, f32[1...) custom-call(s32[4,1,8]{2,1,0:T(1,128)} %bitcast.4, ...), custom_call_target="tpu_custom_call" | custom-call | tf_op jit(solution)/shard_map/pack/pallas_call | solution.py:263
  1.5 3.2 %collective-permute-start.2 = (f32[129,1,128]{2,1,0:T(1,128)S(1)}, f32[129,1,128]{2,1,0:T(1,128)S(1)}, u32[]{:S(2)}, u32[]{:S(2)}) collective-permute-start(f32[129,1,128]{2,1,0:T(1,128)S(1)} %get-tuple-element.29), channel_id=1, source_target_pairs={{0,8},{1,9},{2,10},{3,11},{4,12},{5,13},{6,14},{7,15},{8,0},{9,1},... | collective-permute-start | bytes 198152 | tf_op jit(solution)/shard_map/ppermute | solution.py:286
  4.7 1.3 %collective-permute-start.3 = (f32[129,1,128]{2,1,0:T(1,128)S(1)}, f32[129,1,128]{2,1,0:T(1,128)S(1)}, u32[]{:S(2)}, u32[]{:S(2)}) collective-permute-start(f32[129,1,128]{2,1,0:T(1,128)S(1)} %get-tuple-element.30), channel_id=1, source_target_pairs={{0,4},{1,5},{2,6},{3,7},{4,0},{5,1},{6,2},{7,3},{8,12},{9,13},{10,... | collective-permute-start | bytes 198152 | tf_op jit(solution)/shard_map/ppermute | solution.py:286
  6.0 1.0 %collective-permute-start.4 = (f32[129,1,128]{2,1,0:T(1,128)S(1)}, f32[129,1,128]{2,1,0:T(1,128)S(1)}, u32[]{:S(2)}, u32[]{:S(2)}) collective-permute-start(f32[129,1,128]{2,1,0:T(1,128)S(1)} %get-tuple-element.31), channel_id=1, source_target_pairs={{0,10},{1,11},{2,8},{3,9},{4,14},{5,15},{6,12},{7,13},{8,2},{9,3},... | collective-permute-start | bytes 198152 | tf_op jit(solution)/shard_map/ppermute | solution.py:286
  7.1 0.1 collective-permute-start.5
  7.2 4.3 %collective-permute-start.6 = (f32[129,1,128]{2,1,0:T(1,128)S(1)}, f32[129,1,128]{2,1,0:T(1,128)S(1)}, u32[]{:S(2)}, u32[]{:S(2)}) collective-permute-start(f32[129,1,128]{2,1,0:T(1,128)S(1)} %get-tuple-element.33), channel_id=1, source_target_pairs={{0,14},{1,15},{2,12},{3,13},{4,10},{5,11},{6,8},{7,9},{8,6},{9,7},... | collective-permute-start | bytes 198152 | tf_op jit(solution)/shard_map/ppermute | solution.py:286
  11.4 0.0 collective-permute-done.2.refs_1_
  11.4 0.2 collective-permute-start
  11.6 0.0 collective-permute-done.3.refs_2_
  11.6 1.2 %collective-permute-start.1 = (f32[129,1,128]{2,1,0:T(1,128)S(1)}, f32[129,1,128]{2,1,0:T(1,128)S(1)}, u32[]{:S(2)}, u32[]{:S(2)}) collective-permute-start(f32[129,1,128]{2,1,0:T(1,128)S(1)} %get-tuple-element.27), channel_id=1, source_target_pairs={{0,2},{1,3},{2,0},{3,1},{4,6},{5,7},{6,4},{7,5},{8,10},{9,11},{10,... | collective-permute-start | bytes 198152 | tf_op jit(solution)/shard_map/ppermute | solution.py:286
  12.8 0.0 collective-permute-done.4.refs_3_
  12.8 0.0 collective-permute-done.5.refs_4_
  12.8 1.2 %collective-permute-done.6.refs_5_ = f32[129,1,128]{2,1,0:T(1,128)S(1)} collective-permute-done((f32[129,1,128]{2,1,0:T(1,128)S(1)}, f32[129,1,128]{2,1,0:T(1,128)S(1)}, u32[]{:S(2)}, u32[]{:S(2)}) %collective-permute-start.6) | collective-permute-done | bytes 66080 | tf_op jit(solution)/shard_map/ppermute | solution.py:286
  14.1 0.3 sum_slots.2
  14.3 2.0 %collective-permute-done.refs_0_ = f32[129,1,128]{2,1,0:T(1,128)S(1)} collective-permute-done((f32[129,1,128]{2,1,0:T(1,128)S(1)}, f32[129,1,128]{2,1,0:T(1,128)S(1)}, u32[]{:S(2)}, u32[]{:S(2)}) %collective-permute-start) | collective-permute-done | bytes 66080 | tf_op jit(solution)/shard_map/ppermute | solution.py:286
  16.4 0.0 collective-permute-done.1.refs_1_
  16.4 0.2 sum_slots.3
  16.5 3.3 %collective-permute-start.7 = (f32[64,8,128]{2,1,0:T(8,128)S(1)}, f32[64,8,128]{2,1,0:T(8,128)S(1)}, u32[]{:S(2)}, u32[]{:S(2)}) collective-permute-start(f32[64,8,128]{2,1,0:T(8,128)S(1)} %get-tuple-element.37.refs_3_), channel_id=1, source_target_pairs={{0,1},{1,0},{2,3},{3,2},{4,5},{5,4},{6,7},{7,6},{8,9},{9,8},{10,11... | collective-permute-start | bytes 786440 | tf_op jit(solution)/shard_map/ppermute | solution.py:316
  19.8 0.1 collective-permute-start.8
  19.9 1.1 %collective-permute-done.7.other_ref = f32[64,8,128]{2,1,0:T(8,128)S(1)} collective-permute-done((f32[64,8,128]{2,1,0:T(8,128)S(1)}, f32[64,8,128]{2,1,0:T(8,128)S(1)}, u32[]{:S(2)}, u32[]{:S(2)}) %collective-permute-start.7) | collective-permute-done | bytes 262176 | tf_op jit(solution)/shard_map/ppermute | solution.py:316
  21.0 0.0 copy-start.1
  21.0 0.0 copy-start
  21.0 0.6 %collective-permute-start.11 = (f32[40,8,128]{2,1,0:T(8,128)S(1)}, f32[40,8,128]{2,1,0:T(8,128)S(1)}, u32[]{:S(2)}, u32[]{:S(2)}) collective-permute-start(f32[40,8,128]{2,1,0:T(8,128)S(1)} %get-tuple-element.38.refs_0_), channel_id=1, source_target_pairs={{1,2},{2,1},{3,4},{4,3},{5,6},{6,5},{7,8},{8,7},{9,10},{10,9},{11,... | collective-permute-start | bytes 491528 | tf_op jit(solution)/shard_map/ppermute | solution.py:336
  21.6 1.3 %collective-permute-start.10 = (f32[16,8,128]{2,1,0:T(8,128)S(1)}, f32[16,8,128]{2,1,0:T(8,128)S(1)}, u32[]{:S(2)}, u32[]{:S(2)}) collective-permute-start(f32[16,8,128]{2,1,0:T(8,128)S(1)} %get-tuple-element.39.refs_1_), channel_id=1, source_target_pairs={{1,2},{2,1},{3,4},{4,3},{5,6},{6,5},{7,8},{8,7},{9,10},{10,9},{11,... | collective-permute-start | bytes 196616 | tf_op jit(solution)/shard_map/ppermute | solution.py:336
  22.8 0.5 %collective-permute-start.9 = (f32[8,8,128]{2,1,0:T(8,128)S(1)}, f32[8,8,128]{2,1,0:T(8,128)S(1)}, u32[]{:S(2)}, u32[]{:S(2)}) collective-permute-start(f32[8,8,128]{2,1,0:T(8,128)S(1)} %get-tuple-element.40.refs_2_), channel_id=1, source_target_pairs={{1,2},{2,1},{3,4},{4,3},{5,6},{6,5},{7,8},{8,7},{9,10},{10,9},{11,... | collective-permute-start | bytes 98312 | tf_op jit(solution)/shard_map/ppermute | solution.py:336
  23.3 0.0 collective-permute-done.8.refs_4_
  23.3 0.0 copy-done.1
  23.3 0.0 copy-done
  23.3 2.2 %stack_near.1 = (f32[16,2,4,8,128]{4,3,2,1,0:T(8,128)S(1)}, s32[96]{0:T(128)S(4)}, s32[48]{0:T(128)S(4)}, s32[32]{0:T(128)S(4)}, s32[4]{0:T(128)S(4)}) custom-call(s32[8,16]{1,0:T(8,128)S(1)} %copy-done, s32[8,16]{1,0:T(8,128)S(1)} %copy-done.1, s32[1]{0:T(128)} %bitcast.refs_4_.me_ref, f32[40,8,128]{2,1,0:T(8,128)S(1)} %get-tuple-element.38.refs_0_, ...), custom_call_target="tpu_custom_call" | custom-call | tf_op jit(solution)/shard_map/stack_near/pallas_call | solution.py:339
  25.5 1.1 %collective-permute-done.11.far_ref = f32[40,8,128]{2,1,0:T(8,128)S(1)} collective-permute-done((f32[40,8,128]{2,1,0:T(8,128)S(1)}, f32[40,8,128]{2,1,0:T(8,128)S(1)}, u32[]{:S(2)}, u32[]{:S(2)}) %collective-permute-start.11) | collective-permute-done | bytes 163872 | tf_op jit(solution)/shard_map/ppermute | solution.py:336
  26.6 0.7 %stack_far.3.given_ref = f32[16,2,4,8,128]{4,3,2,1,0:T(8,128)S(1)} custom-call(s32[96]{0:T(128)S(4)} %get-tuple-element.44.list_ref, s32[4]{0:T(128)S(4)} %get-tuple-element.42.count_ref, f32[40,8,128]{2,1,0:T(8,128)S(1)} %collective-permute-done.11.far_ref, f32[16,2,4,8,128]{4,3,2,1,0:T(8,128)S(1)} %get-tuple-element.45.given_ref), custom_call_target="tpu_custom_call", output_to_operand_aliasing={{}: (3, {})} | custom-call | tf_op jit(solution)/shard_map/stack_far/pallas_call | solution.py:352
  27.3 0.0 collective-permute-done.10.far_ref
  27.4 0.2 stack_far.4.given_ref
  27.6 0.1 collective-permute-done.9.far_ref
  27.7 0.9 %stack_far.5 = (f32[16,2,4,8,128]{4,3,2,1,0:T(8,128)S(1)}, f32[8,512]{1,0:T(8,128)}) custom-call(s32[32]{0:T(128)S(4)} %get-tuple-element.41.list_ref, s32[4]{0:T(128)S(4)} %get-tuple-element.42.count_ref, f32[8,8,128]{2,1,0:T(8,128)S(1)} %collective-permute-done.9.far_ref, f32[16,2,4,8,128]{4,3,2,1,0:T(8,128)S(1)} %stack_far.4.given_ref), custom_call_target="tpu_custom_call", output_to_operand_aliasing={{0}: (3, {})} | custom-call | tf_op jit(solution)/shard_map/stack_far/pallas_call | solution.py:352
  (1 shorter events, 0.0 us)
Async XLA Ops:
  1.5 9.9 %collective-permute-start.2 = (f32[129,1,128]{2,1,0:T(1,128)S(1)}, f32[129,1,128]{2,1,0:T(1,128)S(1)}, u32[]{:S(2)}, u32[]{:S(2)}) collective-permute-start(f32[129,1,128]{2,1,0:T(1,128)S(1)} %get-tuple-element.29), channel_id=1, source_target_pairs={{0,8},{1,9},{2,10},{3,11},{4,12},{5,13},{6,14},{7,15},{8,0},{9,1},... | collective-permute-start | bytes 198152 | tf_op jit(solution)/shard_map/ppermute | solution.py:286
  4.7 6.9 %collective-permute-start.3 = (f32[129,1,128]{2,1,0:T(1,128)S(1)}, f32[129,1,128]{2,1,0:T(1,128)S(1)}, u32[]{:S(2)}, u32[]{:S(2)}) collective-permute-start(f32[129,1,128]{2,1,0:T(1,128)S(1)} %get-tuple-element.30), channel_id=1, source_target_pairs={{0,4},{1,5},{2,6},{3,7},{4,0},{5,1},{6,2},{7,3},{8,12},{9,13},{10,... | collective-permute-start | bytes 198152 | tf_op jit(solution)/shard_map/ppermute | solution.py:286
  6.0 6.8 %collective-permute-start.4 = (f32[129,1,128]{2,1,0:T(1,128)S(1)}, f32[129,1,128]{2,1,0:T(1,128)S(1)}, u32[]{:S(2)}, u32[]{:S(2)}) collective-permute-start(f32[129,1,128]{2,1,0:T(1,128)S(1)} %get-tuple-element.31), channel_id=1, source_target_pairs={{0,10},{1,11},{2,8},{3,9},{4,14},{5,15},{6,12},{7,13},{8,2},{9,3},... | collective-permute-start | bytes 198152 | tf_op jit(solution)/shard_map/ppermute | solution.py:286
  7.1 5.8 %collective-permute-start.5 = (f32[129,1,128]{2,1,0:T(1,128)S(1)}, f32[129,1,128]{2,1,0:T(1,128)S(1)}, u32[]{:S(2)}, u32[]{:S(2)}) collective-permute-start(f32[129,1,128]{2,1,0:T(1,128)S(1)} %get-tuple-element.32), channel_id=1, source_target_pairs={{0,6},{1,7},{2,4},{3,5},{4,2},{5,3},{6,0},{7,1},{8,14},{9,15},{10,... | collective-permute-start | bytes 198152 | tf_op jit(solution)/shard_map/ppermute | solution.py:286
  7.2 6.9 %collective-permute-start.6 = (f32[129,1,128]{2,1,0:T(1,128)S(1)}, f32[129,1,128]{2,1,0:T(1,128)S(1)}, u32[]{:S(2)}, u32[]{:S(2)}) collective-permute-start(f32[129,1,128]{2,1,0:T(1,128)S(1)} %get-tuple-element.33), channel_id=1, source_target_pairs={{0,14},{1,15},{2,12},{3,13},{4,10},{5,11},{6,8},{7,9},{8,6},{9,7},... | collective-permute-start | bytes 198152 | tf_op jit(solution)/shard_map/ppermute | solution.py:286
  11.4 4.9 %collective-permute-start = (f32[129,1,128]{2,1,0:T(1,128)S(1)}, f32[129,1,128]{2,1,0:T(1,128)S(1)}, u32[]{:S(2)}, u32[]{:S(2)}) collective-permute-start(f32[129,1,128]{2,1,0:T(1,128)S(1)} %get-tuple-element.26), channel_id=1, source_target_pairs={{0,12},{1,13},{2,14},{3,15},{4,8},{5,9},{6,10},{7,11},{8,4},{9,5},... | collective-permute-start | bytes 198152 | tf_op jit(solution)/shard_map/ppermute | solution.py:286
  11.6 4.7 %collective-permute-start.1 = (f32[129,1,128]{2,1,0:T(1,128)S(1)}, f32[129,1,128]{2,1,0:T(1,128)S(1)}, u32[]{:S(2)}, u32[]{:S(2)}) collective-permute-start(f32[129,1,128]{2,1,0:T(1,128)S(1)} %get-tuple-element.27), channel_id=1, source_target_pairs={{0,2},{1,3},{2,0},{3,1},{4,6},{5,7},{6,4},{7,5},{8,10},{9,11},{10,... | collective-permute-start | bytes 198152 | tf_op jit(solution)/shard_map/ppermute | solution.py:286
  16.5 4.4 %collective-permute-start.7 = (f32[64,8,128]{2,1,0:T(8,128)S(1)}, f32[64,8,128]{2,1,0:T(8,128)S(1)}, u32[]{:S(2)}, u32[]{:S(2)}) collective-permute-start(f32[64,8,128]{2,1,0:T(8,128)S(1)} %get-tuple-element.37.refs_3_), channel_id=1, source_target_pairs={{0,1},{1,0},{2,3},{3,2},{4,5},{5,4},{6,7},{7,6},{8,9},{9,8},{10,11... | collective-permute-start | bytes 786440 | tf_op jit(solution)/shard_map/ppermute | solution.py:316
  19.8 3.5 %collective-permute-start.8 = (f32[64,8,128]{2,1,0:T(8,128)S(1)}, f32[64,8,128]{2,1,0:T(8,128)S(1)}, u32[]{:S(2)}, u32[]{:S(2)}) collective-permute-start(f32[64,8,128]{2,1,0:T(8,128)S(1)} %get-tuple-element.36.mine_ref), channel_id=1, source_target_pairs={{0,1},{1,0},{2,3},{3,2},{4,5},{5,4},{6,7},{7,6},{8,9},{9,8},{10,11... | collective-permute-start | bytes 786440 | tf_op jit(solution)/shard_map/ppermute | solution.py:317
  21.0 2.4 %copy-start.1 = (s32[8,16]{1,0:T(8,128)S(1)}, s32[8,16]{1,0:T(8,128)}, u32[]{:S(2)}) copy-start(s32[8,16]{1,0:T(8,128)} %col_ref.1) | copy-start | bytes 1540
  21.0 2.3 %copy-start = (s32[8,16]{1,0:T(8,128)S(1)}, s32[8,16]{1,0:T(8,128)}, u32[]{:S(2)}) copy-start(s32[8,16]{1,0:T(8,128)} %row_ref.1) | copy-start | bytes 1540
  21.0 5.6 %collective-permute-start.11 = (f32[40,8,128]{2,1,0:T(8,128)S(1)}, f32[40,8,128]{2,1,0:T(8,128)S(1)}, u32[]{:S(2)}, u32[]{:S(2)}) collective-permute-start(f32[40,8,128]{2,1,0:T(8,128)S(1)} %get-tuple-element.38.refs_0_), channel_id=1, source_target_pairs={{1,2},{2,1},{3,4},{4,3},{5,6},{6,5},{7,8},{8,7},{9,10},{10,9},{11,... | collective-permute-start | bytes 491528 | tf_op jit(solution)/shard_map/ppermute | solution.py:336
  21.6 5.8 %collective-permute-start.10 = (f32[16,8,128]{2,1,0:T(8,128)S(1)}, f32[16,8,128]{2,1,0:T(8,128)S(1)}, u32[]{:S(2)}, u32[]{:S(2)}) collective-permute-start(f32[16,8,128]{2,1,0:T(8,128)S(1)} %get-tuple-element.39.refs_1_), channel_id=1, source_target_pairs={{1,2},{2,1},{3,4},{4,3},{5,6},{6,5},{7,8},{8,7},{9,10},{10,9},{11,... | collective-permute-start | bytes 196616 | tf_op jit(solution)/shard_map/ppermute | solution.py:336
  22.8 4.9 %collective-permute-start.9 = (f32[8,8,128]{2,1,0:T(8,128)S(1)}, f32[8,8,128]{2,1,0:T(8,128)S(1)}, u32[]{:S(2)}, u32[]{:S(2)}) collective-permute-start(f32[8,8,128]{2,1,0:T(8,128)S(1)} %get-tuple-element.40.refs_2_), channel_id=1, source_target_pairs={{1,2},{2,1},{3,4},{4,3},{5,6},{6,5},{7,8},{8,7},{9,10},{10,9},{11,... | collective-permute-start | bytes 98312 | tf_op jit(solution)/shard_map/ppermute | solution.py:336

commit v11 on v10

--- a/solution.py
+++ b/solution.py
@@ -90,8 +90,9 @@
         first += count
 
 
-def sum_kernel(capacity, cells, first_call, *refs):
-    in_refs, sky_refs = refs[: -2 if first_call else -4], refs[-2:]
+def sum_kernel(capacity, cells, first_call, sides, *refs):
+    skies = len(sides)
+    in_refs, sky_refs = refs[: -skies if first_call else -2 * skies], refs[-skies:]
     rows, width = sky_refs[0].shape[1:]
     stride = 4 * capacity * rows + 1
     for sky_ref in sky_refs if first_call else ():
@@ -103,8 +104,8 @@
         def one_message(message, carry, flat_ref=flat_ref):
             first = message * stride
             notes = flat_ref[pl.ds(first + stride - 1, 1), :].astype(jnp.int32)
-            for slot in range(2 * capacity):
-                sky_ref = sky_refs[slot // capacity]
+            for slot in (side * capacity + rank for side in sides for rank in range(capacity)):
+                sky_ref = sky_refs[sides.index(slot // capacity)]
                 place = notes[0, slot] - 1
                 there = place >= 0
                 base = jnp.maximum(place, 0)
@@ -299,19 +300,21 @@
         incoming = [incoming.reshape(chips * stride, 1, width)]
     total = epochs * 2 * cells
     sky_shape = jax.ShapeDtypeStruct((total, rows, width), jnp.float32)
-    skies = []
-    for some in (incoming[:EARLY], incoming[EARLY:]):
-        if some:
-            skies = pl.pallas_call(
-                functools.partial(sum_kernel, capacity, cells, not skies),
-                out_shape=[sky_shape, sky_shape],
-                in_specs=[VMEM] * (len(some) + len(skies)),
-                out_specs=[VMEM, VMEM],
-                input_output_aliases={len(some) + i: i for i in range(len(skies))},
-                compiler_params=LIMIT,
-                name="sum_slots",
-            )(*some, *skies)
-    mine, others = skies
+    def summed(some, sides, skies=()):
+        return pl.pallas_call(
+            functools.partial(sum_kernel, capacity, cells, not skies, sides),
+            out_shape=[sky_shape] * len(sides),
+            in_specs=[VMEM] * (len(some) + len(skies)),
+            out_specs=[VMEM] * len(sides),
+            input_output_aliases={len(some) + i: i for i in range(len(skies))},
+            compiler_params=LIMIT,
+            name="sum_slots",
+        )(*some, *skies)
+
+    mine, others = summed(incoming[:EARLY], (0, 1))
+    if incoming[EARLY:]:
+        (others,) = summed(incoming[EARLY:], (1,), (others,))
+        (mine,) = summed(incoming[EARLY:], (0,), (mine,))
     across = [(i, i ^ 1) for i in range(tiles)]
     other = lax.ppermute(others, "tile", across)
     theirs = lax.ppermute(mine, "tile", across)

time: 28.7 us -> 28.8 us (level)
  Pallas kernels: 5.96 us -> 6.33 us
  transfers between devices with their start and end apart: 12 -> 12, of which waited for: 5 -> 4; matrix products, arithmetic and copies ran while one was open for 0% -> 0% of each run, Pallas kernels for 12% -> 13%
where the time goes in v11:
time: 28.8 us; the launch traced here: 28.7 us
  starting transfers between devices  17 us (59%)
  Pallas kernels  6.33 us (22%)
  waiting for transfers between devices  5.32 us (18%)
    ppermute x7, starting transfers between devices, body(): lax.ppermute(outgoing[k], 'tile', [(i, i ^ 2 * k) for i in range(tiles)])  11.3 us
    ppermute x1, starting transfers between devices, body(): other = lax.ppermute(others, 'tile', across)  3.29 us
    ppermute x7, waiting for transfers between devices, body(): lax.ppermute(outgoing[k], 'tile', [(i, i ^ 2 * k) for i in range(tiles)])  3.25 us
    ppermute x3, starting transfers between devices, body(): far = [lax.ppermute(part, ('field', 'tile'), both) for part in own]  2.3 us
    pallas_call x1, Pallas kernels, body(): pl.pallas_call(functools.partial(near_kernel, tiles, GROUP, split), out_s...  2.19 us
    pallas_call x3, Pallas kernels, body(): pl.pallas_call(functools.partial(far_kernel, part, GROUP), out_shape=[sum...  2.04 us
    pallas_call x1, Pallas kernels, body(): pl.pallas_call(functools.partial(pack_kernel, capacity, outputs), out_sha...  1.51 us
    ppermute x3, waiting for transfers between devices, body(): far = [lax.ppermute(part, ('field', 'tile'), both) for part in own]  1.12 us
  transfers between devices with their start and end apart: 12, of which 4 were waited for; matrix products, arithmetic and copies ran while one was open for 0% of the time, Pallas kernels for 13%

profile of v11, /device:TPU:1, one launch (start us, length us, event | category | flops | bytes accessed | tf_op | source)
XLA Modules:
  0.0 28.7 jit_solution(16882667441609288639)
XLA Ops:
  0.0 1.5 %pack.1 = (f32[129,1,128]{2,1,0:T(1,128)S(1)}, f32[129,1,128]{2,1,0:T(1,128)S(1)}, f32[129,1,128]{2,1,0:T(1,128)S(1)}, f32[129,1,128]{2,1,0:T(1,128)S(1)}, f32[1...) custom-call(s32[4,1,8]{2,1,0:T(1,128)} %bitcast.4, ...), custom_call_target="tpu_custom_call" | custom-call | tf_op jit(solution)/shard_map/pack/pallas_call | solution.py:264
  1.5 3.2 %collective-permute-start.2 = (f32[129,1,128]{2,1,0:T(1,128)S(1)}, f32[129,1,128]{2,1,0:T(1,128)S(1)}, u32[]{:S(2)}, u32[]{:S(2)}) collective-permute-start(f32[129,1,128]{2,1,0:T(1,128)S(1)} %get-tuple-element.27), channel_id=1, source_target_pairs={{0,8},{1,9},{2,10},{3,11},{4,12},{5,13},{6,14},{7,15},{8,0},{9,1},... | collective-permute-start | bytes 198152 | tf_op jit(solution)/shard_map/ppermute | solution.py:287
  4.7 1.3 %collective-permute-start.3 = (f32[129,1,128]{2,1,0:T(1,128)S(1)}, f32[129,1,128]{2,1,0:T(1,128)S(1)}, u32[]{:S(2)}, u32[]{:S(2)}) collective-permute-start(f32[129,1,128]{2,1,0:T(1,128)S(1)} %get-tuple-element.28), channel_id=1, source_target_pairs={{0,4},{1,5},{2,6},{3,7},{4,0},{5,1},{6,2},{7,3},{8,12},{9,13},{10,... | collective-permute-start | bytes 198152 | tf_op jit(solution)/shard_map/ppermute | solution.py:287
  6.0 1.0 %collective-permute-start.4 = (f32[129,1,128]{2,1,0:T(1,128)S(1)}, f32[129,1,128]{2,1,0:T(1,128)S(1)}, u32[]{:S(2)}, u32[]{:S(2)}) collective-permute-start(f32[129,1,128]{2,1,0:T(1,128)S(1)} %get-tuple-element.29), channel_id=1, source_target_pairs={{0,10},{1,11},{2,8},{3,9},{4,14},{5,15},{6,12},{7,13},{8,2},{9,3},... | collective-permute-start | bytes 198152 | tf_op jit(solution)/shard_map/ppermute | solution.py:287
  7.1 0.1 collective-permute-start.5
  7.2 4.3 %collective-permute-start.6 = (f32[129,1,128]{2,1,0:T(1,128)S(1)}, f32[129,1,128]{2,1,0:T(1,128)S(1)}, u32[]{:S(2)}, u32[]{:S(2)}) collective-permute-start(f32[129,1,128]{2,1,0:T(1,128)S(1)} %get-tuple-element.31), channel_id=1, source_target_pairs={{0,14},{1,15},{2,12},{3,13},{4,10},{5,11},{6,8},{7,9},{8,6},{9,7},... | collective-permute-start | bytes 198152 | tf_op jit(solution)/shard_map/ppermute | solution.py:287
  11.4 0.0 collective-permute-done.2.refs_1_
  11.4 0.2 collective-permute-start
  11.6 0.0 collective-permute-done.3.refs_2_
  11.6 1.2 %collective-permute-start.1 = (f32[129,1,128]{2,1,0:T(1,128)S(1)}, f32[129,1,128]{2,1,0:T(1,128)S(1)}, u32[]{:S(2)}, u32[]{:S(2)}) collective-permute-start(f32[129,1,128]{2,1,0:T(1,128)S(1)} %get-tuple-element.25), channel_id=1, source_target_pairs={{0,2},{1,3},{2,0},{3,1},{4,6},{5,7},{6,4},{7,5},{8,10},{9,11},{10,... | collective-permute-start | bytes 198152 | tf_op jit(solution)/shard_map/ppermute | solution.py:287
  12.8 0.0 collective-permute-done.4.refs_3_
  12.8 0.0 collective-permute-done.5.refs_4_
  12.8 1.2 %collective-permute-done.6.refs_5_ = f32[129,1,128]{2,1,0:T(1,128)S(1)} collective-permute-done((f32[129,1,128]{2,1,0:T(1,128)S(1)}, f32[129,1,128]{2,1,0:T(1,128)S(1)}, u32[]{:S(2)}, u32[]{:S(2)}) %collective-permute-start.6) | collective-permute-done | bytes 66080 | tf_op jit(solution)/shard_map/ppermute | solution.py:287
  14.1 0.3 sum_slots.3
  14.3 2.0 %collective-permute-done.refs_0_ = f32[129,1,128]{2,1,0:T(1,128)S(1)} collective-permute-done((f32[129,1,128]{2,1,0:T(1,128)S(1)}, f32[129,1,128]{2,1,0:T(1,128)S(1)}, u32[]{:S(2)}, u32[]{:S(2)}) %collective-permute-start) | collective-permute-done | bytes 66080 | tf_op jit(solution)/shard_map/ppermute | solution.py:287
  16.3 0.0 collective-permute-done.1.refs_1_
  16.4 0.2 sum_slots.5.refs_3_
  16.5 3.3 %collective-permute-start.7 = (f32[64,8,128]{2,1,0:T(8,128)S(1)}, f32[64,8,128]{2,1,0:T(8,128)S(1)}, u32[]{:S(2)}, u32[]{:S(2)}) collective-permute-start(f32[64,8,128]{2,1,0:T(8,128)S(1)} %sum_slots.5.refs_3_), channel_id=1, source_target_pairs={{0,1},{1,0},{2,3},{3,2},{4,5},{5,4},{6,7},{7,6},{8,9},{9,8},{10,11... | collective-permute-start | bytes 786440 | tf_op jit(solution)/shard_map/ppermute | solution.py:319
  19.8 0.1 sum_slots.4.mine_ref
  19.9 0.1 collective-permute-start.8
  20.0 0.9 %collective-permute-done.7.other_ref = f32[64,8,128]{2,1,0:T(8,128)S(1)} collective-permute-done((f32[64,8,128]{2,1,0:T(8,128)S(1)}, f32[64,8,128]{2,1,0:T(8,128)S(1)}, u32[]{:S(2)}, u32[]{:S(2)}) %collective-permute-start.7) | collective-permute-done | bytes 262176 | tf_op jit(solution)/shard_map/ppermute | solution.py:319
  21.0 0.0 copy-start.1
  21.0 0.0 copy-start
  21.0 0.6 %collective-permute-start.11 = (f32[40,8,128]{2,1,0:T(8,128)S(1)}, f32[40,8,128]{2,1,0:T(8,128)S(1)}, u32[]{:S(2)}, u32[]{:S(2)}) collective-permute-start(f32[40,8,128]{2,1,0:T(8,128)S(1)} %get-tuple-element.34.refs_0_), channel_id=1, source_target_pairs={{1,2},{2,1},{3,4},{4,3},{5,6},{6,5},{7,8},{8,7},{9,10},{10,9},{11,... | collective-permute-start | bytes 491528 | tf_op jit(solution)/shard_map/ppermute | solution.py:339
  21.6 1.3 %collective-permute-start.10 = (f32[16,8,128]{2,1,0:T(8,128)S(1)}, f32[16,8,128]{2,1,0:T(8,128)S(1)}, u32[]{:S(2)}, u32[]{:S(2)}) collective-permute-start(f32[16,8,128]{2,1,0:T(8,128)S(1)} %get-tuple-element.35.refs_1_), channel_id=1, source_target_pairs={{1,2},{2,1},{3,4},{4,3},{5,6},{6,5},{7,8},{8,7},{9,10},{10,9},{11,... | collective-permute-start | bytes 196616 | tf_op jit(solution)/shard_map/ppermute | solution.py:339
  22.8 0.5 %collective-permute-start.9 = (f32[8,8,128]{2,1,0:T(8,128)S(1)}, f32[8,8,128]{2,1,0:T(8,128)S(1)}, u32[]{:S(2)}, u32[]{:S(2)}) collective-permute-start(f32[8,8,128]{2,1,0:T(8,128)S(1)} %get-tuple-element.36.refs_2_), channel_id=1, source_target_pairs={{1,2},{2,1},{3,4},{4,3},{5,6},{6,5},{7,8},{8,7},{9,10},{10,9},{11,... | collective-permute-start | bytes 98312 | tf_op jit(solution)/shard_map/ppermute | solution.py:339
  23.3 0.0 collective-permute-done.8.refs_4_
  23.3 0.0 copy-done.1
  23.3 0.0 copy-done
  23.3 2.2 %stack_near.1 = (f32[16,2,4,8,128]{4,3,2,1,0:T(8,128)S(1)}, s32[96]{0:T(128)S(4)}, s32[48]{0:T(128)S(4)}, s32[32]{0:T(128)S(4)}, s32[4]{0:T(128)S(4)}) custom-call(s32[8,16]{1,0:T(8,128)S(1)} %copy-done, s32[8,16]{1,0:T(8,128)S(1)} %copy-done.1, s32[1]{0:T(128)} %bitcast.refs_4_.me_ref, f32[40,8,128]{2,1,0:T(8,128)S(1)} %get-tuple-element.34.refs_0_, ...), custom_call_target="tpu_custom_call" | custom-call | tf_op jit(solution)/shard_map/stack_near/pallas_call | solution.py:342
  25.5 1.1 %collective-permute-done.11.far_ref = f32[40,8,128]{2,1,0:T(8,128)S(1)} collective-permute-done((f32[40,8,128]{2,1,0:T(8,128)S(1)}, f32[40,8,128]{2,1,0:T(8,128)S(1)}, u32[]{:S(2)}, u32[]{:S(2)}) %collective-permute-start.11) | collective-permute-done | bytes 163872 | tf_op jit(solution)/shard_map/ppermute | solution.py:339
  26.6 0.7 %stack_far.3.given_ref = f32[16,2,4,8,128]{4,3,2,1,0:T(8,128)S(1)} custom-call(s32[96]{0:T(128)S(4)} %get-tuple-element.40.list_ref, s32[4]{0:T(128)S(4)} %get-tuple-element.38.count_ref, f32[40,8,128]{2,1,0:T(8,128)S(1)} %collective-permute-done.11.far_ref, f32[16,2,4,8,128]{4,3,2,1,0:T(8,128)S(1)} %get-tuple-element.41.given_ref), custom_call_target="tpu_custom_call", output_to_operand_aliasing={{}: (3, {})} | custom-call | tf_op jit(solution)/shard_map/stack_far/pallas_call | solution.py:355
  27.3 0.0 collective-permute-done.10.far_ref
  27.3 0.5 %stack_far.4.given_ref = f32[16,2,4,8,128]{4,3,2,1,0:T(8,128)S(1)} custom-call(s32[48]{0:T(128)S(4)} %get-tuple-element.39.list_ref, s32[4]{0:T(128)S(4)} %get-tuple-element.38.count_ref, f32[16,8,128]{2,1,0:T(8,128)S(1)} %collective-permute-done.10.far_ref, f32[16,2,4,8,128]{4,3,2,1,0:T(8,128)S(1)} %stack_far.3.given_ref), custom_call_target="tpu_custom_call", output_to_operand_aliasing={{}: (3, {})} | custom-call | tf_op jit(solution)/shard_map/stack_far/pallas_call | solution.py:355
  27.8 0.0 collective-permute-done.9.far_ref
  27.8 0.9 %stack_far.5 = (f32[16,2,4,8,128]{4,3,2,1,0:T(8,128)S(1)}, f32[8,512]{1,0:T(8,128)}) custom-call(s32[32]{0:T(128)S(4)} %get-tuple-element.37.list_ref, s32[4]{0:T(128)S(4)} %get-tuple-element.38.count_ref, f32[8,8,128]{2,1,0:T(8,128)S(1)} %collective-permute-done.9.far_ref, f32[16,2,4,8,128]{4,3,2,1,0:T(8,128)S(1)} %stack_far.4.given_ref), custom_call_target="tpu_custom_call", output_to_operand_aliasing={{0}: (3, {})} | custom-call | tf_op jit(solution)/shard_map/stack_far/pallas_call | solution.py:355
  (1 shorter events, 0.0 us)
Async XLA Ops:
  1.5 9.9 %collective-permute-start.2 = (f32[129,1,128]{2,1,0:T(1,128)S(1)}, f32[129,1,128]{2,1,0:T(1,128)S(1)}, u32[]{:S(2)}, u32[]{:S(2)}) collective-permute-start(f32[129,1,128]{2,1,0:T(1,128)S(1)} %get-tuple-element.27), channel_id=1, source_target_pairs={{0,8},{1,9},{2,10},{3,11},{4,12},{5,13},{6,14},{7,15},{8,0},{9,1},... | collective-permute-start | bytes 198152 | tf_op jit(solution)/shard_map/ppermute | solution.py:287
  4.7 6.9 %collective-permute-start.3 = (f32[129,1,128]{2,1,0:T(1,128)S(1)}, f32[129,1,128]{2,1,0:T(1,128)S(1)}, u32[]{:S(2)}, u32[]{:S(2)}) collective-permute-start(f32[129,1,128]{2,1,0:T(1,128)S(1)} %get-tuple-element.28), channel_id=1, source_target_pairs={{0,4},{1,5},{2,6},{3,7},{4,0},{5,1},{6,2},{7,3},{8,12},{9,13},{10,... | collective-permute-start | bytes 198152 | tf_op jit(solution)/shard_map/ppermute | solution.py:287
  6.0 6.8 %collective-permute-start.4 = (f32[129,1,128]{2,1,0:T(1,128)S(1)}, f32[129,1,128]{2,1,0:T(1,128)S(1)}, u32[]{:S(2)}, u32[]{:S(2)}) collective-permute-start(f32[129,1,128]{2,1,0:T(1,128)S(1)} %get-tuple-element.29), channel_id=1, source_target_pairs={{0,10},{1,11},{2,8},{3,9},{4,14},{5,15},{6,12},{7,13},{8,2},{9,3},... | collective-permute-start | bytes 198152 | tf_op jit(solution)/shard_map/ppermute | solution.py:287
  7.1 5.8 %collective-permute-start.5 = (f32[129,1,128]{2,1,0:T(1,128)S(1)}, f32[129,1,128]{2,1,0:T(1,128)S(1)}, u32[]{:S(2)}, u32[]{:S(2)}) collective-permute-start(f32[129,1,128]{2,1,0:T(1,128)S(1)} %get-tuple-element.30), channel_id=1, source_target_pairs={{0,6},{1,7},{2,4},{3,5},{4,2},{5,3},{6,0},{7,1},{8,14},{9,15},{10,... | collective-permute-start | bytes 198152 | tf_op jit(solution)/shard_map/ppermute | solution.py:287
  7.2 6.9 %collective-permute-start.6 = (f32[129,1,128]{2,1,0:T(1,128)S(1)}, f32[129,1,128]{2,1,0:T(1,128)S(1)}, u32[]{:S(2)}, u32[]{:S(2)}) collective-permute-start(f32[129,1,128]{2,1,0:T(1,128)S(1)} %get-tuple-element.31), channel_id=1, source_target_pairs={{0,14},{1,15},{2,12},{3,13},{4,10},{5,11},{6,8},{7,9},{8,6},{9,7},... | collective-permute-start | bytes 198152 | tf_op jit(solution)/shard_map/ppermute | solution.py:287
  11.4 4.9 %collective-permute-start = (f32[129,1,128]{2,1,0:T(1,128)S(1)}, f32[129,1,128]{2,1,0:T(1,128)S(1)}, u32[]{:S(2)}, u32[]{:S(2)}) collective-permute-start(f32[129,1,128]{2,1,0:T(1,128)S(1)} %get-tuple-element.24), channel_id=1, source_target_pairs={{0,12},{1,13},{2,14},{3,15},{4,8},{5,9},{6,10},{7,11},{8,4},{9,5},... | collective-permute-start | bytes 198152 | tf_op jit(solution)/shard_map/ppermute | solution.py:287
  11.6 4.8 %collective-permute-start.1 = (f32[129,1,128]{2,1,0:T(1,128)S(1)}, f32[129,1,128]{2,1,0:T(1,128)S(1)}, u32[]{:S(2)}, u32[]{:S(2)}) collective-permute-start(f32[129,1,128]{2,1,0:T(1,128)S(1)} %get-tuple-element.25), channel_id=1, source_target_pairs={{0,2},{1,3},{2,0},{3,1},{4,6},{5,7},{6,4},{7,5},{8,10},{9,11},{10,... | collective-permute-start | bytes 198152 | tf_op jit(solution)/shard_map/ppermute | solution.py:287
  16.5 4.4 %collective-permute-start.7 = (f32[64,8,128]{2,1,0:T(8,128)S(1)}, f32[64,8,128]{2,1,0:T(8,128)S(1)}, u32[]{:S(2)}, u32[]{:S(2)}) collective-permute-start(f32[64,8,128]{2,1,0:T(8,128)S(1)} %sum_slots.5.refs_3_), channel_id=1, source_target_pairs={{0,1},{1,0},{2,3},{3,2},{4,5},{5,4},{6,7},{7,6},{8,9},{9,8},{10,11... | collective-permute-start | bytes 786440 | tf_op jit(solution)/shard_map/ppermute | solution.py:319
  19.9 3.4 %collective-permute-start.8 = (f32[64,8,128]{2,1,0:T(8,128)S(1)}, f32[64,8,128]{2,1,0:T(8,128)S(1)}, u32[]{:S(2)}, u32[]{:S(2)}) collective-permute-start(f32[64,8,128]{2,1,0:T(8,128)S(1)} %sum_slots.4.mine_ref), channel_id=1, source_target_pairs={{0,1},{1,0},{2,3},{3,2},{4,5},{5,4},{6,7},{7,6},{8,9},{9,8},{10,11... | collective-permute-start | bytes 786440 | tf_op jit(solution)/shard_map/ppermute | solution.py:320
  21.0 2.4 %copy-start.1 = (s32[8,16]{1,0:T(8,128)S(1)}, s32[8,16]{1,0:T(8,128)}, u32[]{:S(2)}) copy-start(s32[8,16]{1,0:T(8,128)} %col_ref.1) | copy-start | bytes 1540
  21.0 2.3 %copy-start = (s32[8,16]{1,0:T(8,128)S(1)}, s32[8,16]{1,0:T(8,128)}, u32[]{:S(2)}) copy-start(s32[8,16]{1,0:T(8,128)} %row_ref.1) | copy-start | bytes 1540
  21.0 5.6 %collective-permute-start.11 = (f32[40,8,128]{2,1,0:T(8,128)S(1)}, f32[40,8,128]{2,1,0:T(8,128)S(1)}, u32[]{:S(2)}, u32[]{:S(2)}) collective-permute-start(f32[40,8,128]{2,1,0:T(8,128)S(1)} %get-tuple-element.34.refs_0_), channel_id=1, source_target_pairs={{1,2},{2,1},{3,4},{4,3},{5,6},{6,5},{7,8},{8,7},{9,10},{10,9},{11,... | collective-permute-start | bytes 491528 | tf_op jit(solution)/shard_map/ppermute | solution.py:339
  21.6 5.8 %collective-permute-start.10 = (f32[16,8,128]{2,1,0:T(8,128)S(1)}, f32[16,8,128]{2,1,0:T(8,128)S(1)}, u32[]{:S(2)}, u32[]{:S(2)}) collective-permute-start(f32[16,8,128]{2,1,0:T(8,128)S(1)} %get-tuple-element.35.refs_1_), channel_id=1, source_target_pairs={{1,2},{2,1},{3,4},{4,3},{5,6},{6,5},{7,8},{8,7},{9,10},{10,9},{11,... | collective-permute-start | bytes 196616 | tf_op jit(solution)/shard_map/ppermute | solution.py:339
  22.8 5.0 %collective-permute-start.9 = (f32[8,8,128]{2,1,0:T(8,128)S(1)}, f32[8,8,128]{2,1,0:T(8,128)S(1)}, u32[]{:S(2)}, u32[]{:S(2)}) collective-permute-start(f32[8,8,128]{2,1,0:T(8,128)S(1)} %get-tuple-element.36.refs_2_), channel_id=1, source_target_pairs={{1,2},{2,1},{3,4},{4,3},{5,6},{6,5},{7,8},{8,7},{9,10},{10,9},{11,... | collective-permute-start | bytes 98312 | tf_op jit(solution)/shard_map/ppermute | solution.py:339

commit v12 on v10

--- a/solution.py
+++ b/solution.py
@@ -10,7 +10,7 @@
 XREACH = 64
 RREACH = 8
 LANES = 128
-GROUP = 16
+GROUP = 12
 PARTS = 3
 EARLY = 6
 ORDER = (4, 2, 5, 3, 7, 6, 1)

time: 28.7 us -> 28.7 us (level)
  transfers between devices with their start and end apart: 12 -> 12, of which waited for: 5 -> 6; matrix products, arithmetic and copies ran while one was open for 0% -> 0% of each run, Pallas kernels for 12% -> 11%
where the time goes in v12:
time: 28.7 us; the launch traced here: 28.5 us
  starting transfers between devices  17 us (59%)
  Pallas kernels  5.78 us (20%)
  waiting for transfers between devices  5.72 us (20%)
    ppermute x7, starting transfers between devices, body(): lax.ppermute(outgoing[k], 'tile', [(i, i ^ 2 * k) for i in range(tiles)])  11.3 us
    ppermute x1, starting transfers between devices, body(): other = lax.ppermute(others, 'tile', across)  3.29 us
    ppermute x7, waiting for transfers between devices, body(): lax.ppermute(outgoing[k], 'tile', [(i, i ^ 2 * k) for i in range(tiles)])  3.26 us
    ppermute x3, starting transfers between devices, body(): far = [lax.ppermute(part, ('field', 'tile'), both) for part in own]  2.29 us
    pallas_call x1, Pallas kernels, body(): pl.pallas_call(functools.partial(near_kernel, tiles, GROUP, split), out_s...  2.19 us
    pallas_call x3, Pallas kernels, body(): pl.pallas_call(functools.partial(far_kernel, part, GROUP), out_shape=[sum...  1.63 us
    pallas_call x1, Pallas kernels, body(): pl.pallas_call(functools.partial(pack_kernel, capacity, outputs), out_sha...  1.51 us
    ppermute x3, waiting for transfers between devices, body(): far = [lax.ppermute(part, ('field', 'tile'), both) for part in own]  1.37 us
  transfers between devices with their start and end apart: 12, of which 6 were waited for; matrix products, arithmetic and copies ran while one was open for 0% of the time, Pallas kernels for 11%

profile of v12, /device:TPU:1, one launch (start us, length us, event | category | flops | bytes accessed | tf_op | source)
XLA Modules:
  0.0 28.5 jit_solution(7951367296057230519)
XLA Ops:
  0.0 1.5 %pack.1 = (f32[129,1,128]{2,1,0:T(1,128)S(1)}, f32[129,1,128]{2,1,0:T(1,128)S(1)}, f32[129,1,128]{2,1,0:T(1,128)S(1)}, f32[129,1,128]{2,1,0:T(1,128)S(1)}, f32[1...) custom-call(s32[4,1,8]{2,1,0:T(1,128)} %bitcast.4, ...), custom_call_target="tpu_custom_call" | custom-call | tf_op jit(solution)/shard_map/pack/pallas_call | solution.py:263
  1.5 3.2 %collective-permute-start.2 = (f32[129,1,128]{2,1,0:T(1,128)S(1)}, f32[129,1,128]{2,1,0:T(1,128)S(1)}, u32[]{:S(2)}, u32[]{:S(2)}) collective-permute-start(f32[129,1,128]{2,1,0:T(1,128)S(1)} %get-tuple-element.29), channel_id=1, source_target_pairs={{0,8},{1,9},{2,10},{3,11},{4,12},{5,13},{6,14},{7,15},{8,0},{9,1},... | collective-permute-start | bytes 198152 | tf_op jit(solution)/shard_map/ppermute | solution.py:286
  4.7 1.3 %collective-permute-start.3 = (f32[129,1,128]{2,1,0:T(1,128)S(1)}, f32[129,1,128]{2,1,0:T(1,128)S(1)}, u32[]{:S(2)}, u32[]{:S(2)}) collective-permute-start(f32[129,1,128]{2,1,0:T(1,128)S(1)} %get-tuple-element.30), channel_id=1, source_target_pairs={{0,4},{1,5},{2,6},{3,7},{4,0},{5,1},{6,2},{7,3},{8,12},{9,13},{10,... | collective-permute-start | bytes 198152 | tf_op jit(solution)/shard_map/ppermute | solution.py:286
  6.0 1.0 %collective-permute-start.4 = (f32[129,1,128]{2,1,0:T(1,128)S(1)}, f32[129,1,128]{2,1,0:T(1,128)S(1)}, u32[]{:S(2)}, u32[]{:S(2)}) collective-permute-start(f32[129,1,128]{2,1,0:T(1,128)S(1)} %get-tuple-element.31), channel_id=1, source_target_pairs={{0,10},{1,11},{2,8},{3,9},{4,14},{5,15},{6,12},{7,13},{8,2},{9,3},... | collective-permute-start | bytes 198152 | tf_op jit(solution)/shard_map/ppermute | solution.py:286
  7.1 0.1 collective-permute-start.5
  7.2 4.3 %collective-permute-start.6 = (f32[129,1,128]{2,1,0:T(1,128)S(1)}, f32[129,1,128]{2,1,0:T(1,128)S(1)}, u32[]{:S(2)}, u32[]{:S(2)}) collective-permute-start(f32[129,1,128]{2,1,0:T(1,128)S(1)} %get-tuple-element.33), channel_id=1, source_target_pairs={{0,14},{1,15},{2,12},{3,13},{4,10},{5,11},{6,8},{7,9},{8,6},{9,7},... | collective-permute-start | bytes 198152 | tf_op jit(solution)/shard_map/ppermute | solution.py:286
  11.4 0.0 collective-permute-done.2.refs_1_
  11.4 0.2 collective-permute-start
  11.6 0.0 collective-permute-done.3.refs_2_
  11.6 1.2 %collective-permute-start.1 = (f32[129,1,128]{2,1,0:T(1,128)S(1)}, f32[129,1,128]{2,1,0:T(1,128)S(1)}, u32[]{:S(2)}, u32[]{:S(2)}) collective-permute-start(f32[129,1,128]{2,1,0:T(1,128)S(1)} %get-tuple-element.27), channel_id=1, source_target_pairs={{0,2},{1,3},{2,0},{3,1},{4,6},{5,7},{6,4},{7,5},{8,10},{9,11},{10,... | collective-permute-start | bytes 198152 | tf_op jit(solution)/shard_map/ppermute | solution.py:286
  12.8 0.0 collective-permute-done.4.refs_3_
  12.8 0.0 collective-permute-done.5.refs_4_
  12.8 1.2 %collective-permute-done.6.refs_5_ = f32[129,1,128]{2,1,0:T(1,128)S(1)} collective-permute-done((f32[129,1,128]{2,1,0:T(1,128)S(1)}, f32[129,1,128]{2,1,0:T(1,128)S(1)}, u32[]{:S(2)}, u32[]{:S(2)}) %collective-permute-start.6) | collective-permute-done | bytes 66080 | tf_op jit(solution)/shard_map/ppermute | solution.py:286
  14.1 0.3 sum_slots.2
  14.3 2.0 %collective-permute-done.refs_0_ = f32[129,1,128]{2,1,0:T(1,128)S(1)} collective-permute-done((f32[129,1,128]{2,1,0:T(1,128)S(1)}, f32[129,1,128]{2,1,0:T(1,128)S(1)}, u32[]{:S(2)}, u32[]{:S(2)}) %collective-permute-start) | collective-permute-done | bytes 66080 | tf_op jit(solution)/shard_map/ppermute | solution.py:286
  16.4 0.0 collective-permute-done.1.refs_1_
  16.4 0.2 sum_slots.3
  16.5 3.3 %collective-permute-start.7 = (f32[64,8,128]{2,1,0:T(8,128)S(1)}, f32[64,8,128]{2,1,0:T(8,128)S(1)}, u32[]{:S(2)}, u32[]{:S(2)}) collective-permute-start(f32[64,8,128]{2,1,0:T(8,128)S(1)} %get-tuple-element.37.refs_3_), channel_id=1, source_target_pairs={{0,1},{1,0},{2,3},{3,2},{4,5},{5,4},{6,7},{7,6},{8,9},{9,8},{10,11... | collective-permute-start | bytes 786440 | tf_op jit(solution)/shard_map/ppermute | solution.py:316
  19.8 0.1 collective-permute-start.8
  19.9 1.1 %collective-permute-done.7.other_ref = f32[64,8,128]{2,1,0:T(8,128)S(1)} collective-permute-done((f32[64,8,128]{2,1,0:T(8,128)S(1)}, f32[64,8,128]{2,1,0:T(8,128)S(1)}, u32[]{:S(2)}, u32[]{:S(2)}) %collective-permute-start.7) | collective-permute-done | bytes 262176 | tf_op jit(solution)/shard_map/ppermute | solution.py:316
  21.0 0.0 copy-start.1
  21.0 0.0 copy-start
  21.0 0.5 %collective-permute-start.11 = (f32[40,8,128]{2,1,0:T(8,128)S(1)}, f32[40,8,128]{2,1,0:T(8,128)S(1)}, u32[]{:S(2)}, u32[]{:S(2)}) collective-permute-start(f32[40,8,128]{2,1,0:T(8,128)S(1)} %get-tuple-element.38.refs_0_), channel_id=1, source_target_pairs={{1,2},{2,1},{3,4},{4,3},{5,6},{6,5},{7,8},{8,7},{9,10},{10,9},{11,... | collective-permute-start | bytes 491528 | tf_op jit(solution)/shard_map/ppermute | solution.py:336
  21.6 1.3 %collective-permute-start.10 = (f32[16,8,128]{2,1,0:T(8,128)S(1)}, f32[16,8,128]{2,1,0:T(8,128)S(1)}, u32[]{:S(2)}, u32[]{:S(2)}) collective-permute-start(f32[16,8,128]{2,1,0:T(8,128)S(1)} %get-tuple-element.39.refs_1_), channel_id=1, source_target_pairs={{1,2},{2,1},{3,4},{4,3},{5,6},{6,5},{7,8},{8,7},{9,10},{10,9},{11,... | collective-permute-start | bytes 196616 | tf_op jit(solution)/shard_map/ppermute | solution.py:336
  22.8 0.5 %collective-permute-start.9 = (f32[8,8,128]{2,1,0:T(8,128)S(1)}, f32[8,8,128]{2,1,0:T(8,128)S(1)}, u32[]{:S(2)}, u32[]{:S(2)}) collective-permute-start(f32[8,8,128]{2,1,0:T(8,128)S(1)} %get-tuple-element.40.refs_2_), channel_id=1, source_target_pairs={{1,2},{2,1},{3,4},{4,3},{5,6},{6,5},{7,8},{8,7},{9,10},{10,9},{11,... | collective-permute-start | bytes 98312 | tf_op jit(solution)/shard_map/ppermute | solution.py:336
  23.3 0.0 collective-permute-done.8.refs_4_
  23.3 0.0 copy-done.1
  23.3 0.0 copy-done
  23.3 2.2 %stack_near.1 = (f32[16,2,4,8,128]{4,3,2,1,0:T(8,128)S(1)}, s32[92]{0:T(128)S(4)}, s32[44]{0:T(128)S(4)}, s32[28]{0:T(128)S(4)}, s32[4]{0:T(128)S(4)}) custom-call(s32[8,16]{1,0:T(8,128)S(1)} %copy-done, s32[8,16]{1,0:T(8,128)S(1)} %copy-done.1, s32[1]{0:T(128)} %bitcast.refs_4_.me_ref, f32[40,8,128]{2,1,0:T(8,128)S(1)} %get-tuple-element.38.refs_0_, ...), custom_call_target="tpu_custom_call" | custom-call | tf_op jit(solution)/shard_map/stack_near/pallas_call | solution.py:339
  25.5 1.1 %collective-permute-done.11.far_ref = f32[40,8,128]{2,1,0:T(8,128)S(1)} collective-permute-done((f32[40,8,128]{2,1,0:T(8,128)S(1)}, f32[40,8,128]{2,1,0:T(8,128)S(1)}, u32[]{:S(2)}, u32[]{:S(2)}) %collective-permute-start.11) | collective-permute-done | bytes 163872 | tf_op jit(solution)/shard_map/ppermute | solution.py:336
  26.6 0.6 %stack_far.3.given_ref = f32[16,2,4,8,128]{4,3,2,1,0:T(8,128)S(1)} custom-call(s32[92]{0:T(128)S(4)} %get-tuple-element.44.list_ref, s32[4]{0:T(128)S(4)} %get-tuple-element.42.count_ref, f32[40,8,128]{2,1,0:T(8,128)S(1)} %collective-permute-done.11.far_ref, f32[16,2,4,8,128]{4,3,2,1,0:T(8,128)S(1)} %get-tuple-element.45.given_ref), custom_call_target="tpu_custom_call", output_to_operand_aliasing={{}: (3, {})} | custom-call | tf_op jit(solution)/shard_map/stack_far/pallas_call | solution.py:352
  27.2 0.1 collective-permute-done.10.far_ref
  27.3 0.2 stack_far.4.given_ref
  27.5 0.1 collective-permute-done.9.far_ref
  27.7 0.8 %stack_far.5 = (f32[16,2,4,8,128]{4,3,2,1,0:T(8,128)S(1)}, f32[8,512]{1,0:T(8,128)}) custom-call(s32[28]{0:T(128)S(4)} %get-tuple-element.41.list_ref, s32[4]{0:T(128)S(4)} %get-tuple-element.42.count_ref, f32[8,8,128]{2,1,0:T(8,128)S(1)} %collective-permute-done.9.far_ref, f32[16,2,4,8,128]{4,3,2,1,0:T(8,128)S(1)} %stack_far.4.given_ref), custom_call_target="tpu_custom_call", output_to_operand_aliasing={{0}: (3, {})} | custom-call | tf_op jit(solution)/shard_map/stack_far/pallas_call | solution.py:352
  (1 shorter events, 0.0 us)
Async XLA Ops:
  1.5 9.9 %collective-permute-start.2 = (f32[129,1,128]{2,1,0:T(1,128)S(1)}, f32[129,1,128]{2,1,0:T(1,128)S(1)}, u32[]{:S(2)}, u32[]{:S(2)}) collective-permute-start(f32[129,1,128]{2,1,0:T(1,128)S(1)} %get-tuple-element.29), channel_id=1, source_target_pairs={{0,8},{1,9},{2,10},{3,11},{4,12},{5,13},{6,14},{7,15},{8,0},{9,1},... | collective-permute-start | bytes 198152 | tf_op jit(solution)/shard_map/ppermute | solution.py:286
  4.7 6.9 %collective-permute-start.3 = (f32[129,1,128]{2,1,0:T(1,128)S(1)}, f32[129,1,128]{2,1,0:T(1,128)S(1)}, u32[]{:S(2)}, u32[]{:S(2)}) collective-permute-start(f32[129,1,128]{2,1,0:T(1,128)S(1)} %get-tuple-element.30), channel_id=1, source_target_pairs={{0,4},{1,5},{2,6},{3,7},{4,0},{5,1},{6,2},{7,3},{8,12},{9,13},{10,... | collective-permute-start | bytes 198152 | tf_op jit(solution)/shard_map/ppermute | solution.py:286
  6.0 6.8 %collective-permute-start.4 = (f32[129,1,128]{2,1,0:T(1,128)S(1)}, f32[129,1,128]{2,1,0:T(1,128)S(1)}, u32[]{:S(2)}, u32[]{:S(2)}) collective-permute-start(f32[129,1,128]{2,1,0:T(1,128)S(1)} %get-tuple-element.31), channel_id=1, source_target_pairs={{0,10},{1,11},{2,8},{3,9},{4,14},{5,15},{6,12},{7,13},{8,2},{9,3},... | collective-permute-start | bytes 198152 | tf_op jit(solution)/shard_map/ppermute | solution.py:286
  7.1 5.8 %collective-permute-start.5 = (f32[129,1,128]{2,1,0:T(1,128)S(1)}, f32[129,1,128]{2,1,0:T(1,128)S(1)}, u32[]{:S(2)}, u32[]{:S(2)}) collective-permute-start(f32[129,1,128]{2,1,0:T(1,128)S(1)} %get-tuple-element.32), channel_id=1, source_target_pairs={{0,6},{1,7},{2,4},{3,5},{4,2},{5,3},{6,0},{7,1},{8,14},{9,15},{10,... | collective-permute-start | bytes 198152 | tf_op jit(solution)/shard_map/ppermute | solution.py:286
  7.2 6.9 %collective-permute-start.6 = (f32[129,1,128]{2,1,0:T(1,128)S(1)}, f32[129,1,128]{2,1,0:T(1,128)S(1)}, u32[]{:S(2)}, u32[]{:S(2)}) collective-permute-start(f32[129,1,128]{2,1,0:T(1,128)S(1)} %get-tuple-element.33), channel_id=1, source_target_pairs={{0,14},{1,15},{2,12},{3,13},{4,10},{5,11},{6,8},{7,9},{8,6},{9,7},... | collective-permute-start | bytes 198152 | tf_op jit(solution)/shard_map/ppermute | solution.py:286
  11.4 4.9 %collective-permute-start = (f32[129,1,128]{2,1,0:T(1,128)S(1)}, f32[129,1,128]{2,1,0:T(1,128)S(1)}, u32[]{:S(2)}, u32[]{:S(2)}) collective-permute-start(f32[129,1,128]{2,1,0:T(1,128)S(1)} %get-tuple-element.26), channel_id=1, source_target_pairs={{0,12},{1,13},{2,14},{3,15},{4,8},{5,9},{6,10},{7,11},{8,4},{9,5},... | collective-permute-start | bytes 198152 | tf_op jit(solution)/shard_map/ppermute | solution.py:286
  11.6 4.7 %collective-permute-start.1 = (f32[129,1,128]{2,1,0:T(1,128)S(1)}, f32[129,1,128]{2,1,0:T(1,128)S(1)}, u32[]{:S(2)}, u32[]{:S(2)}) collective-permute-start(f32[129,1,128]{2,1,0:T(1,128)S(1)} %get-tuple-element.27), channel_id=1, source_target_pairs={{0,2},{1,3},{2,0},{3,1},{4,6},{5,7},{6,4},{7,5},{8,10},{9,11},{10,... | collective-permute-start | bytes 198152 | tf_op jit(solution)/shard_map/ppermute | solution.py:286
  16.5 4.4 %collective-permute-start.7 = (f32[64,8,128]{2,1,0:T(8,128)S(1)}, f32[64,8,128]{2,1,0:T(8,128)S(1)}, u32[]{:S(2)}, u32[]{:S(2)}) collective-permute-start(f32[64,8,128]{2,1,0:T(8,128)S(1)} %get-tuple-element.37.refs_3_), channel_id=1, source_target_pairs={{0,1},{1,0},{2,3},{3,2},{4,5},{5,4},{6,7},{7,6},{8,9},{9,8},{10,11... | collective-permute-start | bytes 786440 | tf_op jit(solution)/shard_map/ppermute | solution.py:316
  19.8 3.5 %collective-permute-start.8 = (f32[64,8,128]{2,1,0:T(8,128)S(1)}, f32[64,8,128]{2,1,0:T(8,128)S(1)}, u32[]{:S(2)}, u32[]{:S(2)}) collective-permute-start(f32[64,8,128]{2,1,0:T(8,128)S(1)} %get-tuple-element.36.mine_ref), channel_id=1, source_target_pairs={{0,1},{1,0},{2,3},{3,2},{4,5},{5,4},{6,7},{7,6},{8,9},{9,8},{10,11... | collective-permute-start | bytes 786440 | tf_op jit(solution)/shard_map/ppermute | solution.py:317
  21.0 2.4 %copy-start.1 = (s32[8,16]{1,0:T(8,128)S(1)}, s32[8,16]{1,0:T(8,128)}, u32[]{:S(2)}) copy-start(s32[8,16]{1,0:T(8,128)} %col_ref.1) | copy-start | bytes 1540
  21.0 2.3 %copy-start = (s32[8,16]{1,0:T(8,128)S(1)}, s32[8,16]{1,0:T(8,128)}, u32[]{:S(2)}) copy-start(s32[8,16]{1,0:T(8,128)} %row_ref.1) | copy-start | bytes 1540
  21.0 5.6 %collective-permute-start.11 = (f32[40,8,128]{2,1,0:T(8,128)S(1)}, f32[40,8,128]{2,1,0:T(8,128)S(1)}, u32[]{:S(2)}, u32[]{:S(2)}) collective-permute-start(f32[40,8,128]{2,1,0:T(8,128)S(1)} %get-tuple-element.38.refs_0_), channel_id=1, source_target_pairs={{1,2},{2,1},{3,4},{4,3},{5,6},{6,5},{7,8},{8,7},{9,10},{10,9},{11,... | collective-permute-start | bytes 491528 | tf_op jit(solution)/shard_map/ppermute | solution.py:336
  21.6 5.8 %collective-permute-start.10 = (f32[16,8,128]{2,1,0:T(8,128)S(1)}, f32[16,8,128]{2,1,0:T(8,128)S(1)}, u32[]{:S(2)}, u32[]{:S(2)}) collective-permute-start(f32[16,8,128]{2,1,0:T(8,128)S(1)} %get-tuple-element.39.refs_1_), channel_id=1, source_target_pairs={{1,2},{2,1},{3,4},{4,3},{5,6},{6,5},{7,8},{8,7},{9,10},{10,9},{11,... | collective-permute-start | bytes 196616 | tf_op jit(solution)/shard_map/ppermute | solution.py:336
  22.8 4.9 %collective-permute-start.9 = (f32[8,8,128]{2,1,0:T(8,128)S(1)}, f32[8,8,128]{2,1,0:T(8,128)S(1)}, u32[]{:S(2)}, u32[]{:S(2)}) collective-permute-start(f32[8,8,128]{2,1,0:T(8,128)S(1)} %get-tuple-element.40.refs_2_), channel_id=1, source_target_pairs={{1,2},{2,1},{3,4},{4,3},{5,6},{6,5},{7,8},{8,7},{9,10},{10,9},{11,... | collective-permute-start | bytes 98312 | tf_op jit(solution)/shard_map/ppermute | solution.py:336
